TPU v7x, 32 devices: a whole 2x2x4 slice. The times are simulated.
32 devices in a mesh: heads: 4 (over y, x), rows: 8 (over z, core).
Axes of the slice: x: 2, y: 2, z: 4, core: 2. Of those that a mesh axis runs over, the one named last changes fastest.
Arguments:
- layer_input: bfloat16 [17408, 768], P(('rows', 'heads')), may hold values from -6 to 6
- encoder_out: bfloat16 [16384, 768], P(('rows', 'heads')), may hold values from -6 to 6
- doc_lengths: int32 [16, 8], P('rows'), may hold values from 1 to 817, as said below
- self_query: bfloat16 [768, 768], P(None, 'heads'), may hold values from -0.21875 to 0.21875
- self_qbias: float32 [768], P('heads'), may hold values from -3 to 3
- self_key_weight: bfloat16 [768, 768], P(None, 'heads'), may hold values from -0.21875 to 0.21875
- self_value: bfloat16 [768, 768], P(None, 'heads'), may hold values from -0.21875 to 0.21875
- self_vbias: float32 [768], P('heads'), may hold values from -3 to 3
- self_out: bfloat16 [768, 768], P('heads'), may hold values from -1.5 to 1.5
- self_obias: float32 [768], replicated, may hold values from -2 to 2
- first_gain: float32 [768], replicated, may hold values from 0.5 to 1.5
- first_shift: float32 [768], replicated, may hold values from -2 to 2
- cross_query: bfloat16 [768, 768], P(None, 'heads'), may hold values from -0.21875 to 0.21875
- cross_qbias: float32 [768], P('heads'), may hold values from -3 to 3
- cross_key: bfloat16 [768, 768], P(None, 'heads'), may hold values from -0.21875 to 0.21875
- cross_value: bfloat16 [768, 768], P(None, 'heads'), may hold values from -0.21875 to 0.21875
- cross_vbias: float32 [768], P('heads'), may hold values from -3 to 3
- cross_out: bfloat16 [768, 768], P('heads'), may hold values from -3 to 3
- cross_obias: float32 [768], replicated, may hold values from -2 to 2
- second_gain: float32 [768], replicated, may hold values from 0.5 to 1.5
- second_shift: float32 [768], replicated, may hold values from -2 to 2
- up_weight: bfloat16 [768, 3072], replicated, may hold values from -0.21875 to 0.21875
- up_bias: float32 [3072], replicated, may hold values from -3 to 3
- down_weight: bfloat16 [3072, 768], replicated, may hold values from -0.109375 to 0.109375
- down_bias: float32 [768], replicated, may hold values from -2 to 2
- third_gain: float32 [768], replicated, may hold values from 0.5 to 1.5
- third_shift: float32 [768], replicated, may hold values from -2 to 2
- out_grad: bfloat16 [17408, 768], P(('rows', 'heads')), may hold values from -6 to 6
Outputs:
- output: bfloat16 [17408, 768], P(('rows', 'heads'))
- input_grad: bfloat16 [17408, 768], P(('rows', 'heads'))
- encoder_grad: bfloat16 [16384, 768], P(('rows', 'heads'))
- selfquery_grad: float32 [768, 768], P(None, 'heads')
- selfqbias_grad: float32 [768], P('heads')
- selfkey_grad: float32 [768, 768], P(None, 'heads')
- selfvalue_grad: float32 [768, 768], P(None, 'heads')
- selfvbias_grad: float32 [768], P('heads')
- selfout_grad: float32 [768, 768], P('heads')
- selfobias_grad: float32 [768], replicated
- firstgain_grad: float32 [768], replicated
- firstshift_grad: float32 [768], replicated
- crossquery_grad: float32 [768, 768], P(None, 'heads')
- crossqbias_grad: float32 [768], P('heads')
- crosskey_grad: float32 [768, 768], P(None, 'heads')
- crossvalue_grad: float32 [768, 768], P(None, 'heads')
- crossvbias_grad: float32 [768], P('heads')
- crossout_grad: float32 [768, 768], P('heads')
- crossobias_grad: float32 [768], replicated
- secondgain_grad: float32 [768], replicated
- secondshift_grad: float32 [768], replicated
- upweight_grad: float32 [768, 3072], P(None, ('heads', 'rows'))
- upbias_grad: float32 [3072], P(('heads', 'rows'))
- downweight_grad: float32 [3072, 768], P(('heads', 'rows'))
- downbias_grad: float32 [768], replicated
- thirdgain_grad: float32 [768], replicated
- thirdshift_grad: float32 [768], replicated
Inputs may be any that keep to these rules, and one draw needn't show every extreme that they name: `doc_lengths`: each row's 8 lengths sum to 1088; exactly one of them is 817 and the others sum to 271.
All inputs are finite; a program needn't handle non-finite values.
Results may differ from a plain program's by a relative error of at most 0.025.
The roundings to bfloat16 on the way count: a program that leaves them out, or rounds other values in their place, can miss the bound.
Values may be sent and summed in bfloat16 or wider, within the bound.
No kernel may reach another device: no remote copies, remote signals or barrier semaphores. Data moves between devices by JAX's collectives and lax.ppermute only.
A program may use at most 192 MiB of HBM per device.

v0:
```python
import jax
import jax.numpy as jnp
from jax import lax
from jax.sharding import PartitionSpec as P

HEAD = 64
ROW_TOKEN_COUNT = 1088
ENC = 1024


EPS = 1e-05


def matrix_product(left, right):
    return jnp.dot(left, right, preferred_element_type=jnp.float32)


def row_product(left, right):
    return lax.dot_general(
        left, right, (((0,), (0,)), ((), ())), preferred_element_type=jnp.float32
    )


def backward_matrix_product(left, weight):
    return lax.dot_general(
        left, weight, (((1,), (1,)), ((), ())), preferred_element_type=jnp.float32
    )


def column_sum(values):
    return jnp.sum(values.astype(jnp.float32), axis=0)


def layer_norm(values, gain, shift):
    center = values - jnp.mean(values, axis=-1, keepdims=True)
    spread = jnp.mean(center * center, axis=-1, keepdims=True)
    return center * lax.rsqrt(spread + EPS) * gain + shift


def exact_gelu(values):
    return jax.nn.gelu(values, approximate=False)


def seg_mask(lengths_row, count):
    ends = jnp.cumsum(lengths_row)
    position = lax.iota(jnp.int32, count)
    segment = jnp.sum((position[:, None] >= ends[None, :]).astype(jnp.int32), axis=1)
    return (segment[:, None] == segment[None, :]) & (position[None, :] <= position[:, None])


def scores_of(query, keys, allowed):
    scores = jnp.einsum("qhe,khe->hqk", query, keys, preferred_element_type=jnp.float32)
    if allowed is None:
        return scores
    return jnp.where(allowed[None], scores, -1000000000.0)


def attend_forward(query, keys, values, allowed):
    scores = scores_of(query, keys, allowed)
    highest = jnp.max(scores, axis=2, keepdims=True)
    raised = jnp.exp(scores - highest)
    total = jnp.sum(raised, axis=2, keepdims=True)
    shares = (raised / total).astype(jnp.bfloat16)
    output = jnp.einsum("hqk,khe->qhe", shares, values, preferred_element_type=jnp.float32)
    return (output, highest + jnp.log(total))


def attend_backward(query, keys, values, allowed, logsum, grad_out):
    scores = scores_of(query, keys, allowed)
    shares = jnp.exp(scores - logsum)
    grad_values = jnp.einsum(
        "hqk,qhe->khe", shares.astype(jnp.bfloat16), grad_out, preferred_element_type=jnp.float32
    )
    grad_shares = jnp.einsum("qhe,khe->hqk", grad_out, values, preferred_element_type=jnp.float32)
    inner_sum = jnp.sum(shares * grad_shares, axis=2, keepdims=True)
    grad_scores = (shares * (grad_shares - inner_sum)).astype(jnp.bfloat16)
    grad_query = jnp.einsum("hqk,khe->qhe", grad_scores, keys, preferred_element_type=jnp.float32)
    grad_keys = jnp.einsum("hqk,qhe->khe", grad_scores, query, preferred_element_type=jnp.float32)
    return (grad_query, grad_keys, grad_values)


def shards(
    layer_input,
    encoder_out,
    doc_lengths,
    self_query,
    self_qbias,
    self_key_weight,
    self_value,
    self_vbias,
    self_out,
    self_obias,
    first_gain,
    first_shift,
    cross_query,
    cross_qbias,
    cross_key,
    cross_value,
    cross_vbias,
    cross_out,
    cross_obias,
    second_gain,
    second_shift,
    up_weight,
    up_bias,
    down_weight,
    down_bias,
    third_gain,
    third_shift,
    out_grad,
):
    seqs = doc_lengths.shape[0]
    local_width = self_query.shape[1]
    local_heads = local_width // HEAD

    def separate_heads(values, count):
        return values.reshape(seqs, count, local_heads, HEAD)

    def join_heads(values):
        return values.reshape(-1, local_width)

    (
        gathered_rows,
        enc_all,
        squery_full,
        self_key_complete,
        svalue_full,
        sout_full,
        cquery_full,
        ckey_full,
        cvalue_full,
        cout_full,
    ) = (
        lax.all_gather(layer_input, "heads", axis=0, tiled=True),
        lax.all_gather(encoder_out, "heads", axis=0, tiled=True),
        lax.all_gather(self_query, "heads", axis=1, tiled=True),
        lax.all_gather(self_key_weight, "heads", axis=1, tiled=True),
        lax.all_gather(self_value, "heads", axis=1, tiled=True),
        lax.all_gather(self_out, "heads", axis=0, tiled=True),
        lax.all_gather(cross_query, "heads", axis=1, tiled=True),
        lax.all_gather(cross_key, "heads", axis=1, tiled=True),
        lax.all_gather(cross_value, "heads", axis=1, tiled=True),
        lax.all_gather(cross_out, "heads", axis=0, tiled=True),
    )
    document_masks = jax.vmap(lambda row: seg_mask(row, ROW_TOKEN_COUNT))(doc_lengths)
    squery = ((matrix_product(gathered_rows, self_query) + self_qbias) * 0.125).astype(jnp.bfloat16)
    self_key_rows = matrix_product(gathered_rows, self_key_weight).astype(jnp.bfloat16)
    svalues = (matrix_product(gathered_rows, self_value) + self_vbias).astype(jnp.bfloat16)
    self_query_heads4, self_key_heads4, self_value_heads4 = (
        separate_heads(squery, ROW_TOKEN_COUNT),
        separate_heads(self_key_rows, ROW_TOKEN_COUNT),
        separate_heads(svalues, ROW_TOKEN_COUNT),
    )
    self_att, self_logsumexp = lax.map(
        lambda pack: attend_forward(pack[0], pack[1], pack[2], pack[3]),
        (self_query_heads4, self_key_heads4, self_value_heads4, document_masks),
    )
    self_low = join_heads(self_att).astype(jnp.bfloat16)
    self_tok = lax.all_to_all(self_low, "heads", split_axis=0, concat_axis=1, tiled=True)
    self_branch = matrix_product(self_tok, sout_full) + self_obias
    first_sum = layer_input.astype(jnp.float32) + self_branch
    first_hidden, first_back = jax.vjp(layer_norm, first_sum, first_gain, first_shift)
    first_low = first_hidden.astype(jnp.bfloat16)
    first_all = lax.all_gather(first_low, "heads", axis=0, tiled=True)
    cquery = ((matrix_product(first_all, cross_query) + cross_qbias) * 0.125).astype(jnp.bfloat16)
    ckeys = matrix_product(enc_all, cross_key).astype(jnp.bfloat16)
    cvalues = (matrix_product(enc_all, cross_value) + cross_vbias).astype(jnp.bfloat16)
    cquery4, ckeys4, cvalues4 = (
        separate_heads(cquery, ROW_TOKEN_COUNT),
        separate_heads(ckeys, ENC),
        separate_heads(cvalues, ENC),
    )
    cross_att, cross_lse = lax.map(
        lambda pack: attend_forward(pack[0], pack[1], pack[2], None), (cquery4, ckeys4, cvalues4)
    )
    cross_low = join_heads(cross_att).astype(jnp.bfloat16)
    cross_tok = lax.all_to_all(cross_low, "heads", split_axis=0, concat_axis=1, tiled=True)
    cross_branch = matrix_product(cross_tok, cout_full) + cross_obias
    second_sum = first_hidden + cross_branch
    second_hidden, second_back = jax.vjp(layer_norm, second_sum, second_gain, second_shift)
    second_low = second_hidden.astype(jnp.bfloat16)
    upper = matrix_product(second_low, up_weight) + up_bias
    active, gelu_back = jax.vjp(exact_gelu, upper)
    active_low = active.astype(jnp.bfloat16)
    third_sum = second_hidden + matrix_product(active_low, down_weight) + down_bias
    result, third_back = jax.vjp(layer_norm, third_sum, third_gain, third_shift)
    dthird, thirdgain_g, thirdshift_g = third_back(out_grad.astype(jnp.float32))
    dbranch = dthird.astype(jnp.bfloat16)
    downbias_g = column_sum(dbranch)
    dupper = gelu_back(backward_matrix_product(dbranch, down_weight))[0].astype(jnp.bfloat16)
    dsecond, secondgain_g, secondshift_g = second_back(
        dthird + backward_matrix_product(dupper, up_weight)
    )
    dcross = dsecond.astype(jnp.bfloat16)
    crossobias_g = column_sum(dcross)
    dcross_all = lax.all_gather(dcross, "heads", axis=0, tiled=True)
    crossout_g = row_product(cross_low, dcross_all)
    dcross_att = separate_heads(
        backward_matrix_product(dcross_all, cross_out).astype(jnp.bfloat16), ROW_TOKEN_COUNT
    )
    cgrad_q, cgrad_k, cgrad_v = lax.map(
        lambda pack: attend_backward(pack[0], pack[1], pack[2], None, pack[3], pack[4]),
        (cquery4, ckeys4, cvalues4, cross_lse, dcross_att),
    )
    cross_dq = (join_heads(cgrad_q) * 0.125).astype(jnp.bfloat16)
    cross_dk = join_heads(cgrad_k).astype(jnp.bfloat16)
    cross_dv = join_heads(cgrad_v).astype(jnp.bfloat16)
    crossquery_g = row_product(first_all, cross_dq)
    crossqbias_g = column_sum(cross_dq)
    crosskey_g = row_product(enc_all, cross_dk)
    crossvalue_g = row_product(enc_all, cross_dv)
    crossvbias_g = column_sum(cross_dv)
    cdq_tok, cdk_tok, cdv_tok = (
        lax.all_to_all(cross_dq, "heads", split_axis=0, concat_axis=1, tiled=True),
        lax.all_to_all(cross_dk, "heads", split_axis=0, concat_axis=1, tiled=True),
        lax.all_to_all(cross_dv, "heads", split_axis=0, concat_axis=1, tiled=True),
    )
    first_cross = backward_matrix_product(cdq_tok, cquery_full)
    encoder_g = backward_matrix_product(cdk_tok, ckey_full) + backward_matrix_product(
        cdv_tok, cvalue_full
    )
    dfirst, firstgain_g, firstshift_g = first_back(dsecond + first_cross)
    dself = dfirst.astype(jnp.bfloat16)
    selfobias_g = column_sum(dself)
    dself_all = lax.all_gather(dself, "heads", axis=0, tiled=True)
    selfout_g = row_product(self_low, dself_all)
    self_attention_gradient = separate_heads(
        backward_matrix_product(dself_all, self_out).astype(jnp.bfloat16), ROW_TOKEN_COUNT
    )
    sgrad_q, sgrad_k, sgrad_v = lax.map(
        lambda pack: attend_backward(pack[0], pack[1], pack[2], pack[3], pack[4], pack[5]),
        (
            self_query_heads4,
            self_key_heads4,
            self_value_heads4,
            document_masks,
            self_logsumexp,
            self_attention_gradient,
        ),
    )
    self_dq = (join_heads(sgrad_q) * 0.125).astype(jnp.bfloat16)
    self_dk = join_heads(sgrad_k).astype(jnp.bfloat16)
    self_dv = join_heads(sgrad_v).astype(jnp.bfloat16)
    selfquery_g = row_product(gathered_rows, self_dq)
    selfqbias_g = column_sum(self_dq)
    selfkey_g = row_product(gathered_rows, self_dk)
    selfvalue_g = row_product(gathered_rows, self_dv)
    selfvbias_g = column_sum(self_dv)
    sdq_tok, self_key_token_gradient, sdv_tok = (
        lax.all_to_all(self_dq, "heads", split_axis=0, concat_axis=1, tiled=True),
        lax.all_to_all(self_dk, "heads", split_axis=0, concat_axis=1, tiled=True),
        lax.all_to_all(self_dv, "heads", split_axis=0, concat_axis=1, tiled=True),
    )
    input_g = (
        backward_matrix_product(sdq_tok, squery_full)
        + backward_matrix_product(self_key_token_gradient, self_key_complete)
        + backward_matrix_product(sdv_tok, svalue_full)
        + dfirst
    )
    (
        selfquery_g,
        selfqbias_g,
        selfkey_g,
        selfvalue_g,
        selfvbias_g,
        selfout_g,
        crossquery_g,
        crossqbias_g,
        crosskey_g,
        crossvalue_g,
        crossvbias_g,
        crossout_g,
    ) = lax.psum(
        (
            selfquery_g,
            selfqbias_g,
            selfkey_g,
            selfvalue_g,
            selfvbias_g,
            selfout_g,
            crossquery_g,
            crossqbias_g,
            crosskey_g,
            crossvalue_g,
            crossvbias_g,
            crossout_g,
        ),
        "rows",
    )
    upweight_g, downweight_g, upbias_g = (
        lax.psum_scatter(
            row_product(second_low, dupper), ("heads", "rows"), scatter_dimension=1, tiled=True
        ),
        lax.psum_scatter(
            row_product(active_low, dbranch), ("heads", "rows"), scatter_dimension=0, tiled=True
        ),
        lax.psum_scatter(column_sum(dupper), ("heads", "rows"), scatter_dimension=0, tiled=True),
    )
    (
        downbias_g,
        selfobias_g,
        crossobias_g,
        firstgain_g,
        firstshift_g,
        secondgain_g,
        secondshift_g,
        thirdgain_g,
        thirdshift_g,
    ) = lax.psum(
        (
            downbias_g,
            selfobias_g,
            crossobias_g,
            firstgain_g,
            firstshift_g,
            secondgain_g,
            secondshift_g,
            thirdgain_g,
            thirdshift_g,
        ),
        ("heads", "rows"),
    )
    return (
        result.astype(jnp.bfloat16),
        input_g.astype(jnp.bfloat16),
        encoder_g.astype(jnp.bfloat16),
        selfquery_g,
        selfqbias_g,
        selfkey_g,
        selfvalue_g,
        selfvbias_g,
        selfout_g,
        selfobias_g,
        firstgain_g,
        firstshift_g,
        crossquery_g,
        crossqbias_g,
        crosskey_g,
        crossvalue_g,
        crossvbias_g,
        crossout_g,
        crossobias_g,
        secondgain_g,
        secondshift_g,
        upweight_g,
        upbias_g,
        downweight_g,
        downbias_g,
        thirdgain_g,
        thirdshift_g,
    )


def solution(mesh):
    return jax.shard_map(
        shards,
        mesh=mesh,
        in_specs=(
            P(("rows", "heads"), None),
            P(("rows", "heads"), None),
            P("rows", None),
            P(None, "heads"),
            P("heads"),
            P(None, "heads"),
            P(None, "heads"),
            P("heads"),
            P("heads", None),
            P(),
            P(),
            P(),
            P(None, "heads"),
            P("heads"),
            P(None, "heads"),
            P(None, "heads"),
            P("heads"),
            P("heads", None),
            P(),
            P(),
            P(),
            P(),
            P(),
            P(),
            P(),
            P(),
            P(),
            P(("rows", "heads"), None),
        ),
        out_specs=(
            P(("rows", "heads"), None),
            P(("rows", "heads"), None),
            P(("rows", "heads"), None),
            P(None, "heads"),
            P("heads"),
            P(None, "heads"),
            P(None, "heads"),
            P("heads"),
            P("heads", None),
            P(),
            P(),
            P(),
            P(None, "heads"),
            P("heads"),
            P(None, "heads"),
            P(None, "heads"),
            P("heads"),
            P("heads", None),
            P(),
            P(),
            P(),
            P(None, ("heads", "rows")),
            P(("heads", "rows")),
            P(("heads", "rows"), None),
            P(),
            P(),
            P(),
        ),
        check_vma=False,
    )
```

profile of v0, /device:TPU:9, one launch (start us, length us, event | category | flops | bytes accessed | tf_op | source)
XLA Modules:
  0.0 1084.2 jit_solution(13007039885798312471)
XLA Ops:
  16.5 40.2 %all-gather.14.cloned.1.call-done = bf16[2176,768]{1,0:T(8,128)(2,1)} async-done(((bf16[544,768]{1,0:T(8,128)(2,1)}), bf16[2176,768]{1,0:T(8,128)(2,1)}) %all-gather.14.cloned.1.call-update) | async-done | bytes 3342352 | tf_op jit(solution)/shard_map/all_gather | solution.py:134
  76.7 51.7 %while.52 = (s32[]{:T(128)}, bf16[2,1088,3,64]{1,3,2,0:T(8,128)(2,1)S(1)}, f32[2,3,1088,1]{2,1,3,0:T(4,128)S(1)}, bf16[2,1088,3,64]{1,3,2,0:T(8,128)(2,1)}, pred...) while((s32[]{:T(128)}, ...), condition=%wide.region_5.6_spmd, body=%wide.region_2.5_spmd.sunk | while | flops 933970752 | bytes 49367388 | solution.py:154
  78.6 7.8 fusion.227
  86.5 7.3 fusion.228
  93.8 9.0 fusion.229
  104.5 7.8 fusion.227
  112.4 7.8 fusion.228
  120.2 8.2 fusion.229
  138.5 12.4 %all-to-all-done = bf16[4,544,192]{1,2,0:T(8,128)(2,1)} async-done(((bf16[4,544,192]{1,2,0:T(8,128)(2,1)}), bf16[4,544,192]{1,2,0:T(8,128)(2,1)}, u32[]{:S(2)}, u32[]{:S(2)}) %all-to-all-start) | async-done | bytes 835616 | tf_op jit(solution)/shard_map/all_to_all | solution.py:159
  167.1 34.8 %all-gather.20.cloned.1.call-done = bf16[2176,768]{1,0:T(8,128)(2,1)} async-done(((bf16[544,768]{1,0:T(8,128)(2,1)}), bf16[2176,768]{1,0:T(8,128)(2,1)}) %all-gather.20.cloned.1.call-update) | async-done | bytes 3342352 | tf_op jit(solution)/shard_map/all_gather | solution.py:164
  208.2 44.6 %while.53 = (s32[]{:T(128)}, bf16[2,1088,3,64]{1,3,2,0:T(8,128)(2,1)}, f32[2,3,1088,1]{2,1,3,0:T(4,128)S(1)}, bf16[2,1024,3,64]{1,3,2,0:T(8,128)(2,1)}, bf16[2,1...) while((s32[]{:T(128)}, bf16[2,1088,3,64]{1,3,2,0:T(8,128)(2,1)}, ...), condition=%wide.region_11.12_spmd, body=%wide.region_8.11_spmd.sunk | while | flops 875688768 | bytes 45451628 | solution.py:173
  208.6 6.8 fusion.231
  215.4 7.1 fusion.232
  222.5 8.3 fusion.233
  230.8 6.8 fusion.231
  237.6 7.1 fusion.232
  244.7 8.1 fusion.233
  262.1 4.2 all-to-all-start.1
  266.4 12.5 %all-to-all-done.1 = bf16[4,544,192]{1,2,0:T(8,128)(2,1)} async-done(((bf16[4,544,192]{1,2,0:T(8,128)(2,1)}), bf16[4,544,192]{1,2,0:T(8,128)(2,1)}, u32[]{:S(2)}, u32[]{:S(2)}) %all-to-all-start.1) | async-done | bytes 835616 | tf_op jit(solution)/shard_map/all_to_all | solution.py:177
  282.3 20.8 %multiply_convert_fusion.2 = (bf16[544,3072]{1,0:T(8,128)(2,1)S(1)}, f32[544,3072]{1,0:T(8,128)}, f32[544,3072]{1,0:T(8,128)}) fusion(f32[3072]{0:T(1024)S(1)} %copy-done.82, bf16[768,3072]{1,0:T(8,128)(2,1)} %param.57, f32[544,768]{1,0:T(8,128)S(1)} %get-tuple-element.470, f32[768]{0:T(1024)S(1)} %copy-done.86, f32[768]{0:T(1024)S(1)} %copy-done.79, ...), kind=kOutput, calls=%fused_computation.107 | convolution fusion | flops 2679300096 | bytes 23124224 | tf_op jit(solution)/shard_map/dot_general | solution.py:15
  310.3 10.1 convert_reduce_fusion
  320.4 7.2 multiply_reduce_fusion.2
  332.1 45.7 %all-gather.24.cloned.1.call-done = bf16[2176,768]{1,0:T(8,128)(2,1)} async-done(((bf16[544,768]{1,0:T(8,128)(2,1)}), bf16[2176,768]{1,0:T(8,128)(2,1)}) %all-gather.24.cloned.1.call-update) | async-done | bytes 3342352 | tf_op jit(solution)/shard_map/all_gather | solution.py:196
  385.4 46.5 %while.54 = (s32[]{:T(128)}, f32[2,1088,3,64]{1,3,2,0:T(8,128)}, bf16[2,1024,3,64]{1,3,2,0:T(8,128)(2,1)}, bf16[2,1024,3,64]{1,3,2,0:T(8,128)(2,1)}, bf16[2,1024...) while((s32[]{:T(128)}, f32[2,1088,3,64]{1,3,2,0:T(8,128)}, ...), condition=%wide.region_22.23_spmd, body=%wide.region_20.22_spmd.sunk | while | flops 2169172736 | bytes 125445088 | solution.py:201
  387.7 6.5 multiply_reduce_fusion.11
  394.3 6.8 multiply_convert_fusion.9
  410.9 6.5 multiply_reduce_fusion.11
  417.4 6.6 multiply_convert_fusion.9
  439.4 4.2 all-to-all-start.2
  443.7 12.4 %all-to-all-done.2 = bf16[4,544,192]{1,2,0:T(8,128)(2,1)} async-done(((bf16[4,544,192]{1,2,0:T(8,128)(2,1)}), bf16[4,544,192]{1,2,0:T(8,128)(2,1)}, u32[]{:S(2)}, u32[]{:S(2)}) %all-to-all-start.2) | async-done | bytes 835616 | tf_op jit(solution)/shard_map/all_to_all | solution.py:214
  467.4 9.8 fusion.111
  481.6 9.7 fusion.130
  501.5 4.4 all-to-all-start.6
  522.7 73.6 %while.55 = (s32[]{:T(128)}, f32[2,1088,3,64]{1,3,2,0:T(8,128)}, bf16[2,1088,3,64]{1,3,2,0:T(8,128)(2,1)}, bf16[2,1088,3,64]{1,3,2,0:T(8,128)(2,1)}, bf16[2,1088...) while((s32[]{:T(128)}, f32[2,1088,3,64]{1,3,2,0:T(8,128)}, ...), condition=%wide.region_27.28_spmd, body=%wide.region_25.27_spmd.sunk | while | flops 2301195008 | bytes 134269136 | solution.py:230
  522.7 8.6 fusion.254
  534.0 8.5 multiply_reduce_fusion.12
  542.5 7.0 multiply_convert_fusion.10
  559.2 8.6 fusion.254
  570.6 8.5 multiply_reduce_fusion.12
  579.1 7.2 multiply_convert_fusion.10
  623.0 6.4 all-to-all-done.7
  629.4 4.2 all-to-all-start.3
  652.7 48.1 %all-reduce.1 = (f32[768]{0:T(1024)}, f32[768]{0:T(1024)}, f32[768]{0:T(1024)}, f32[768]{0:T(1024)}, f32[768]{0:T(1024)}, /*index=5*/f32[768]{0:T(1024)}, f32[30...) all-reduce(f32[768]{0:T(1024)S(1)} %copy-done.64, ...), channel_id=1, replica_groups=mesh['heads'=4,'rows'=8] {'heads','rows'}, use_global_device_ids=true, to_apply=%region_37.38 | all-reduce | flops 9984 | bytes 79872 | tf_op jit(solution)/shard_map/psum | solution.py:309
  703.6 11.3 %all-reduce.2 = (f32[192]{0:T(256)}, f32[192]{0:T(256)}, f32[192]{0:T(256)}, f32[192]{0:T(256)}) all-reduce(f32[192]{0:T(256)S(1)} %reduce_sum.349, f32[192]{0:T(256)S(1)} %reduce_sum.351, f32[192]{0:T(256)S(1)} %reduce_sum.356, f32[192]{0:T(256)S(1)} %reduce_sum.358), channel_id=1, replica_groups=mesh['heads'=4,'rows'=8] {'rows'}, use_global_device_ids=true, to_apply=%region_30.31 | all-reduce | flops 768 | bytes 6144 | tf_op jit(solution)/shard_map/psum | solution.py:273
  726.9 9.5 all-to-all-done.5
  740.6 70.4 %reduce-scatter.3.cloned.1.call-done = f32[768,96]{0,1:T(8,128)} async-done(((f32[768,3072]{0,1:T(8,128)}), f32[768,96]{0,1:T(8,128)}) %reduce-scatter.3.cloned.1.call-update) | async-done | bytes 294928 | tf_op jit(solution)/shard_map/reduce_scatter | solution.py:291
  811.0 141.8 %reduce-scatter.5.cloned.1.call-done = f32[96,768]{1,0:T(8,128)} async-done(((f32[3072,768]{1,0:T(8,128)}), f32[96,768]{1,0:T(8,128)}) %reduce-scatter.5.cloned.1.call-update) | async-done | bytes 294928 | tf_op jit(solution)/shard_map/reduce_scatter | solution.py:294
  952.8 114.6 %all-reduce.6.cloned.1.call-done = (f32[768,192]{0,1:T(8,128)}, f32[768,192]{0,1:T(8,128)}, f32[768,192]{0,1:T(8,128)}, f32[192,768]{1,0:T(8,128)}, f32[768,192]...) async-done(((f32[768,192]{0,1:T(8,128)}, f32[768,192]{0,1:T(8,128)}, f32[768,192]{0,1:T(8,128)}, f32[192,768]{1,0:T(8,128)}, ...) | async-done | bytes 4718608 | tf_op jit(solution)/shard_map/psum | solution.py:273
  (408 shorter events, 265.5 us)
Async XLA Ops:
  7.2 49.5 %all-gather.14.cloned.1.call-start = ((), (), s32[]{:S(2)}) async-start(), calls=%async_computation.10 | async-start | bytes 4177920 | tf_op jit(solution)/shard_map/all_gather | solution.py:134
  7.9 130.5 %all-gather.16.cloned.1.call-start = ((), (), s32[]{:S(2)}) async-start(), calls=%async_computation.11 | async-start | bytes 1474560 | tf_op jit(solution)/shard_map/all_gather | solution.py:139
  8.7 149.4 %all-gather.18.cloned.1.call-start = ((), (), s32[]{:S(2)}) async-start(), calls=%async_computation.12 | async-start | bytes 3932160 | tf_op jit(solution)/shard_map/all_gather | solution.py:135
  9.8 46.9 %copy-start.48 = (bf16[768,192]{0,1:T(8,128)(2,1)S(1)}, bf16[768,192]{0,1:T(8,128)(2,1)}, u32[]{:S(2)}) copy-start(bf16[768,192]{0,1:T(8,128)(2,1)} %param.42) | copy-start | bytes 884740
  9.8 46.9 %copy-start.88 = (f32[192]{0:T(256)S(1)}, f32[192]{0:T(256)}, u32[]{:S(2)}) copy-start(f32[192]{0:T(256)} %param.43) | copy-start | bytes 2308
  130.0 20.9 %copy-start.13 = (bf16[2,1088,3,64]{1,0,3,2:T(2,128)(2,1)}, bf16[2,1088,3,64]{1,0,3,2:T(2,128)(2,1)S(1)}, u32[]{:S(2)}) copy-start(bf16[2,1088,3,64]{1,0,3,2:T(2,128)(2,1)S(1)} %copy.164) | copy-start | bytes 2506756
  130.0 20.9 %copy-start.83 = (f32[768]{0:T(1024)S(1)}, f32[768]{0:T(1024)}, u32[]{:S(2)}) copy-start(f32[768]{0:T(1024)} %param.45) | copy-start | bytes 9220
  134.2 16.7 %all-to-all-start = ((bf16[4,544,192]{1,2,0:T(8,128)(2,1)}), bf16[4,544,192]{1,2,0:T(8,128)(2,1)}, u32[]{:S(2)}, u32[]{:S(2)}) async-start(bf16[4,544,192]{1,2,0:T(8,128)(2,1)} %copy.165), calls=%async_computation | async-start | bytes 1966080 | tf_op jit(solution)/shard_map/all_to_all | solution.py:159
  138.4 63.6 %all-gather.20.cloned.1.call-start = ((), (), s32[]{:S(2)}) async-start(), calls=%async_computation.13 | async-start | bytes 4177920 | tf_op jit(solution)/shard_map/all_gather | solution.py:164
  153.7 125.2 %copy-start.8 = (f32[544,768]{1,0:T(8,128)}, f32[544,768]{1,0:T(8,128)S(1)}, u32[]{:S(2)}) copy-start(f32[544,768]{1,0:T(8,128)S(1)} %get-tuple-element.468) | copy-start | bytes 5013508
  153.7 125.2 %copy-start.49 = (f32[544]{0:T(1024)}, f32[544]{0:T(1024)S(1)}, u32[]{:S(2)}) copy-start(f32[544]{0:T(1024)S(1)} %broadcast_multiply_fusion.2) | copy-start | bytes 6532
  154.1 124.8 %copy-start.55 = (f32[544]{0:T(1024)}, f32[544]{0:T(1024)S(1)}, u32[]{:S(2)}) copy-start(f32[544]{0:T(1024)S(1)} %fusion.108) | copy-start | bytes 6532
  155.4 111.0 %all-gather.22.cloned.1.call-start = ((), (), s32[]{:S(2)}) async-start(), calls=%async_computation.14 | async-start | bytes 1474560 | tf_op jit(solution)/shard_map/all_gather | solution.py:143
  162.9 39.1 %copy-start.91 = (f32[192]{0:T(256)S(1)}, f32[192]{0:T(256)}, u32[]{:S(2)}) copy-start(f32[192]{0:T(256)} %param.49) | copy-start | bytes 2308
  255.8 23.1 %copy-start.84 = (f32[768]{0:T(1024)S(1)}, f32[768]{0:T(1024)}, u32[]{:S(2)}) copy-start(f32[768]{0:T(1024)} %param.54) | copy-start | bytes 9220
  262.1 16.8 %all-to-all-start.1 = ((bf16[4,544,192]{1,2,0:T(8,128)(2,1)}), bf16[4,544,192]{1,2,0:T(8,128)(2,1)}, u32[]{:S(2)}, u32[]{:S(2)}) async-start(bf16[4,544,192]{1,2,0:T(8,128)(2,1)} %copy.170), calls=%async_computation.1 | async-start | bytes 1966080 | tf_op jit(solution)/shard_map/all_to_all | solution.py:177
  266.3 111.5 %all-gather.24.cloned.1.call-start = ((), (), s32[]{:S(2)}) async-start(), calls=%async_computation.15 | async-start | bytes 4177920 | tf_op jit(solution)/shard_map/all_gather | solution.py:196
  279.0 24.1 %slice-start = ((s8[4718592]{0:T(1024)(128)(4,1)}), s8[4194304]{0:T(1024)(128)(4,1)S(1)}, s32[]{:S(2)}) async-start(s8[4718592]{0:T(1024)(128)(4,1)} %bitcast.362), calls=%async_computation.26 | async-start | bytes 8388608
  281.8 45.8 %copy-start.24 = (f32[544,768]{1,0:T(8,128)}, f32[544,768]{1,0:T(8,128)S(1)}, u32[]{:S(2)}) copy-start(f32[544,768]{1,0:T(8,128)S(1)} %get-tuple-element.470) | copy-start | bytes 5013508
  281.9 45.8 %copy-start.57 = (f32[544]{0:T(1024)}, f32[544]{0:T(1024)S(1)}, u32[]{:S(2)}) copy-start(f32[544]{0:T(1024)S(1)} %broadcast_multiply_fusion.1) | copy-start | bytes 6532
  282.3 45.4 %copy-start.69 = (f32[544]{0:T(1024)}, f32[544]{0:T(1024)S(1)}, u32[]{:S(2)}) copy-start(f32[544]{0:T(1024)S(1)} %fusion.109) | copy-start | bytes 6532
  282.3 20.8 %slice-start.1 = ((s8[4718592]{0:T(1024)(128)(4,1)}), s8[524288]{0:T(1024)(128)(4,1)S(1)}, s32[]{:S(2)}) async-start(s8[4718592]{0:T(1024)(128)(4,1)} %bitcast.362), calls=%async_computation.27 | async-start | bytes 1048576
  282.3 20.8 %copy-start.85 = (f32[768]{0:T(1024)S(1)}, f32[768]{0:T(1024)}, u32[]{:S(2)}) copy-start(f32[768]{0:T(1024)} %param.60) | copy-start | bytes 9220
  327.7 50.1 %copy-start.44 = (bf16[192,768]{1,0:T(8,128)(2,1)S(1)}, bf16[192,768]{1,0:T(8,128)(2,1)}, u32[]{:S(2)}) copy-start(bf16[192,768]{1,0:T(8,128)(2,1)} %param.53) | copy-start | bytes 884740
  328.4 49.4 %copy-start.65 = (f32[544]{0:T(1024)}, f32[544]{0:T(1024)S(1)}, u32[]{:S(2)}) copy-start(f32[544]{0:T(1024)S(1)} %negate_multiply_fusion.2) | copy-start | bytes 6532
  331.3 112.4 %all-gather.26.cloned.1.call-start = ((), (), s32[]{:S(2)}) async-start(), calls=%async_computation.16 | async-start | bytes 1474560 | tf_op jit(solution)/shard_map/all_gather | solution.py:140
  435.2 21.0 %copy-start.9 = (f32[544,768]{1,0:T(8,128)S(1)}, f32[544,768]{1,0:T(8,128)}, u32[]{:S(2)}) copy-start(f32[544,768]{1,0:T(8,128)} %copy-done.8) | copy-start | bytes 5013508
  435.2 21.0 %copy-start.50 = (f32[544]{0:T(1024)S(1)}, f32[544]{0:T(1024)}, u32[]{:S(2)}) copy-start(f32[544]{0:T(1024)} %copy-done.49) | copy-start | bytes 6532
  435.2 21.0 %copy-start.56 = (f32[544]{0:T(1024)S(1)}, f32[544]{0:T(1024)}, u32[]{:S(2)}) copy-start(f32[544]{0:T(1024)} %copy-done.55) | copy-start | bytes 6532
  435.2 20.9 %copy-start.66 = (f32[544]{0:T(1024)S(1)}, f32[544]{0:T(1024)}, u32[]{:S(2)}) copy-start(f32[544]{0:T(1024)} %copy-done.65) | copy-start | bytes 6532
  435.2 20.9 %copy-start.68 = (f32[768]{0:T(1024)S(1)}, f32[768]{0:T(1024)}, u32[]{:S(2)}) copy-start(f32[768]{0:T(1024)} %param.46) | copy-start | bytes 9220
  439.4 16.7 %all-to-all-start.2 = ((bf16[4,544,192]{1,2,0:T(8,128)(2,1)}), bf16[4,544,192]{1,2,0:T(8,128)(2,1)}, u32[]{:S(2)}, u32[]{:S(2)}) async-start(bf16[4,544,192]{1,2,0:T(8,128)(2,1)} %copy.176), calls=%async_computation.2 | async-start | bytes 1966080 | tf_op jit(solution)/shard_map/all_to_all | solution.py:214
  443.6 72.7 %all-gather.28.cloned.1.call-start = ((), (), s32[]{:S(2)}) async-start(), calls=%async_computation.17 | async-start | bytes 4177920 | tf_op jit(solution)/shard_map/all_gather | solution.py:225
  461.0 16.2 %copy-start.51 = (f32[544]{0:T(1024)}, f32[544]{0:T(1024)S(1)}, u32[]{:S(2)}) copy-start(f32[544]{0:T(1024)S(1)} %negate_multiply_fusion.1) | copy-start | bytes 6532
  463.9 181.3 %all-gather.36.cloned.1.call-start = ((), (), s32[]{:S(2)}) async-start(), calls=%async_computation.21 | async-start | bytes 1474560 | tf_op jit(solution)/shard_map/all_gather | solution.py:141
  464.6 184.2 %all-gather.38.cloned.1.call-start = ((), (), s32[]{:S(2)}) async-start(), calls=%async_computation.22 | async-start | bytes 1474560 | tf_op jit(solution)/shard_map/all_gather | solution.py:142
  465.2 254.3 %all-gather.30.cloned.1.call-start = ((), (), s32[]{:S(2)}) async-start(), calls=%async_computation.18 | async-start | bytes 1474560 | tf_op jit(solution)/shard_map/all_gather | solution.py:136
  465.9 257.2 %all-gather.32.cloned.1.call-start = ((), (), s32[]{:S(2)}) async-start(), calls=%async_computation.19 | async-start | bytes 1474560 | tf_op jit(solution)/shard_map/all_gather | solution.py:137
  466.5 260.4 %all-gather.34.cloned.1.call-start = ((), (), s32[]{:S(2)}) async-start(), calls=%async_computation.20 | async-start | bytes 1474560 | tf_op jit(solution)/shard_map/all_gather | solution.py:138
  467.3 343.7 %reduce-scatter.3.cloned.1.call-start = ((), (), s32[]{:S(2)}) async-start(), calls=%async_computation.23 | async-start | bytes 9732096 | tf_op jit(solution)/shard_map/reduce_scatter | solution.py:291
  477.2 475.5 %reduce-scatter.5.cloned.1.call-start = ((), (), s32[]{:S(2)}) async-start(), calls=%async_computation.24 | async-start | bytes 9732096 | tf_op jit(solution)/shard_map/reduce_scatter | solution.py:294
  501.5 112.7 %all-to-all-start.6 = ((bf16[4,512,192]{1,2,0:T(8,128)(2,1)}), bf16[4,512,192]{1,2,0:T(8,128)(2,1)}, u32[]{:S(2)}, u32[]{:S(2)}) async-start(bf16[4,512,192]{1,2,0:T(8,128)(2,1)} %copy.188), calls=%async_computation.6 | async-start | bytes 1572864 | tf_op jit(solution)/shard_map/all_to_all | solution.py:215
  614.2 15.2 %all-to-all-start.7 = ((bf16[4,512,192]{1,2,0:T(8,128)(2,1)}), bf16[4,512,192]{1,2,0:T(8,128)(2,1)}, u32[]{:S(2)}, u32[]{:S(2)}) async-start(bf16[4,512,192]{1,2,0:T(8,128)(2,1)} %copy.190), calls=%async_computation.7 | async-start | bytes 1572864 | tf_op jit(solution)/shard_map/all_to_all | solution.py:216
  629.4 12.2 %all-to-all-start.3 = ((bf16[4,544,192]{1,2,0:T(8,128)(2,1)}), bf16[4,544,192]{1,2,0:T(8,128)(2,1)}, u32[]{:S(2)}, u32[]{:S(2)}) async-start(bf16[4,544,192]{1,2,0:T(8,128)(2,1)} %copy.182), calls=%async_computation.3 | async-start | bytes 1966080 | tf_op jit(solution)/shard_map/all_to_all | solution.py:250
  633.6 433.8 %all-reduce.6.cloned.1.call-start = ((), (), s32[]{:S(2)}) async-start(), calls=%async_computation.25 | async-start | bytes 9437184 | tf_op jit(solution)/shard_map/psum | solution.py:273
  641.6 73.3 %all-to-all-start.4 = ((bf16[4,544,192]{1,2,0:T(8,128)(2,1)}), bf16[4,544,192]{1,2,0:T(8,128)(2,1)S(1)}, u32[]{:S(2)}, u32[]{:S(2)}) async-start(bf16[4,544,192]{1,2,0:T(8,128)(2,1)} %copy.184), calls=%async_computation.4 | async-start | bytes 1966080 | tf_op jit(solution)/shard_map/all_to_all | solution.py:251
  648.8 52.6 %copy-start.17 = (bf16[2,1088,3,64]{1,0,3,2:T(2,128)(2,1)S(1)}, bf16[2,1088,3,64]{1,0,3,2:T(2,128)(2,1)}, u32[]{:S(2)}) copy-start(bf16[2,1088,3,64]{1,0,3,2:T(2,128)(2,1)} %copy-done.16) | copy-start | bytes 2506756
  715.9 20.5 %all-to-all-start.5 = ((bf16[4,544,192]{1,2,0:T(8,128)(2,1)}), bf16[4,544,192]{1,2,0:T(8,128)(2,1)S(1)}, u32[]{:S(2)}, u32[]{:S(2)}) async-start(bf16[4,544,192]{1,2,0:T(8,128)(2,1)} %copy.186), calls=%async_computation.5 | async-start | bytes 1966080 | tf_op jit(solution)/shard_map/all_to_all | solution.py:252
  (79 other events, 339.6 us)
Sparse Core Ops, SparseCore 0:
  9.9 46.7 all-gather.13
  58.5 27.7 all-gather.15
  88.1 43.9 all-gather.17
  155.5 46.4 all-gather.19
  203.6 27.7 all-gather.21
  331.4 46.2 all-gather.23
  379.6 27.7 all-gather.25
  464.0 48.0 all-gather.27
  514.0 30.9 all-gather.35
  546.6 27.7 all-gather.37
  576.2 27.7 all-gather.29
  605.7 30.6 all-gather.31
  638.2 31.6 all-gather.33
  676.2 134.7 reduce-scatter.2
  818.3 134.3 reduce-scatter.4
  957.3 110.0 all-reduce.5
where the time goes:
time: 1090 us; the launch traced here: 1080 us
  waiting for transfers between devices  508 us (47%)
  matrix products  281 us (26%)
  local copies, waits for them, and re-layouts  107 us (10%)
  other arithmetic  78.6 us (7%)
  blocking collectives  59.4 us (5%)
  starting transfers between devices  33.3 us (3%)
  between operations  15.4 us (1%)
    reduce_scatter x1, waiting for transfers between devices, shards(): lax.psum_scatter(row_product(active_low, dbranch), ('heads', 'rows'), sca...  142 us
    psum x1, waiting for transfers between devices, shards(): lax.psum((selfquery_g, selfqbias_g, selfkey_g, selfvalue_g, selfvbias_g,...  115 us
    reduce_scatter x1, waiting for transfers between devices, shards(): lax.psum_scatter(row_product(second_low, dupper), ('heads', 'rows'), scat...  70.4 us
    dot_general x8, matrix products, scores_of(): jnp.einsum('qhe,khe->hqk', query, keys, preferred_element_type=jnp.float32)  50 us
    dot_general x10, matrix products, matrix_product(): return jnp.dot(left, right, preferred_element_type=jnp.float32)  49.6 us
    psum x1, blocking collectives, shards(): lax.psum((downbias_g, selfobias_g, crossobias_g, firstgain_g, firstshift_...  48.1 us
    dot_general x10, matrix products, backward_matrix_product(): lax.dot_general(left, weight, (((1,), (1,)), ((), ())), preferred_element...  46.7 us
    all_gather x1, waiting for transfers between devices, shards(): dcross_all = lax.all_gather(dcross, 'heads', axis=0, tiled=True)  45.7 us
  transfers between devices with their start and end apart: 24, of which 12 were waited for; matrix products, arithmetic and copies ran while one was open for 36% of the time, Pallas kernels for 0%

commit v1 on v0

v1 whole, which is shorter than its diff:
```python
import jax
import jax.numpy as jnp
from jax import lax
from jax.experimental import pallas as pl
from jax.experimental.pallas import tpu as pltpu
from jax.sharding import PartitionSpec as P

BF = jnp.bfloat16
F32 = jnp.float32
HEAD = 64
PAIR = 128
EPS = 1e-05
ROW = 1088
CHUNK = 272
OWN = 544
ENC = 1024
HALF_ENC = 512
D = 768
GROUP = 192
PIECE = 96
FF = 3072
MIB = 1 << 20


def nn(a, b):
    return jnp.dot(a, b, preferred_element_type=F32)


def nt(a, b):
    return lax.dot_general(a, b, (((1,), (1,)), ((), ())), preferred_element_type=F32)


def tn(a, b):
    return lax.dot_general(a, b, (((0,), (0,)), ((), ())), preferred_element_type=F32)


def lane_ids(shape):
    return lax.broadcasted_iota(jnp.int32, shape, len(shape) - 1)


def pair_lanes(p):
    return pl.ds(pl.multiple_of(p * PAIR, PAIR), PAIR)


def normalize(total):
    center = total - jnp.mean(total, axis=-1, keepdims=True)
    scale = lax.rsqrt(jnp.mean(center * center, axis=-1, keepdims=True) + EPS)
    return center * scale, scale


def norm_back(grad, hat, scale, gain):
    scaled = grad * gain
    inner = scaled - jnp.mean(scaled, axis=-1, keepdims=True)
    return scale * (inner - hat * jnp.mean(scaled * hat, axis=-1, keepdims=True))


def column(values):
    return jnp.sum(values.astype(F32), axis=0, keepdims=True)


def pick_lane(ref, rows, lane):
    block = ref[rows, :]
    return jnp.sum(jnp.where(lane_ids(block.shape) == lane, block, 0.0), axis=-1, keepdims=True)


def weight_copies(w, slot, core, own, near, far, dst, sems, groups=(0, 1, 2, 3)):
    copies = []
    for n, i in enumerate(groups):
        base = GROUP * n
        if i == 0:
            copies.append(
                pltpu.make_async_copy(own[w], dst.at[pl.ds(base, GROUP)], sems.at[slot, 0])
            )
            continue
        rows = pl.ds(w * PIECE, PIECE)
        for which, refs in ((core, near), (1 - core, far)):
            to = pl.multiple_of(base + PIECE * which, PIECE)
            at = i if refs is near else 3 + i
            copies.append(
                pltpu.make_async_copy(
                    refs[i - 1].at[rows], dst.at[pl.ds(to, PIECE)], sems.at[slot, at]
                )
            )
    return copies


def gathered_bias(own_line, near, which):
    lines = [own_line]
    for ref in near:
        at = 3 * which
        split = ref[at : at + 3, :GROUP].astype(F32)
        lines.append(split[0:1] + split[1:2] + split[2:3])
    return jnp.concatenate(lines, axis=1)


def start(copies):
    for one in copies:
        one.start()


def finish(copies):
    for one in copies:
        one.wait()


def by_core(core, body):
    for value in (0, 1):

        @pl.when(core == value)
        def _():
            body(value)


def store_pieces(core, block, first_group, at, own, snd):
    def put(value):
        for g in range(block.shape[0] // GROUP):
            for half in (0, 1):
                row = g * GROUP + half * PIECE
                target = own if half == value else snd
                target[first_group + g, at : at + PIECE, :] = block[row : row + PIECE]

    by_core(core, put)


def store_bias_rows(lines, own, snd, at):
    for i in range(2):
        block = jnp.concatenate([one[:, i * GROUP : (i + 1) * GROUP] for one in lines], axis=0)
        block = jnp.concatenate([block, jnp.zeros((len(lines), D - GROUP), F32)], axis=1)
        block = jnp.concatenate([block, jnp.zeros((32 - len(lines), D), F32)], axis=0).astype(BF)
        own[i, at : at + 32, :] = block
        snd[i, at : at + 32, :] = block


def forward_heads(q2, keys, values, bias, row_stats, p):
    lane = lane_ids(q2.shape)
    outs = []
    for t in (0, 1):
        query = jnp.where((lane // HEAD) == t, q2, jnp.zeros_like(q2))
        scores = nt(query, keys)
        if bias is not None:
            scores = scores + bias
        highest = jnp.max(scores, axis=-1, keepdims=True)
        raised = jnp.exp(scores - highest)
        total = jnp.sum(raised, axis=-1, keepdims=True)
        outs.append(nn(raised.astype(BF), values) / total)
        row_stats = jnp.where(
            lane_ids(row_stats.shape) == 2 * p + t, highest + jnp.log(total), row_stats
        )
    return jnp.where((lane // HEAD) == 0, outs[0], outs[1]).astype(BF), row_stats


def backward_heads(q2, g2, o2, keys, values, bias, stats, p):
    lane = lane_ids(q2.shape)
    key_lane = lane_ids(keys.shape)
    product = g2.astype(F32) * o2.astype(F32)
    zero = jnp.zeros_like(q2)
    grad_q = grad_k = grad_v = 0.0
    for t in (0, 1):
        mine = (lane // HEAD) == t
        query = jnp.where(mine, q2, zero)
        grad = jnp.where(mine, g2, zero)
        inner = jnp.sum(jnp.where(mine, product, 0.0), axis=-1, keepdims=True)
        lse = jnp.sum(
            jnp.where(lane_ids(stats.shape) == 2 * p + t, stats, 0.0), axis=-1, keepdims=True
        )
        scores = nt(query, keys)
        if bias is not None:
            scores = scores + bias
        shares = jnp.exp(scores - lse)
        grad_shares = nt(grad, values)
        grad_scores = (shares * (grad_shares - inner)).astype(BF)
        grad_v = grad_v + tn(shares.astype(BF), grad)
        grad_k = grad_k + tn(grad_scores, query)
        grad_q = grad_q + nn(
            grad_scores, jnp.where((key_lane // HEAD) == t, keys, jnp.zeros_like(keys))
        )
    return grad_q, grad_k, grad_v


def document_ends(xa, place):
    pair_at = place[1] // 2
    lengths = jnp.where(
        pair_at == 0,
        xa[CHUNK : CHUNK + 1, :8].astype(F32) * 16.0 + xa[CHUNK + 2 : CHUNK + 3, :8].astype(F32),
        xa[CHUNK + 1 : CHUNK + 2, :8].astype(F32) * 16.0
        + xa[CHUNK + 3 : CHUNK + 4, :8].astype(F32),
    )
    ends, total = [], 0.0
    for d in range(8):
        total = total + lengths[:, d : d + 1]
        ends.append(total)
    return ends


def mask_bias(ends, chunk, width):
    qpos = chunk * CHUNK + lax.broadcasted_iota(jnp.int32, (CHUNK, 1), 0)
    kpos = lax.broadcasted_iota(jnp.int32, (1, width), 1)
    qat, kat = qpos.astype(F32), kpos.astype(F32)
    qseg = jnp.zeros((CHUNK, 1), F32)
    kseg = jnp.zeros((1, width), F32)
    for end in ends:
        qseg = qseg + jnp.where(qat >= end, 1.0, 0.0)
        kseg = kseg + jnp.where(kat >= end, 1.0, 0.0)
    return jnp.where((qseg == kseg) & (kpos <= qpos), 0.0, -1000000000.0)


def chunk_of(core, which):
    return (2 * core, 3 - 2 * core, 2 - 2 * core, 1 + 2 * core)[which]


def chunk_rows(core, which):
    return pl.ds(pl.multiple_of(chunk_of(core, which) * CHUNK, 16), CHUNK)


def key_counts(core):
    return ((0, 1), (1, 4)) if core == 0 else ((0, 3), (1, 2))


def self_forward(
    place, xa, xb, ya, yb, w0, w1, w2, n1, n2, n3, f1, f2, f3, qbias, vbias,
    q_out, k_out, v_out, att, stats,
    wq, wk, wv, bias, lines, sems, line_sems,
):
    core = place[0]
    near, far = (n1, n2, n3), (f1, f2, f3)
    bias_copies = [
        pltpu.make_async_copy(ref.at[pl.ds(4 * PIECE, 16)], lines.at[i], line_sems.at[i])
        for i, ref in enumerate(near)
    ]
    sets = [
        weight_copies(w, w, core, (w0, w1, w2), near, far, dst, sems)
        for w, dst in enumerate((wq, wk, wv))
    ]
    start(bias_copies)
    for one in sets:
        start(one)
    ends = document_ends(xa, place)
    for slot in (0, 1):
        bias[slot] = mask_bias(ends, chunk_of(core, slot), ROW)
    xs = (xa[0:CHUNK, :], xb[...], ya[0:CHUNK, :], yb[...])
    finish(bias_copies)
    held = [lines.at[i] for i in range(3)]
    finish(sets[0])
    line = gathered_bias(qbias[...], held, 0)
    for which in (0, 1):
        q_out[which * CHUNK : (which + 1) * CHUNK, :] = (
            (nt(xs[which], wq[...]) + line) * 0.125
        ).astype(BF)
    finish(sets[1])
    for which, x in enumerate(xs):
        k_out[chunk_rows(core, which), :] = nt(x, wk[...]).astype(BF)
    finish(sets[2])
    line = gathered_bias(vbias[...], held, 1)
    for which, x in enumerate(xs):
        v_out[chunk_rows(core, which), :] = (nt(x, wv[...]) + line).astype(BF)
    stats[...] = jnp.zeros_like(stats)

    def attend(value):
        def pair(p, carry):
            lanes = pair_lanes(p)
            for slot, count in key_counts(value):
                rows = pl.ds(slot * CHUNK, CHUNK)
                width = count * CHUNK
                out, now = forward_heads(
                    q_out[rows, lanes], k_out[0:width, lanes], v_out[0:width, lanes],
                    bias[slot, :, 0:width], stats[rows, :], p,
                )
                att[rows, lanes] = out
                stats[rows, :] = now
            return carry

        lax.fori_loop(0, 6, pair, 0)

    by_core(core, attend)


def self_finish(
    place, xa, xb, att, w3, n1, n2, n3, f1, f2, f3, obias,
    hat_out, scale_out, wo, sems,
):
    copies = weight_copies(
        3, 0, place[0], (None, None, None, w3), (n1, n2, n3), (f1, f2, f3), wo, sems
    )
    start(copies)
    finish(copies)
    for which, x in enumerate((xa[0:CHUNK, :], xb[...])):
        rows = pl.ds(which * CHUNK, CHUNK)
        total = x.astype(F32) + (nn(att[rows, :], wo[...]) + obias[...])
        hat, scale = normalize(total)
        hat_out[rows, :] = hat
        scale_out[rows, :] = jnp.broadcast_to(scale, (CHUNK, 128))


def cross_forward(
    place, hat1, gain1, shift1, ea, eb, w0, w1, w2, w3, n1, n2, n3, f1, f2, f3,
    qbias, vbias, obias,
    q_out, k_out, v_out, att, stats, hat_out,
    wq, wk, wv, wo, lines, sems, line_sems,
):
    core = place[0]
    near, far = (n1, n2, n3), (f1, f2, f3)
    bias_copies = [
        pltpu.make_async_copy(ref.at[pl.ds(4 * PIECE, 16)], lines.at[i], line_sems.at[i])
        for i, ref in enumerate(near)
    ]
    sets = [
        weight_copies(w, w, core, (w0, w1, w2, w3), near, far, dst, sems)
        for w, dst in enumerate((wq, wk, wv, wo))
    ]
    start(bias_copies)
    for one in (1, 2, 0, 3):
        start(sets[one])
    finish(bias_copies)
    held = [lines.at[i] for i in range(3)]
    finish(sets[1])
    for which, e in enumerate((ea, eb)):
        rows = pl.ds(which * HALF_ENC, HALF_ENC)
        k_out[rows, :] = nt(e[...], wk[...]).astype(BF)
    finish(sets[2])
    line = gathered_bias(vbias[...], held, 1)
    for which, e in enumerate((ea, eb)):
        rows = pl.ds(which * HALF_ENC, HALF_ENC)
        v_out[rows, :] = (nt(e[...], wv[...]) + line).astype(BF)
    finish(sets[0])
    line = gathered_bias(qbias[...], held, 0)
    for slot in (0, 1):
        rows = pl.ds(slot * CHUNK, CHUNK)
        hidden = (hat1[rows, :] * gain1[...] + shift1[...]).astype(BF)
        q_out[rows, :] = ((nt(hidden, wq[...]) + line) * 0.125).astype(BF)
    stats[...] = jnp.zeros_like(stats)

    def pair(p, carry):
        lanes = pair_lanes(p)
        for slot in (0, 1):
            rows = pl.ds(slot * CHUNK, CHUNK)
            out, now = forward_heads(
                q_out[rows, lanes], k_out[:, lanes], v_out[:, lanes], None, stats[rows, :], p
            )
            att[rows, lanes] = out
            stats[rows, :] = now
        return carry

    lax.fori_loop(0, 6, pair, 0)
    finish(sets[3])
    for slot in (0, 1):
        rows = pl.ds(slot * CHUNK, CHUNK)
        hidden = hat1[rows, :] * gain1[...] + shift1[...]
        total = hidden + (nn(att[rows, :], wo[...]) + obias[...])
        hat, scale = normalize(total)
        hat_out[rows, :] = hat
        block = stats[rows, :]
        stats[rows, :] = jnp.where(lane_ids(block.shape) == 12, scale, block)


FF_STEP = 512
FF_BLOCK = 384


def gelu_parts(u):
    size = jnp.abs(u)
    t = 1.0 / (1.0 + (0.3275911 * 0.7071067811865476) * size)
    poly = t * (
        0.254829592
        + t * (-0.284496736 + t * (1.421413741 + t * (-1.453152027 + t * 1.061405429)))
    )
    bell = jnp.exp(-0.5 * u * u)
    tail = 0.5 * poly * bell
    phi = jnp.where(u >= 0.0, 1.0 - tail, tail)
    return u * phi, phi + u * bell * 0.3989422804014327


def feed_forward(piece):
    def kernel(
        place, hat2, stats, gain2, shift2, up_hbm, up_bias, down_hbm, down_bias, gain3, shift3,
        ga, gb,
        out, dsecond, own, snd, vec, upb,
        up, down, active, slope, hid, total, third, sems,
    ):
        core, group = place[0], place[1]
        steps = FF // FF_STEP
        ups = [
            pltpu.make_async_copy(
                up_hbm.at[:, pl.ds(i * FF_STEP, FF_STEP)],
                up.at[:, pl.ds(i * FF_STEP, FF_STEP)],
                sems.at[0, i],
            )
            for i in range(steps)
        ]
        downs = [
            pltpu.make_async_copy(
                down_hbm.at[pl.ds(i * FF_STEP, FF_STEP)],
                down.at[pl.ds(i * FF_STEP, FF_STEP)],
                sems.at[1, i],
            )
            for i in range(steps)
        ]
        for i in range(steps):
            ups[i].start()
            downs[i].start()
        second = hat2[...] * gain2[...] + shift2[...]
        hid[...] = second.astype(BF)
        total[...] = second + down_bias[...]
        for i in range(steps):
            cols = pl.ds(i * FF_STEP, FF_STEP)
            ups[i].wait()
            u = nn(hid[...], up[:, cols]) + up_bias[:, cols]
            act, slo = gelu_parts(u)
            active[:, cols] = act.astype(BF)
            slope[:, cols] = slo
            downs[i].wait()
            total[...] += nn(active[:, cols], down[cols, :])
        hat3, scale3 = normalize(total[...])
        out[...] = (hat3 * gain3[...] + shift3[...]).astype(BF)
        grad = jnp.concatenate([ga[...], gb[...]], axis=0).astype(F32)
        vec[0:1, :] = column(grad * hat3)
        vec[1:2, :] = column(grad)
        dthird = norm_back(grad, hat3, scale3, gain3[...])
        total[...] = dthird
        third[...] = dthird.astype(BF)
        vec[2:3, :] = column(third[...])

        def block(i, carry):
            for s in (0, 1):
                at = pl.multiple_of((group ^ i) * D + s * FF_BLOCK, FF_BLOCK)
                cols = pl.ds(at, FF_BLOCK)
                du = (nt(third[...], down[cols, :]) * slope[:, cols]).astype(BF)
                upb[:, cols] = column(du)
                total[...] += nt(du, up[:, cols])
                grads = (tn(du, hid[...]).astype(BF), tn(active[:, cols], third[...]).astype(BF))

                def put(value):
                    for which in (0, 1):
                        for m in range(FF_BLOCK // piece):
                            target = own if m % 2 == value else snd
                            to = s * (FF_BLOCK // 2) + (m // 2) * piece
                            target[i, which, to : to + piece, :] = grads[which][
                                m * piece : (m + 1) * piece
                            ]

                by_core(core, put)
            return carry

        lax.fori_loop(0, 4, block, 0)
        grad = total[...]
        hat = hat2[...]
        scale = pick_lane(stats, slice(None), 12)
        vec[3:4, :] = column(grad * hat)
        vec[4:5, :] = column(grad)
        dsec = norm_back(grad, hat, scale, gain2[...])
        dsecond[...] = dsec
        vec[5:6, :] = column(dsec.astype(BF))
        vec[6:8, :] = jnp.zeros((2, D), F32)

    return kernel


def cross_pairs(first, grad, att, q, k, v, stats, dq, dk, dv):
    def pair(p, carry):
        lanes = pair_lanes(first + p)
        out = pair_lanes(p)
        grad_k = grad_v = 0.0
        for slot in (0, 1):
            rows = pl.ds(slot * CHUNK, CHUNK)
            gq, gk, gv = backward_heads(
                q[rows, lanes], grad[rows, lanes], att[rows, lanes], k[:, lanes], v[:, lanes],
                None, stats[rows, :], first + p,
            )
            dq[rows, out] = (gq * 0.125).astype(BF)
            grad_k = grad_k + gk
            grad_v = grad_v + gv
        dk[:, out] = grad_k.astype(BF)
        dv[:, out] = grad_v.astype(BF)
        return carry

    lax.fori_loop(0, 3, pair, 0)


def weight_grads(core, dq, dk, dv, queries, keys, own, snd):
    store_pieces(core, tn(dq[...], queries).astype(BF), 0, 0, own, snd)
    for which, full in ((1, dk), (2, dv)):
        block = 0.0
        for rows, x in keys:
            block = block + tn(full[rows, :], x)
        store_pieces(core, block.astype(BF), 0, which * PIECE, own, snd)
    store_bias_rows([column(dq[...]), column(dv[...])], own, snd, 3 * PIECE)


def out_grads(core, att, low, wo, grad, own, snd):
    for g in (0, 2):
        block = tn(att[:, g * GROUP : (g + 2) * GROUP], low[...]).astype(BF)
        store_pieces(core, block, g, 0, own, snd)
    grad[...] = nt(low[...], wo[...]).astype(BF)


def cross_backward_a(
    place, dsecond, att, q, k, v, stats, hat1, gain1, shift1, ea, eb,
    w0, w1, w2, w3, n1, n2, n3, f1, f2, f3,
    grad, dfirst, enc_own, enc_other, own, snd, own_o, snd_o,
    wq, wk, wv, wo, dq, dk, dv, low, sems,
):
    core = place[0]
    near, far, ws = (n1, n2, n3), (f1, f2, f3), (w0, w1, w2, w3)
    sets = [weight_copies(3, 3, core, ws, near, far, wo, sems)] + [
        weight_copies(w, w, core, ws, near, far, dst, sems, (2, 3))
        for w, dst in enumerate((wq, wk, wv))
    ]
    for one in sets:
        start(one)
    low[...] = dsecond[...].astype(BF)
    finish(sets[0])
    out_grads(core, att, low, wo, grad, own_o, snd_o)
    cross_pairs(3, grad, att, q, k, v, stats, dq, dk, dv)
    low[...] = (hat1[...] * gain1[...] + shift1[...]).astype(BF)
    halves = (pl.ds(0, HALF_ENC), pl.ds(HALF_ENC, HALF_ENC))
    weight_grads(
        core, dq, dk, dv, low[...], ((halves[0], ea[...]), (halves[1], eb[...])), own, snd
    )
    for one in sets[1:]:
        finish(one)
    for half, target in zip(halves, (enc_own, enc_other)):
        target[...] = nn(dk[half, :], wk[...]) + nn(dv[half, :], wv[...])
    dfirst[...] = dsecond[...] + nn(dq[...], wq[...])


def cross_backward_b(
    place, dfirst_a, enc_own_a, enc_other_a, grad, att, q, k, v, stats, hat1, scale1, gain1,
    shift1, ea, eb, w0, w1, w2, n1, n2, n3, f1, f2, f3,
    dfirst, enc_own, enc_other, own, snd, vec,
    wq, wk, wv, dq, dk, dv, low, sems,
):
    core = place[0]
    near, far, ws = (n1, n2, n3), (f1, f2, f3), (w0, w1, w2)
    sets = [
        weight_copies(w, w, core, ws, near, far, dst, sems, (0, 1))
        for w, dst in enumerate((wq, wk, wv))
    ]
    for one in sets:
        start(one)
    cross_pairs(0, grad, att, q, k, v, stats, dq, dk, dv)
    hat = hat1[...]
    low[...] = (hat * gain1[...] + shift1[...]).astype(BF)
    halves = (pl.ds(0, HALF_ENC), pl.ds(HALF_ENC, HALF_ENC))
    weight_grads(
        core, dq, dk, dv, low[...], ((halves[0], ea[...]), (halves[1], eb[...])), own, snd
    )
    for one in sets:
        finish(one)
    enc_own[...] = enc_own_a[...] + nn(dk[halves[0], :], wk[...]) + nn(dv[halves[0], :], wv[...])
    enc_other[...] = (
        enc_other_a[...] + nn(dk[halves[1], :], wk[...]) + nn(dv[halves[1], :], wv[...])
    ).astype(BF)
    total = dfirst_a[...] + nn(dq[...], wq[...])
    vec[0:1, :] = column(total * hat)
    vec[1:2, :] = column(total)
    dfi = norm_back(total, hat, scale1[:, 0:1], gain1[...])
    dfirst[...] = dfi
    vec[2:3, :] = column(dfi.astype(BF))
    vec[3:8, :] = jnp.zeros((5, D), F32)


def self_pairs(core, first, ends, grad, att, q, k, v, stats, dq, dk, dv, bias, sum_k, sum_v):
    for slot in (0, 1):
        bias[slot] = mask_bias(ends, chunk_of(core, slot), ROW)

    def attend(value):
        def pair(p, carry):
            lanes = pair_lanes(first + p)
            out = pair_lanes(p)
            sum_k[...] = jnp.zeros_like(sum_k)
            sum_v[...] = jnp.zeros_like(sum_v)
            for slot, count in key_counts(value):
                rows = pl.ds(slot * CHUNK, CHUNK)
                width = count * CHUNK
                gq, gk, gv = backward_heads(
                    q[rows, lanes], grad[rows, lanes], att[rows, lanes],
                    k[0:width, lanes], v[0:width, lanes],
                    bias[slot, :, 0:width], stats[rows, :], first + p,
                )
                dq[rows, out] = (gq * 0.125).astype(BF)
                sum_k[0:width, :] += gk
                sum_v[0:width, :] += gv
            dk[:, out] = sum_k[...].astype(BF)
            dv[:, out] = sum_v[...].astype(BF)
            return carry

        lax.fori_loop(0, 3, pair, 0)

    by_core(core, attend)


def self_part(core, first, ends, grad, att, q, k, v, stats, xs, sets, own, snd, scratch):
    wq, wk, wv, dq, dk, dv, bias, sum_k, sum_v = scratch
    self_pairs(core, first, ends, grad, att, q, k, v, stats, dq, dk, dv, bias, sum_k, sum_v)
    keys = [(chunk_rows(core, c4), x) for c4, x in enumerate(xs)]
    queries = jnp.concatenate([xs[0], xs[1]], axis=0)
    weight_grads(core, dq, dk, dv, queries, keys, own, snd)
    for one in sets:
        finish(one)
    parts = []
    for c4 in range(4):
        rows = chunk_rows(core, c4)
        part = nn(dk[rows, :], wk[...]) + nn(dv[rows, :], wv[...])
        if c4 < 2:
            part = part + nn(dq[c4 * CHUNK : (c4 + 1) * CHUNK, :], wq[...])
        parts.append(part)
    return parts


def self_backward_a(
    place, dfirst, att, q, k, v, stats, xa, xb, ya, yb, w0, w1, w2, w3, n1, n2, n3, f1, f2, f3,
    in_own, in_other, grad, own, snd, own_o, snd_o,
    wq, wk, wv, wo, dq, dk, dv, low, bias, sum_k, sum_v, sems,
):
    core = place[0]
    near, far, ws = (n1, n2, n3), (f1, f2, f3), (w0, w1, w2, w3)
    sets = [weight_copies(3, 3, core, ws, near, far, wo, sems)] + [
        weight_copies(w, w, core, ws, near, far, dst, sems, (2, 3))
        for w, dst in enumerate((wq, wk, wv))
    ]
    for one in sets:
        start(one)
    low[...] = dfirst[...].astype(BF)
    finish(sets[0])
    out_grads(core, att, low, wo, grad, own_o, snd_o)
    xs = (xa[0:CHUNK, :], xb[...], ya[0:CHUNK, :], yb[...])
    parts = self_part(
        core, 3, document_ends(xa, place), grad, att, q, k, v, stats, xs, sets[1:], own, snd,
        (wq, wk, wv, dq, dk, dv, bias, sum_k, sum_v),
    )
    for n in (0, 1):
        in_own[n] = parts[n] + dfirst[n * CHUNK : (n + 1) * CHUNK, :]
        in_other[n] = parts[2 + n]


def self_backward_b(
    place, grad, in_own_a, in_other_a, att, q, k, v, stats, xa, xb, ya, yb,
    w0, w1, w2, n1, n2, n3, f1, f2, f3,
    in_own, in_other, own, snd,
    wq, wk, wv, dq, dk, dv, bias, sum_k, sum_v, sems,
):
    core = place[0]
    near, far, ws = (n1, n2, n3), (f1, f2, f3), (w0, w1, w2)
    sets = [
        weight_copies(w, w, core, ws, near, far, dst, sems, (0, 1))
        for w, dst in enumerate((wq, wk, wv))
    ]
    for one in sets:
        start(one)
    xs = (xa[0:CHUNK, :], xb[...], ya[0:CHUNK, :], yb[...])
    parts = self_part(
        core, 0, document_ends(xa, place), grad, att, q, k, v, stats, xs, sets, own, snd,
        (wq, wk, wv, dq, dk, dv, bias, sum_k, sum_v),
    )
    for n in (0, 1):
        in_own[n] = parts[n] + in_own_a[n]
        in_other[n] = (parts[2 + n] + in_other_a[n]).astype(BF)


def mark(place):
    pass


def in_vmem(n):
    return [pl.BlockSpec(memory_space=pltpu.VMEM)] * n


def in_any(n):
    return [pl.BlockSpec(memory_space=pl.ANY)] * n


def call(kernel, specs, outs, scratch, args, name, pins=()):
    first = 1 + len(specs)
    last = first + len(pins)
    end = last + len(outs)

    def body(*refs):
        kernel(*refs[:first], *refs[last:end], *refs[end + 1 :])
        refs[end][...] = jnp.zeros((8, 128), F32)

    return pl.pallas_call(
        body,
        in_specs=[pl.BlockSpec(memory_space=pltpu.SMEM)] + specs + in_any(len(pins)),
        out_specs=in_vmem(len(outs) + 1),
        out_shape=[jax.ShapeDtypeStruct(shape, dtype) for shape, dtype in outs + [((8, 128), F32)]],
        scratch_shapes=scratch,
        compiler_params=pltpu.CompilerParams(vmem_limit_bytes=56 * MIB),
        cost_estimate=pl.CostEstimate(flops=1000, bytes_accessed=1000, transcendentals=0),
        name=name,
    )(*args, *pins)


def after(value, zero):
    return value + zero[0, 0].astype(value.dtype)


def solution(mesh):
    names = tuple(mesh.axis_names)
    heads, rows = mesh.shape["heads"], mesh.shape["rows"]
    depth = rows // 2
    piece = FF // (heads * rows)

    def send(value, where, label="moved"):
        pairs = []
        for r in range(rows):
            for h in range(heads):
                to_r, to_h = where(r, h)
                index = {"rows": (r, to_r), "heads": (h, to_h)}
                a = b = 0
                for name in names:
                    a = a * mesh.shape[name] + index[name][0]
                    b = b * mesh.shape[name] + index[name][1]
                pairs.append((a, b))
        with jax.named_scope(label):
            return lax.ppermute(value, names, pairs)

    def swap(r, h):
        return (r & ~1) | (h & 1), (h & ~1) | (r & 1)

    def swap_b(r, h):
        return (r & ~1) | (1 - (h & 1)), (h & ~1) | (r & 1)

    def swap_b_back(r, h):
        return (r & ~1) | (h & 1), (h & ~1) | (1 - (r & 1))

    def core_to(r, h):
        return r ^ 1, h

    def head_to(d):
        return lambda r, h: (r, h ^ d)

    def depth_to(d):
        return lambda r, h: (r ^ (2 * d), h)

    def unrelate(parts, k):
        parts = list(parts)
        bit = 1
        while bit < len(parts):
            odd = (k & bit) != 0
            parts = [jnp.where(odd, parts[n ^ bit], parts[n]) for n in range(len(parts))]
            bit *= 2
        return parts

    def shards(
        layer_input, encoder_out, doc_lengths,
        self_query, self_qbias, self_key_weight, self_value, self_vbias, self_out, self_obias,
        first_gain, first_shift,
        cross_query, cross_qbias, cross_key, cross_value, cross_vbias, cross_out, cross_obias,
        second_gain, second_shift, up_weight, up_bias, down_weight, down_bias,
        third_gain, third_shift, out_grad,
    ):
        h = lax.axis_index("heads")
        r = lax.axis_index("rows")
        core, k = r % 2, r // 2
        place = jnp.stack([core, h]).astype(jnp.int32)

        def line(vector):
            return vector.reshape(1, -1)

        def split_rows(biases):
            rows = []
            for one in biases:
                for _ in range(3):
                    top = one.astype(BF)
                    rows.append(top)
                    one = one - top.astype(F32)
            rows = jnp.stack(rows)
            return jnp.pad(rows, ((0, 16 - rows.shape[0]), (0, D - GROUP)))

        def half_of(parts, biases):
            rows = [lax.dynamic_slice_in_dim(one, core * PIECE, PIECE, axis=0) for one in parts]
            return jnp.concatenate(rows + [split_rows(biases)], axis=0)

        lengths = jnp.concatenate([doc_lengths // 16, doc_lengths % 16], axis=0).astype(BF)
        lengths = jnp.pad(lengths, ((0, 12), (0, D - 8)))
        xa = send(jnp.concatenate([layer_input[:CHUNK], lengths], axis=0), swap, "x_a")
        xb = send(layer_input[CHUNK:], swap_b, "x_b")
        self_own = [self_query.T, self_key_weight.T, self_value.T, self_out]
        mine = half_of(self_own, [self_qbias, self_vbias])
        self_near = [send(mine, head_to(d), "w_self_near") for d in (1, 2, 3)]
        ya = send(xa, core_to, "y_a")
        yb = send(xb, core_to, "y_b")
        self_far = [send(one, core_to, "w_self_far") for one in self_near]
        self_w = self_near + self_far
        (zero,) = call(mark, [], [], [], [place], "arrived", pins=self_near)
        cross_own = [cross_query.T, cross_key.T, cross_value.T, cross_out]
        mine = after(half_of(cross_own, [cross_qbias, cross_vbias]), zero)
        enc = after(encoder_out, zero)
        cross_near = [send(mine, head_to(d), "w_cross_near") for d in (1, 2, 3)]
        ea = send(enc, swap, "e_a")

        weight = pltpu.VMEM((D, D), BF)
        half_weight = pltpu.VMEM((D // 2, D), BF)
        half_tokens = pltpu.VMEM((OWN, D // 2), BF)
        bias_lines = [pltpu.VMEM((3, 16, D), BF)]
        masks = pltpu.VMEM((2, CHUNK, ROW), F32)
        token_bf = ((OWN, D), BF)
        token_f32 = ((OWN, D), F32)
        lines = ((OWN, 128), F32)
        dma = pltpu.SemaphoreType.DMA
        q, kk, v, att, stats1, zero = call(
            self_forward,
            in_vmem(4) + in_any(9) + in_vmem(2),
            [token_bf, ((ROW, D), BF), ((ROW, D), BF), token_bf, lines],
            [weight] * 3 + [masks] + bias_lines + [dma((3, 7)), dma((3,))],
            [place, xa, xb, ya, yb] + self_own[:3] + self_w + [line(self_qbias), line(self_vbias)],
            "self_forward", pins=[mine, enc],
        )
        cross_far = [send(after(one, zero), core_to, "w_cross_far") for one in cross_near]
        eb = send(after(ea, zero), core_to, "e_b")
        hat1, scale1, zero = call(
            self_finish,
            in_vmem(3) + in_any(7) + in_vmem(1),
            [token_f32, lines],
            [weight, dma((1, 7))],
            [place, xa, xb, att, self_own[3]] + self_w + [line(self_obias)],
            "self_finish", pins=cross_near + [ea],
        )
        ga = send(after(out_grad[:CHUNK], zero), swap, "g_a")
        gb = send(after(out_grad[CHUNK:], zero), swap_b, "g_b")
        cross_w = cross_near + cross_far
        cq, ck, cv, catt, stats2, hat2, zero = call(
            cross_forward,
            in_vmem(5) + in_any(10) + in_vmem(3),
            [token_bf, ((ENC, D), BF), ((ENC, D), BF), token_bf, lines, token_f32],
            [weight] * 4 + bias_lines + [dma((4, 7)), dma((3,))],
            [place, hat1, line(first_gain), line(first_shift), ea, eb] + cross_own + cross_w
            + [line(cross_qbias), line(cross_vbias), line(cross_obias)],
            "cross_forward",
        )
        ff_shape = ((4, 2, FF // 8, D), BF)
        out, dsecond, ff_own, ff_snd, vec_a, upb, zero = call(
            feed_forward(piece),
            in_vmem(4) + in_any(1) + in_vmem(1) + in_any(1) + in_vmem(5),
            [token_bf, token_f32, ff_shape, ff_shape, ((8, D), F32), ((1, FF), F32)],
            [
                pltpu.VMEM((D, FF), BF), pltpu.VMEM((FF, D), BF), pltpu.VMEM((OWN, FF), BF),
                pltpu.VMEM((OWN, FF), F32), pltpu.VMEM((OWN, D), BF), pltpu.VMEM((OWN, D), F32),
                pltpu.VMEM((OWN, D), BF), dma((2, FF // FF_STEP)),
            ],
            [
                place, hat2, stats2, line(second_gain), line(second_shift), up_weight,
                line(up_bias), down_weight, line(down_bias), line(third_gain), line(third_shift),
                ga, gb,
            ],
            "feed_forward",
        )

        ff_got = send(ff_snd, core_to, "ff_core")
        out_a = send(out[:CHUNK], swap, "out_a")
        out_b = send(out[CHUNK:], swap_b_back, "out_b")

        piece_rows = ((2, 3 * PIECE + 32, D), BF)
        out_rows = ((4, PIECE, D), BF)
        enc_f32 = ((HALF_ENC, D), F32)
        key_grads = [pltpu.VMEM((ENC, D // 2), BF)] * 2
        grad, dfirst_a, enc_own, enc_snd, ca_own, ca_snd, co_own, co_snd, zero = call(
            cross_backward_a,
            in_vmem(11) + in_any(10),
            [token_bf, token_f32, enc_f32, enc_f32, piece_rows, piece_rows, out_rows, out_rows],
            [half_weight] * 3 + [weight, half_tokens] + key_grads
            + [pltpu.VMEM((OWN, D), BF), dma((4, 7))],
            [place, dsecond, catt, cq, ck, cv, stats2, hat1, line(first_gain), line(first_shift),
             ea, eb] + cross_own + cross_w,
            "cross_backward_a",
        )

        def both(own, got, d, w):
            return own[d, w].astype(F32) + got[d, w].astype(F32)

        ff_x = after(jnp.stack([both(ff_own, ff_got, d, 0) for d in (1, 3)]).astype(BF), zero)
        ff_y = after(jnp.stack([both(ff_own, ff_got, d, 1) for d in (2, 3)]).astype(BF), zero)
        ff_gx = send(ff_x, head_to(1), "ff_heads")
        ff_gy = send(ff_y, head_to(2), "ff_heads")
        ca_got = send(after(ca_snd, zero), core_to, "ca_core")
        co_got = send(after(co_snd, zero), core_to, "co_core")
        dfirst, enc_own, enc_snd, cb_own, cb_snd, vec_b, zero = call(
            cross_backward_b,
            in_vmem(15) + in_any(9),
            [token_f32, enc_f32, ((HALF_ENC, D), BF), piece_rows, piece_rows, ((8, D), F32)],
            [half_weight] * 3 + [half_tokens] + key_grads
            + [pltpu.VMEM((OWN, D), BF), dma((3, 7))],
            [place, dfirst_a, enc_own, enc_snd, grad, catt, cq, ck, cv, stats2, hat1, scale1,
             line(first_gain), line(first_shift), ea, eb] + cross_own[:3] + cross_w,
            "cross_backward_b", pins=[ff_x, ff_y, out_a, out_b],
        )
        output = jnp.concatenate([out_a, out_b], axis=0)
        vectors = jnp.concatenate([vec_a[:6], vec_b[:3], upb.reshape(4, D)], axis=0)
        vectors = lax.all_gather(vectors, names)
        ff_x2 = after((both(ff_own, ff_got, 2, 0) + ff_gx[1].astype(F32)).astype(BF), zero)
        ff_y2 = after((both(ff_own, ff_got, 1, 1) + ff_gy[1].astype(F32)).astype(BF), zero)
        ff_gx2 = send(ff_x2, head_to(2), "ff_heads_2")
        ff_gy2 = send(ff_y2, head_to(1), "ff_heads_2")
        cb_got = send(after(cb_snd, zero), core_to, "cb_core")
        enc_got = send(after(enc_snd, zero), core_to, "enc_core")

        slots_f32 = ((2, CHUNK, D), F32)
        row_grads = [pltpu.VMEM((ROW, D // 2), BF)] * 2
        sums = [pltpu.VMEM((ROW, PAIR), F32)] * 2
        in_own, in_snd, sgrad, sa_own, sa_snd, so_own, so_snd, zero = call(
            self_backward_a,
            in_vmem(10) + in_any(10),
            [slots_f32, slots_f32, token_bf, piece_rows, piece_rows, out_rows, out_rows],
            [half_weight] * 3 + [weight, half_tokens] + row_grads
            + [pltpu.VMEM((OWN, D), BF), masks] + sums + [dma((4, 7))],
            [place, dfirst, att, q, kk, v, stats1, xa, xb, ya, yb] + self_own + self_w,
            "self_backward_a", pins=[ff_x2, ff_y2, ca_got, co_got],
        )
        sa_got = send(after(sa_snd, zero), core_to, "sa_core")
        so_got = send(after(so_snd, zero), core_to, "so_core")

        def depth_parts(blocks):
            return lax.dynamic_index_in_dim(blocks, k, 0, keepdims=False), [
                lax.dynamic_index_in_dim(blocks, k ^ d, 0, keepdims=False).astype(BF)
                for d in range(1, depth)
            ]

        def depth_send(parts, label):
            return [send(one, depth_to(d + 1), label) for d, one in enumerate(parts)]

        def summed(first, rest):
            for one in rest:
                first = first + one.astype(F32)
            return first

        ff_up = both(ff_own, ff_got, 0, 0) + ff_gx[0].astype(F32) + ff_gx2.astype(F32)
        ff_down = both(ff_own, ff_got, 0, 1) + ff_gy[0].astype(F32) + ff_gy2.astype(F32)
        ff_sum = after(jnp.stack([ff_up, ff_down]), zero)
        ff_mine, ff_parts = depth_parts(ff_sum.reshape(2, depth, piece, D).swapaxes(0, 1))
        ff_back = depth_send(ff_parts, "ff_depth")
        enc_sum = after((enc_own + enc_got.astype(F32)).astype(BF), zero)
        encoder_g = send(enc_sum, swap, "enc_grad")

        class Heads:
            def __init__(self, a_own, a_got, b_own, b_got, o_own, o_got, zero, label):
                pairs = ((b_own, b_got), (a_own, a_got))
                cut = 2 * PIECE

                def first(d):
                    own, got = pairs[d // 2]
                    return own[d % 2, :cut].astype(F32) + got[d % 2, :cut].astype(F32)

                def last(d):
                    own, got = pairs[d // 2]
                    rest = own[d % 2, cut:].astype(F32) + got[d % 2, cut:].astype(F32)
                    return jnp.concatenate(
                        [rest, o_own[d].astype(F32) + o_got[d].astype(F32)], axis=0
                    )

                self.first, self.last, self.label = first, last, label
                self.x = after(jnp.stack([first(1), first(3)]).astype(BF), zero)
                self.y = after(jnp.stack([last(2), last(3)]).astype(BF), zero)
                self.gx = send(self.x, head_to(1), label)
                self.gy = send(self.y, head_to(2), label)

            def second(self):
                x = (self.first(2) + self.gx[1].astype(F32)).astype(BF)
                y = (self.last(1) + self.gy[1].astype(F32)).astype(BF)
                gx = send(x, head_to(2), self.label + "_2")
                gy = send(y, head_to(1), self.label + "_2")
                return jnp.concatenate(
                    [
                        self.first(0) + self.gx[0].astype(F32) + gx.astype(F32),
                        self.last(0) + self.gy[0].astype(F32) + gy.astype(F32),
                    ],
                    axis=0,
                )

        cross_heads = Heads(ca_own, ca_got, cb_own, cb_got, co_own, co_got, zero, "c_heads")
        in_own, in_snd, sb_own, sb_snd, zero = call(
            self_backward_b,
            in_vmem(12) + in_any(9),
            [slots_f32, ((2, CHUNK, D), BF), piece_rows, piece_rows],
            [half_weight] * 3 + [half_tokens] + row_grads + [masks] + sums + [dma((3, 7))],
            [place, sgrad, in_own, in_snd, att, q, kk, v, stats1, xa, xb, ya, yb]
            + self_own[:3] + self_w,
            "self_backward_b", pins=ff_parts + [cross_heads.x, cross_heads.y, enc_sum],
        )
        sb_got = send(sb_snd, core_to, "sb_core")
        in_got = send(in_snd, core_to, "in_core")
        self_heads = Heads(sa_own, sa_got, sb_own, sb_got, so_own, so_got, zero, "s_heads")
        totals = [after(cross_heads.second(), zero), self_heads.second()]
        ff = after(summed(ff_mine, ff_back), zero)
        upweight_g = ff[0].T
        downweight_g = ff[1]
        in_sum = (in_own + in_got.astype(F32)).astype(BF)
        input_g = jnp.concatenate(
            [send(in_sum[0], swap, "in_a"), send(in_sum[1], swap_b_back, "in_b")], axis=0
        )

        grads, bias_rows = [], []
        for total, label in zip(totals, ("c", "s")):
            size = total.shape[0]
            mine, parts = depth_parts(total.reshape(depth, size // depth, D))
            part = summed(mine, depth_send(parts, label + "_depth")).astype(BF)
            parts = unrelate(
                [part] + [send(part, depth_to(d), label + "_back") for d in range(1, depth)], k
            )
            mine = jnp.concatenate(parts, axis=0)
            other = send(mine, core_to, label + "_far")
            for at in (0, PIECE, 2 * PIECE, 3 * PIECE + 32):
                a, b = mine[at : at + PIECE], other[at : at + PIECE]
                grads.append(
                    jnp.concatenate(
                        [jnp.where(core == 0, a, b), jnp.where(core == 0, b, a)], axis=0
                    ).astype(F32)
                )
            bias_rows += [mine[3 * PIECE + n, :GROUP].astype(F32) for n in (0, 1)]
        cq_g, ck_g, cv_g, co_g, sq_g, sk_g, sv_g, so_g = grads
        cqb, cvb, sqb, svb = bias_rows
        vectors = jnp.sum(vectors, axis=0)
        ff_at = (h * rows + r) * piece
        upbias_g = lax.dynamic_slice_in_dim(vectors[9:].reshape(FF), ff_at, piece)
        return (
            output, input_g, encoder_g,
            sq_g.T, sqb, sk_g.T, sv_g.T, svb, so_g, vectors[8], vectors[6], vectors[7],
            cq_g.T, cqb, ck_g.T, cv_g.T, cvb, co_g, vectors[5],
            vectors[3], vectors[4], upweight_g, upbias_g, downweight_g, vectors[2],
            vectors[0], vectors[1],
        )

    rowed, headed = P(("rows", "heads"), None), P(None, "heads")
    by_head, by_head_rows, whole = P("heads"), P("heads", None), P()
    ffed = ("heads", "rows")
    return jax.shard_map(
        shards,
        mesh=mesh,
        in_specs=(
            rowed, rowed, P("rows", None),
            headed, by_head, headed, headed, by_head, by_head_rows, whole, whole, whole,
            headed, by_head, headed, headed, by_head, by_head_rows, whole, whole, whole,
            whole, whole, whole, whole, whole, whole, rowed,
        ),
        out_specs=(
            rowed, rowed, rowed,
            headed, by_head, headed, headed, by_head, by_head_rows, whole, whole, whole,
            headed, by_head, headed, headed, by_head, by_head_rows, whole, whole, whole,
            P(None, ffed), P(ffed), P(ffed, None), whole, whole, whole,
        ),
        check_vma=False,
    )
```

time: 1090 us -> 531 us (0.49)
  waiting for transfers between devices: 508 us -> 121 us
  matrix products: 281 us -> 0 us
  Pallas kernels: 0 us -> 204 us
  local copies, waits for them, and re-layouts: 107 us -> 36.1 us
  blocking collectives: 59.4 us -> 0 us
  starting transfers between devices: 33.3 us -> 75.1 us
    dot_general x58 -> x0, matrix products: 281 us -> none  [the longest x8 50 us: scores_of(): jnp.einsum('qhe,khe->hqk', query, keys, preferred_element_type=jnp.float32)]
    reduce_scatter x2 -> x0, waiting for transfers between devices: 212 us -> none  [the longest x1 142 us: shards(): lax.psum_scatter(row_product(active_low, dbranch), ('heads', 'rows'), sca...]
    pallas_call x0 -> x9, Pallas kernels: none -> 204 us  [call(): pl.pallas_call(body, in_specs=[pl.BlockSpec(memory_space=pltpu.SMEM)] + s...]
    ppermute x0 -> x63, waiting for transfers between devices: none -> 121 us  [send(): return lax.ppermute(value, names, pairs)]
    all_gather x13 -> x1, waiting for transfers between devices: 121 us -> 0.02 us  [shards(): vectors = lax.all_gather(vectors, names)]
    psum x1 -> x0, waiting for transfers between devices: 115 us -> none  [shards(): lax.psum((selfquery_g, selfqbias_g, selfkey_g, selfvalue_g, selfvbias_g,...]
    ppermute x0 -> x63, starting transfers between devices: none -> 75.1 us  [send(): return lax.ppermute(value, names, pairs)]
    psum x2 -> x0, blocking collectives: 59.4 us -> none  [the longest x1 48.1 us: shards(): lax.psum((downbias_g, selfobias_g, crossobias_g, firstgain_g, firstshift_...]
  transfers between devices with their start and end apart: 24 -> 64, of which waited for: 12 -> 21; matrix products, arithmetic and copies ran while one was open for 36% -> 17% of each run, Pallas kernels for 0% -> 31%
where the time goes in v1:
time: 531 us; the launch traced here: 525 us
  Pallas kernels  204 us (38%)
  waiting for transfers between devices  121 us (23%)
  starting transfers between devices  75.1 us (14%)
  other arithmetic  71.5 us (13%)
  local copies, waits for them, and re-layouts  36.1 us (7%)
  between operations  17 us (3%)
    pallas_call x9, Pallas kernels, call(): pl.pallas_call(body, in_specs=[pl.BlockSpec(memory_space=pltpu.SMEM)] + s...  204 us
    ppermute x63, waiting for transfers between devices, send(): return lax.ppermute(value, names, pairs)  121 us
    ppermute x63, starting transfers between devices, send(): return lax.ppermute(value, names, pairs)  75.1 us
    add x24, other arithmetic, after(): return value + zero[0, 0].astype(value.dtype)  28.9 us
    unnamed x165, local copies, waits for them, and re-layouts  17.8 us
  transfers between devices with their start and end apart: 64, of which 21 were waited for; matrix products, arithmetic and copies ran while one was open for 17% of the time, Pallas kernels for 31%

profile of v1, /device:TPU:9, one launch (start us, length us, event | category | flops | bytes accessed | tf_op | source)
XLA Modules:
  0.0 524.7 jit_solution(11199171799650255890)
XLA Ops:
  18.5 2.0 fusion.56
  21.4 4.5 collective-permute-start
  29.7 23.8 %collective-permute-done.1.refs_2_.refs_8_.refs_10_ = bf16[272,768]{1,0:T(8,128)(2,1)S(1)} collective-permute-done((bf16[272,768]{1,0:T(8,128)(2,1)}, bf16[272,768]{1,0:T(8,128)(2,1)S(1)}, u32[]{:S(2)}, u32[]{:S(2)}) %collective-permute-start.1) | collective-permute-done | bytes 417824 | tf_op jit(solution)/shard_map/x_b/ppermute | solution.py:714
  65.7 3.3 collective-permute-start.13
  70.6 21.0 %self_forward.1 = (bf16[544,768]{1,0:T(8,128)(2,1)}, bf16[1088,768]{1,0:T(8,128)(2,1)}, bf16[1088,768]{1,0:T(8,128)(2,1)}, bf16[544,768]{1,0:T(8,128)(2,1)}, f32[544,128]{1,0:T(8,128)}, /*index=5*/f32[8,128]{1,0:T(8,128)}) custom-call(s32[2]{0:T(128)} %pad_add_fusion.refs_0_, bf16[288,768]{1,0:T(8,128)(2,1)} %copy-done.11, bf16[272,768]{1,0:T(8,128)(2,1)} %copy-done.12, ...), custom_call_target="tpu_custom_call" | custom-call | flops 1000 | bytes 1000 | tf_op jit(solution)/shard_map/self_forward/pallas_call | solution.py:680
  94.3 2.5 collective-permute-start.17
  99.5 2.0 collective-permute-start.15
  101.6 5.2 self_finish.1
  108.8 14.0 %collective-permute-start.18 = (bf16[272,768]{1,0:T(8,128)(2,1)S(1)}, bf16[272,768]{1,0:T(8,128)(2,1)S(1)}, u32[]{:S(2)}, u32[]{:S(2)}) collective-permute-start(bf16[272,768]{1,0:T(8,128)(2,1)S(1)} %get-tuple-element.182), channel_id=1, source_target_pairs={{0,0},{8,1},{16,16},{24,17},{1,8},{9,9},{17,24},{25,25},{2,2},{10,... | collective-permute-start | bytes 1253384 | tf_op jit(solution)/shard_map/g_a/ppermute | solution.py:714
  129.0 23.7 %cross_forward.1 = (bf16[544,768]{1,0:T(8,128)(2,1)}, bf16[1024,768]{1,0:T(8,128)(2,1)}, bf16[1024,768]{1,0:T(8,128)(2,1)}, bf16[544,768]{1,0:T(8,128)(2,1)}, f3...) custom-call(s32[2]{0:T(128)} %pad_add_fusion.refs_0_, ...), custom_call_target="tpu_custom_call" | custom-call | flops 1000 | bytes 1000 | tf_op jit(solution)/shard_map/cross_forward/pallas_call | solution.py:680
  153.6 40.6 %feed_forward.1 = (bf16[544,768]{1,0:T(8,128)(2,1)}, f32[544,768]{1,0:T(8,128)}, bf16[4,2,384,768]{3,2,1,0:T(8,128)(2,1)}, bf16[4,2,384,768]{3,2,1,0:T(8,128)(2,...) custom-call(s32[2]{0:T(128)} %pad_add_fusion.refs_0_, f32[544,768]{1,0:T(8,128)} %get-tuple-element.80.refs_1_, ...), custom_call_target="tpu_custom_call" | custom-call | flops 1000 | bytes 1000 | tf_op jit(solution)/shard_map/feed_forward/pallas_call | solution.py:680
  194.7 28.8 %cross_backward_a.1 = (bf16[544,768]{1,0:T(8,128)(2,1)}, f32[544,768]{1,0:T(8,128)}, f32[512,768]{1,0:T(8,128)}, f32[512,768]{1,0:T(8,128)}, bf16[2,320,768]{2,1...) custom-call(s32[2]{0:T(128)} %pad_add_fusion.refs_0_, ...), custom_call_target="tpu_custom_call" | custom-call | flops 1000 | bytes 1000 | tf_op jit(solution)/shard_map/cross_backward_a/pallas_call | solution.py:680
  224.8 1.8 broadcast_add_fusion.11
  227.7 3.5 collective-permute-start.20
  234.8 6.3 %collective-permute-done.20.refs_27_ = bf16[272,768]{1,0:T(8,128)(2,1)S(1)} collective-permute-done((bf16[272,768]{1,0:T(8,128)(2,1)}, bf16[272,768]{1,0:T(8,128)(2,1)S(1)}, u32[]{:S(2)}, u32[]{:S(2)}) %collective-permute-start.20) | collective-permute-done | bytes 417824 | tf_op jit(solution)/shard_map/out_a/ppermute | solution.py:714
  243.8 2.9 fusion.11
  250.3 25.9 %cross_backward_b.1 = (f32[544,768]{1,0:T(8,128)}, f32[512,768]{1,0:T(8,128)}, bf16[512,768]{1,0:T(8,128)(2,1)}, bf16[2,320,768]{2,1,0:T(8,128)(2,1)}, bf16[2,32...) custom-call(s32[2]{0:T(128)} %pad_add_fusion.refs_0_, f32[544,768]{1,0:T(8,128)} %get-tuple-element.89.refs_1_, ...), custom_call_target="tpu_custom_call" | custom-call | flops 1000 | bytes 1000 | tf_op jit(solution)/shard_map/cross_backward_b/pallas_call | solution.py:680
  277.4 3.0 broadcast_add_fusion.1
  288.8 2.0 add_bitcast_fusion
  290.8 17.3 %collective-permute-done.24 = bf16[2,384,768]{2,1,0:T(8,128)(2,1)} collective-permute-done((bf16[2,384,768]{2,1,0:T(8,128)(2,1)S(1)}, bf16[2,384,768]{2,1,0:T(8,128)(2,1)}, u32[]{:S(2)}, u32[]{:S(2)}) %collective-permute-start.24) | collective-permute-done | bytes 1179680 | tf_op jit(solution)/shard_map/ff_heads/ppermute | solution.py:714
  308.2 3.2 fusion.14
  312.8 1.9 collective-permute-start.28
  314.7 30.3 %self_backward_a.1 = (f32[2,272,768]{2,1,0:T(8,128)}, f32[2,272,768]{2,1,0:T(8,128)}, bf16[544,768]{1,0:T(8,128)(2,1)}, bf16[2,320,768]{2,1,0:T(8,128)(2,1)}, bf...) custom-call(s32[2]{0:T(128)} %pad_add_fusion.refs_0_, ...), custom_call_target="tpu_custom_call" | custom-call | flops 1000 | bytes 1000 | tf_op jit(solution)/shard_map/self_backward_a/pallas_call | solution.py:680
  352.2 3.0 collective-permute-start.34
  355.3 2.8 fusion.1
  360.0 2.3 collective-permute-done.49
  362.3 2.3 collective-permute-start.61
  364.6 1.9 fusion.28
  367.5 27.1 %self_backward_b.1 = (f32[2,272,768]{2,1,0:T(8,128)}, bf16[2,272,768]{2,1,0:T(8,128)(2,1)}, bf16[2,320,768]{2,1,0:T(8,128)(2,1)}, bf16[2,320,768]{2,1,0:T(8,128)(2,1)}, f32[8,128]{1,0:T(8,128)}) custom-call(s32[2]{0:T(128)} %pad_add_fusion.refs_0_, bf16[544,768]{1,0:T(8,128)(2,1)} %get-tuple-element.105.refs_1_, f32[2,272,768]{2,1,0:T(8,128)} %get-tuple-element.106.refs_2_, ...), custom_call_target="tpu_custom_call" | custom-call | flops 1000 | bytes 1000 | tf_op jit(solution)/shard_map/self_backward_b/pallas_call | solution.py:680
  399.6 1.9 fusion.17
  401.5 3.5 collective-permute-done.50
  413.0 3.1 collective-permute-done.53
  416.1 2.7 collective-permute-done.54
  418.8 6.9 %collective-permute-done.55 = bf16[104,768]{1,0:T(8,128)(2,1)S(1)} collective-permute-done((bf16[104,768]{1,0:T(8,128)(2,1)S(1)}, bf16[104,768]{1,0:T(8,128)(2,1)S(1)}, u32[]{:S(2)}, u32[]{:S(2)}) %collective-permute-start.55) | collective-permute-done | bytes 159776 | tf_op jit(solution)/shard_map/c_depth/ppermute | solution.py:714
  425.8 2.2 collective-permute-start.56
  432.1 2.1 collective-permute-done.56
  435.3 4.2 collective-permute-done.57
  440.5 2.1 collective-permute-start.59
  445.1 3.4 collective-permute-start.32
  450.3 9.6 %collective-permute-done.37 = bf16[2,192,768]{2,1,0:T(8,128)(2,1)S(1)} collective-permute-done((bf16[2,192,768]{2,1,0:T(8,128)(2,1)S(1)}, bf16[2,192,768]{2,1,0:T(8,128)(2,1)S(1)}, u32[]{:S(2)}, u32[]{:S(2)}) %collective-permute-start.37) | collective-permute-done | bytes 589856 | tf_op jit(solution)/shard_map/s_heads/ppermute | solution.py:714
  461.6 8.0 %collective-permute-done.32 = bf16[272,768]{1,0:T(8,128)(2,1)S(1)} collective-permute-done((bf16[272,768]{1,0:T(8,128)(2,1)S(1)}, bf16[272,768]{1,0:T(8,128)(2,1)S(1)}, u32[]{:S(2)}, u32[]{:S(2)}) %collective-permute-start.32) | collective-permute-done | bytes 417824 | tf_op jit(solution)/shard_map/in_a/ppermute | solution.py:714
  470.6 5.6 %collective-permute-done.41 = bf16[224,768]{1,0:T(8,128)(2,1)S(1)} collective-permute-done((bf16[224,768]{1,0:T(8,128)(2,1)S(1)}, bf16[224,768]{1,0:T(8,128)(2,1)S(1)}, u32[]{:S(2)}, u32[]{:S(2)}) %collective-permute-start.41) | collective-permute-done | bytes 344096 | tf_op jit(solution)/shard_map/s_heads_2/ppermute | solution.py:714
  479.8 3.3 collective-permute-done.42
  483.2 3.4 collective-permute-done.43
  486.5 6.9 %collective-permute-done.44 = bf16[104,768]{1,0:T(8,128)(2,1)S(1)} collective-permute-done((bf16[104,768]{1,0:T(8,128)(2,1)S(1)}, bf16[104,768]{1,0:T(8,128)(2,1)S(1)}, u32[]{:S(2)}, u32[]{:S(2)}) %collective-permute-start.44) | collective-permute-done | bytes 159776 | tf_op jit(solution)/shard_map/s_depth/ppermute | solution.py:714
  496.2 5.2 collective-permute-done.45
  501.4 4.9 collective-permute-done.46
  515.6 2.1 copy.64
  (387 shorter events, 117.6 us)
Async XLA Ops:
  7.2 422.1 %all-gather.4.cloned.1.call-start = ((), (), s32[]{:S(2)}) async-start(), calls=%async_computation | async-start | bytes 1622016 | tf_op jit(solution)/shard_map/all_gather | solution.py:888
  15.8 39.6 %collective-permute-start.4 = (bf16[400,768]{1,0:T(8,128)(2,1)}, bf16[400,768]{1,0:T(8,128)(2,1)S(1)}, u32[]{:S(2)}, u32[]{:S(2)}) collective-permute-start(bf16[400,768]{1,0:T(8,128)(2,1)} %pad_dynamic-update-slice_fusion.1), channel_id=1, source_target_pairs={{0,8},{8,0},{16,24},{24,16},{1,9},{9,1},{17,25},{25,17},{2,10},{10... | collective-permute-start | bytes 1843208 | tf_op jit(solution)/shard_map/w_self_near/ppermute | solution.py:714
  17.0 39.4 %collective-permute-start.5 = (bf16[400,768]{1,0:T(8,128)(2,1)}, bf16[400,768]{1,0:T(8,128)(2,1)S(1)}, u32[]{:S(2)}, u32[]{:S(2)}) collective-permute-start(bf16[400,768]{1,0:T(8,128)(2,1)} %pad_dynamic-update-slice_fusion.1), channel_id=1, source_target_pairs={{0,16},{8,24},{16,0},{24,8},{1,17},{9,25},{17,1},{25,9},{2,18},{10... | collective-permute-start | bytes 1843208 | tf_op jit(solution)/shard_map/w_self_near/ppermute | solution.py:714
  18.3 38.2 %collective-permute-start.6 = (bf16[400,768]{1,0:T(8,128)(2,1)}, bf16[400,768]{1,0:T(8,128)(2,1)S(1)}, u32[]{:S(2)}, u32[]{:S(2)}) collective-permute-start(bf16[400,768]{1,0:T(8,128)(2,1)} %pad_dynamic-update-slice_fusion.1), channel_id=1, source_target_pairs={{0,24},{8,16},{16,8},{24,0},{1,25},{9,17},{17,9},{25,1},{2,26},{10... | collective-permute-start | bytes 1843208 | tf_op jit(solution)/shard_map/w_self_near/ppermute | solution.py:714
  21.4 34.0 %collective-permute-start = (bf16[288,768]{1,0:T(8,128)(2,1)}, bf16[288,768]{1,0:T(8,128)(2,1)S(1)}, u32[]{:S(2)}, u32[]{:S(2)}) collective-permute-start(bf16[288,768]{1,0:T(8,128)(2,1)} %pad_maximum_fusion.5), channel_id=1, source_target_pairs={{0,0},{8,1},{16,16},{24,17},{1,8},{9,9},{17,24},{25,25},{2,2},{10,... | collective-permute-start | bytes 1327112 | tf_op jit(solution)/shard_map/x_a/ppermute | solution.py:714
  25.9 27.6 %collective-permute-start.1 = (bf16[272,768]{1,0:T(8,128)(2,1)}, bf16[272,768]{1,0:T(8,128)(2,1)S(1)}, u32[]{:S(2)}, u32[]{:S(2)}) collective-permute-start(bf16[272,768]{1,0:T(8,128)(2,1)} %get-tuple-element.183), channel_id=1, source_target_pairs={{0,1},{8,0},{16,17},{24,16},{1,9},{9,8},{17,25},{25,24},{2,3},{10,... | collective-permute-start | bytes 1253384 | tf_op jit(solution)/shard_map/x_b/ppermute | solution.py:714
  61.8 30.9 %collective-permute-start.12 = (bf16[400,768]{1,0:T(8,128)(2,1)S(1)}, bf16[400,768]{1,0:T(8,128)(2,1)S(1)}, u32[]{:S(2)}, u32[]{:S(2)}) collective-permute-start(bf16[400,768]{1,0:T(8,128)(2,1)S(1)} %broadcast_add_fusion.9.refs_16_), channel_id=1, source_target_pairs={{0,24},{8,16},{16,8},{24,0},{1,25},{9,17},{17,9},{25,1},{2,26},{10... | collective-permute-start | bytes 1843208 | tf_op jit(solution)/shard_map/w_cross_near/ppermute | solution.py:714
  63.5 33.3 %collective-permute-start.11 = (bf16[400,768]{1,0:T(8,128)(2,1)S(1)}, bf16[400,768]{1,0:T(8,128)(2,1)S(1)}, u32[]{:S(2)}, u32[]{:S(2)}) collective-permute-start(bf16[400,768]{1,0:T(8,128)(2,1)S(1)} %broadcast_add_fusion.9.refs_16_), channel_id=1, source_target_pairs={{0,16},{8,24},{16,0},{24,8},{1,17},{9,25},{17,1},{25,9},{2,18},{10... | collective-permute-start | bytes 1843208 | tf_op jit(solution)/shard_map/w_cross_near/ppermute | solution.py:714
  65.7 31.9 %collective-permute-start.13 = (bf16[512,768]{1,0:T(8,128)(2,1)S(1)}, bf16[512,768]{1,0:T(8,128)(2,1)S(1)}, u32[]{:S(2)}, u32[]{:S(2)}) collective-permute-start(bf16[512,768]{1,0:T(8,128)(2,1)S(1)} %broadcast_add_fusion.5.refs_17_), channel_id=1, source_target_pairs={{0,0},{8,1},{16,16},{24,17},{1,8},{9,9},{17,24},{25,25},{2,2},{10,... | collective-permute-start | bytes 2359304 | tf_op jit(solution)/shard_map/e_a/ppermute | solution.py:714
  69.6 29.3 %collective-permute-start.10 = (bf16[400,768]{1,0:T(8,128)(2,1)S(1)}, bf16[400,768]{1,0:T(8,128)(2,1)S(1)}, u32[]{:S(2)}, u32[]{:S(2)}) collective-permute-start(bf16[400,768]{1,0:T(8,128)(2,1)S(1)} %broadcast_add_fusion.9.refs_16_), channel_id=1, source_target_pairs={{0,8},{8,0},{16,24},{24,16},{1,9},{9,1},{17,25},{25,17},{2,10},{10... | collective-permute-start | bytes 1843208 | tf_op jit(solution)/shard_map/w_cross_near/ppermute | solution.py:714
  94.3 28.6 %collective-permute-start.17 = (bf16[400,768]{1,0:T(8,128)(2,1)}, bf16[400,768]{1,0:T(8,128)(2,1)S(1)}, u32[]{:S(2)}, u32[]{:S(2)}) collective-permute-start(bf16[400,768]{1,0:T(8,128)(2,1)} %broadcast_add_fusion.6), channel_id=1, source_target_pairs={{0,1},{8,9},{16,17},{24,25},{1,0},{9,8},{17,16},{25,24},{2,3},{10,... | collective-permute-start | bytes 1843208 | tf_op jit(solution)/shard_map/w_cross_far/ppermute | solution.py:714
  97.5 30.2 %collective-permute-start.16 = (bf16[400,768]{1,0:T(8,128)(2,1)S(1)}, bf16[400,768]{1,0:T(8,128)(2,1)S(1)}, u32[]{:S(2)}, u32[]{:S(2)}) collective-permute-start(bf16[400,768]{1,0:T(8,128)(2,1)S(1)} %broadcast_add_fusion.7), channel_id=1, source_target_pairs={{0,1},{8,9},{16,17},{24,25},{1,0},{9,8},{17,16},{25,24},{2,3},{10,... | collective-permute-start | bytes 1843208 | tf_op jit(solution)/shard_map/w_cross_far/ppermute | solution.py:714
  98.3 29.4 %collective-permute-start.14 = (bf16[512,768]{1,0:T(8,128)(2,1)S(1)}, bf16[512,768]{1,0:T(8,128)(2,1)S(1)}, u32[]{:S(2)}, u32[]{:S(2)}) collective-permute-start(bf16[512,768]{1,0:T(8,128)(2,1)S(1)} %broadcast_add_fusion.4), channel_id=1, source_target_pairs={{0,1},{8,9},{16,17},{24,25},{1,0},{9,8},{17,16},{25,24},{2,3},{10,... | collective-permute-start | bytes 2359304 | tf_op jit(solution)/shard_map/e_b/ppermute | solution.py:714
  99.5 28.1 %collective-permute-start.15 = (bf16[400,768]{1,0:T(8,128)(2,1)S(1)}, bf16[400,768]{1,0:T(8,128)(2,1)S(1)}, u32[]{:S(2)}, u32[]{:S(2)}) collective-permute-start(bf16[400,768]{1,0:T(8,128)(2,1)S(1)} %broadcast_add_fusion.8), channel_id=1, source_target_pairs={{0,1},{8,9},{16,17},{24,25},{1,0},{9,8},{17,16},{25,24},{2,3},{10,... | collective-permute-start | bytes 1843208 | tf_op jit(solution)/shard_map/w_cross_far/ppermute | solution.py:714
  108.8 43.9 %collective-permute-start.18 = (bf16[272,768]{1,0:T(8,128)(2,1)S(1)}, bf16[272,768]{1,0:T(8,128)(2,1)S(1)}, u32[]{:S(2)}, u32[]{:S(2)}) collective-permute-start(bf16[272,768]{1,0:T(8,128)(2,1)S(1)} %get-tuple-element.182), channel_id=1, source_target_pairs={{0,0},{8,1},{16,16},{24,17},{1,8},{9,9},{17,24},{25,25},{2,2},{10,... | collective-permute-start | bytes 1253384 | tf_op jit(solution)/shard_map/g_a/ppermute | solution.py:714
  122.9 29.9 %collective-permute-start.19 = (bf16[272,768]{1,0:T(8,128)(2,1)S(1)}, bf16[272,768]{1,0:T(8,128)(2,1)S(1)}, u32[]{:S(2)}, u32[]{:S(2)}) collective-permute-start(bf16[272,768]{1,0:T(8,128)(2,1)S(1)} %get-tuple-element.181), channel_id=1, source_target_pairs={{0,1},{8,0},{16,17},{24,16},{1,9},{9,8},{17,25},{25,24},{2,3},{10,... | collective-permute-start | bytes 1253384 | tf_op jit(solution)/shard_map/g_b/ppermute | solution.py:714
  194.2 49.6 %collective-permute-start.22 = (bf16[4,2,384,768]{3,2,1,0:T(8,128)(2,1)}, bf16[4,2,384,768]{3,2,1,0:T(8,128)(2,1)}, u32[]{:S(2)}, u32[]{:S(2)}) collective-permute-start(bf16[4,2,384,768]{3,2,1,0:T(8,128)(2,1)} %get-tuple-element.95), channel_id=1, source_target_pairs={{0,1},{8,9},{16,17},{24,25},{1,0},{9,8},{17,16},{25,24},{2,3},{10,... | collective-permute-start | bytes 14155784 | tf_op jit(solution)/shard_map/ff_core/ppermute | solution.py:714
  226.7 16.2 %collective-permute-start.26 = (bf16[4,96,768]{2,1,0:T(8,128)(2,1)S(1)}, bf16[4,96,768]{2,1,0:T(8,128)(2,1)S(1)}, u32[]{:S(2)}, u32[]{:S(2)}) collective-permute-start(bf16[4,96,768]{2,1,0:T(8,128)(2,1)S(1)} %broadcast_add_fusion.11), channel_id=1, source_target_pairs={{0,1},{8,9},{16,17},{24,25},{1,0},{9,8},{17,16},{25,24},{2,3},{10,... | collective-permute-start | bytes 1769480 | tf_op jit(solution)/shard_map/co_core/ppermute | solution.py:714
  227.7 13.5 %collective-permute-start.20 = (bf16[272,768]{1,0:T(8,128)(2,1)}, bf16[272,768]{1,0:T(8,128)(2,1)S(1)}, u32[]{:S(2)}, u32[]{:S(2)}) collective-permute-start(bf16[272,768]{1,0:T(8,128)(2,1)} %get-tuple-element.179), channel_id=1, source_target_pairs={{0,0},{8,1},{16,16},{24,17},{1,8},{9,9},{17,24},{25,25},{2,2},{10,... | collective-permute-start | bytes 1253384 | tf_op jit(solution)/shard_map/out_a/ppermute | solution.py:714
  231.2 10.6 %collective-permute-start.21 = (bf16[272,768]{1,0:T(8,128)(2,1)S(1)}, bf16[272,768]{1,0:T(8,128)(2,1)S(1)}, u32[]{:S(2)}, u32[]{:S(2)}) collective-permute-start(bf16[272,768]{1,0:T(8,128)(2,1)S(1)} %get-tuple-element.180), channel_id=1, source_target_pairs={{0,8},{8,9},{16,24},{24,25},{1,0},{9,1},{17,16},{25,17},{2,10},{10... | collective-permute-start | bytes 1253384 | tf_op jit(solution)/shard_map/out_b/ppermute | solution.py:714
  233.0 47.4 %collective-permute-start.25 = (bf16[2,320,768]{2,1,0:T(8,128)(2,1)}, bf16[2,320,768]{2,1,0:T(8,128)(2,1)S(1)}, u32[]{:S(2)}, u32[]{:S(2)}) collective-permute-start(bf16[2,320,768]{2,1,0:T(8,128)(2,1)} %broadcast_add_fusion.2), channel_id=1, source_target_pairs={{0,1},{8,9},{16,17},{24,25},{1,0},{9,8},{17,16},{25,24},{2,3},{10,... | collective-permute-start | bytes 2949128 | tf_op jit(solution)/shard_map/ca_core/ppermute | solution.py:714
  280.6 27.6 %collective-permute-start.24 = (bf16[2,384,768]{2,1,0:T(8,128)(2,1)S(1)}, bf16[2,384,768]{2,1,0:T(8,128)(2,1)}, u32[]{:S(2)}, u32[]{:S(2)}) collective-permute-start(bf16[2,384,768]{2,1,0:T(8,128)(2,1)S(1)} %copy-done.16), channel_id=1, source_target_pairs={{0,16},{8,24},{16,0},{24,8},{1,17},{9,25},{17,1},{25,9},{2,18},{10... | collective-permute-start | bytes 3538952 | tf_op jit(solution)/shard_map/ff_heads/ppermute | solution.py:714
  280.9 27.3 %collective-permute-start.23 = (bf16[2,384,768]{2,1,0:T(8,128)(2,1)S(1)}, bf16[2,384,768]{2,1,0:T(8,128)(2,1)}, u32[]{:S(2)}, u32[]{:S(2)}) collective-permute-start(bf16[2,384,768]{2,1,0:T(8,128)(2,1)S(1)} %copy-done.17), channel_id=1, source_target_pairs={{0,8},{8,0},{16,24},{24,16},{1,9},{9,1},{17,25},{25,17},{2,10},{10... | collective-permute-start | bytes 3538952 | tf_op jit(solution)/shard_map/ff_heads/ppermute | solution.py:714
  285.8 64.4 %collective-permute-start.30 = (bf16[512,768]{1,0:T(8,128)(2,1)}, bf16[512,768]{1,0:T(8,128)(2,1)}, u32[]{:S(2)}, u32[]{:S(2)}) collective-permute-start(bf16[512,768]{1,0:T(8,128)(2,1)} %broadcast_add_fusion.3), channel_id=1, source_target_pairs={{0,1},{8,9},{16,17},{24,25},{1,0},{9,8},{17,16},{25,24},{2,3},{10,... | collective-permute-start | bytes 2359304 | tf_op jit(solution)/shard_map/enc_core/ppermute | solution.py:714
  311.5 40.7 %collective-permute-start.27 = (bf16[384,768]{1,0:T(8,128)(2,1)S(1)}, bf16[384,768]{1,0:T(8,128)(2,1)}, u32[]{:S(2)}, u32[]{:S(2)}) collective-permute-start(bf16[384,768]{1,0:T(8,128)(2,1)S(1)} %get-tuple-element.139.refs_21_), channel_id=1, source_target_pairs={{0,16},{8,24},{16,0},{24,8},{1,17},{9,25},{17,1},{25,9},{2,18},{10... | collective-permute-start | bytes 1769480 | tf_op jit(solution)/shard_map/ff_heads_2/ppermute | solution.py:714
  312.8 42.4 %collective-permute-start.28 = (bf16[384,768]{1,0:T(8,128)(2,1)S(1)}, bf16[384,768]{1,0:T(8,128)(2,1)}, u32[]{:S(2)}, u32[]{:S(2)}) collective-permute-start(bf16[384,768]{1,0:T(8,128)(2,1)S(1)} %get-tuple-element.138.refs_22_), channel_id=1, source_target_pairs={{0,8},{8,0},{16,24},{24,16},{1,9},{9,1},{17,25},{25,17},{2,10},{10... | collective-permute-start | bytes 1769480 | tf_op jit(solution)/shard_map/ff_heads_2/ppermute | solution.py:714
  347.1 15.2 %collective-permute-start.49 = (bf16[2,192,768]{2,1,0:T(8,128)(2,1)S(1)}, bf16[2,192,768]{2,1,0:T(8,128)(2,1)S(1)}, u32[]{:S(2)}, u32[]{:S(2)}) collective-permute-start(bf16[2,192,768]{2,1,0:T(8,128)(2,1)S(1)} %maximum_add_fusion.10.refs_25_), channel_id=1, source_target_pairs={{0,8},{8,0},{16,24},{24,16},{1,9},{9,1},{17,25},{25,17},{2,10},{10... | collective-permute-start | bytes 1769480 | tf_op jit(solution)/shard_map/c_heads/ppermute | solution.py:714
  348.2 48.2 %collective-permute-start.51 = (bf16[2,224,768]{2,1,0:T(8,128)(2,1)}, bf16[2,224,768]{2,1,0:T(8,128)(2,1)}, u32[]{:S(2)}, u32[]{:S(2)}) collective-permute-start(bf16[2,224,768]{2,1,0:T(8,128)(2,1)} %maximum_add_fusion.4.refs_26_), channel_id=1, source_target_pairs={{0,16},{8,24},{16,0},{24,8},{1,17},{9,25},{17,1},{25,9},{2,18},{10... | collective-permute-start | bytes 2064392 | tf_op jit(solution)/shard_map/c_heads/ppermute | solution.py:714
  350.2 16.3 %collective-permute-start.39 = (bf16[4,96,768]{2,1,0:T(8,128)(2,1)S(1)}, bf16[4,96,768]{2,1,0:T(8,128)(2,1)S(1)}, u32[]{:S(2)}, u32[]{:S(2)}) collective-permute-start(bf16[4,96,768]{2,1,0:T(8,128)(2,1)S(1)} %broadcast_add_fusion.10), channel_id=1, source_target_pairs={{0,1},{8,9},{16,17},{24,25},{1,0},{9,8},{17,16},{25,24},{2,3},{10,... | collective-permute-start | bytes 1769480 | tf_op jit(solution)/shard_map/so_core/ppermute | solution.py:714
  352.2 44.3 %collective-permute-start.34 = (bf16[512,768]{1,0:T(8,128)(2,1)S(1)}, bf16[512,768]{1,0:T(8,128)(2,1)}, u32[]{:S(2)}, u32[]{:S(2)}) collective-permute-start(bf16[512,768]{1,0:T(8,128)(2,1)S(1)} %fusion.4.refs_27_), channel_id=1, source_target_pairs={{0,0},{8,1},{16,16},{24,17},{1,8},{9,9},{17,24},{25,25},{2,2},{10,... | collective-permute-start | bytes 2359304 | tf_op jit(solution)/shard_map/enc_grad/ppermute | solution.py:714
  359.9 38.2 %collective-permute-start.60 = (bf16[2,96,768]{2,1,0:T(8,128)(2,1)}, bf16[2,96,768]{2,1,0:T(8,128)(2,1)}, u32[]{:S(2)}, u32[]{:S(2)}) collective-permute-start(bf16[2,96,768]{2,1,0:T(8,128)(2,1)} %get-tuple-element.146.refs_22_), channel_id=1, source_target_pairs={{0,2},{8,10},{16,18},{24,26},{1,3},{9,11},{17,19},{25,27},{2,0},{1... | collective-permute-start | bytes 884744 | tf_op jit(solution)/shard_map/ff_depth/ppermute | solution.py:714
  362.3 36.6 %collective-permute-start.61 = (bf16[2,96,768]{2,1,0:T(8,128)(2,1)}, bf16[2,96,768]{2,1,0:T(8,128)(2,1)}, u32[]{:S(2)}, u32[]{:S(2)}) collective-permute-start(bf16[2,96,768]{2,1,0:T(8,128)(2,1)} %get-tuple-element.145.refs_23_), channel_id=1, source_target_pairs={{0,4},{8,12},{16,20},{24,28},{1,5},{9,13},{17,21},{25,29},{2,6},{1... | collective-permute-start | bytes 884744 | tf_op jit(solution)/shard_map/ff_depth/ppermute | solution.py:714
  366.5 32.5 %collective-permute-start.62 = (bf16[2,96,768]{2,1,0:T(8,128)(2,1)}, bf16[2,96,768]{2,1,0:T(8,128)(2,1)}, u32[]{:S(2)}, u32[]{:S(2)}) collective-permute-start(bf16[2,96,768]{2,1,0:T(8,128)(2,1)} %get-tuple-element.144.refs_24_), channel_id=1, source_target_pairs={{0,6},{8,14},{16,22},{24,30},{1,7},{9,15},{17,23},{25,31},{2,4},{1... | collective-permute-start | bytes 884744 | tf_op jit(solution)/shard_map/ff_depth/ppermute | solution.py:714
  398.1 46.5 %collective-permute-start.35 = (bf16[2,320,768]{2,1,0:T(8,128)(2,1)}, bf16[2,320,768]{2,1,0:T(8,128)(2,1)S(1)}, u32[]{:S(2)}, u32[]{:S(2)}) collective-permute-start(bf16[2,320,768]{2,1,0:T(8,128)(2,1)} %get-tuple-element.118), channel_id=1, source_target_pairs={{0,1},{8,9},{16,17},{24,25},{1,0},{9,8},{17,16},{25,24},{2,3},{10,... | collective-permute-start | bytes 2949128 | tf_op jit(solution)/shard_map/sb_core/ppermute | solution.py:714
  398.9 44.3 %collective-permute-start.31 = (bf16[2,272,768]{2,1,0:T(8,128)(2,1)}, bf16[2,272,768]{2,1,0:T(8,128)(2,1)}, u32[]{:S(2)}, u32[]{:S(2)}) collective-permute-start(bf16[2,272,768]{2,1,0:T(8,128)(2,1)} %get-tuple-element.116), channel_id=1, source_target_pairs={{0,1},{8,9},{16,17},{24,25},{1,0},{9,8},{17,16},{25,24},{2,3},{10,... | collective-permute-start | bytes 2506760 | tf_op jit(solution)/shard_map/in_core/ppermute | solution.py:714
  412.8 12.9 %collective-permute-start.55 = (bf16[104,768]{1,0:T(8,128)(2,1)S(1)}, bf16[104,768]{1,0:T(8,128)(2,1)S(1)}, u32[]{:S(2)}, u32[]{:S(2)}) collective-permute-start(bf16[104,768]{1,0:T(8,128)(2,1)S(1)} %get-tuple-element.156), channel_id=1, source_target_pairs={{0,6},{8,14},{16,22},{24,30},{1,7},{9,15},{17,23},{25,31},{2,4},{1... | collective-permute-start | bytes 479240 | tf_op jit(solution)/shard_map/c_depth/ppermute | solution.py:714
  428.0 11.5 %collective-permute-start.57 = (bf16[104,768]{1,0:T(8,128)(2,1)S(1)}, bf16[104,768]{1,0:T(8,128)(2,1)S(1)}, u32[]{:S(2)}, u32[]{:S(2)}) collective-permute-start(bf16[104,768]{1,0:T(8,128)(2,1)S(1)} %fusion.20), channel_id=1, source_target_pairs={{0,4},{8,12},{16,20},{24,28},{1,5},{9,13},{17,21},{25,29},{2,6},{1... | collective-permute-start | bytes 479240 | tf_op jit(solution)/shard_map/c_back/ppermute | solution.py:714
  428.0 11.5 %collective-permute-start.58 = (bf16[104,768]{1,0:T(8,128)(2,1)S(1)}, bf16[104,768]{1,0:T(8,128)(2,1)}, u32[]{:S(2)}, u32[]{:S(2)}) collective-permute-start(bf16[104,768]{1,0:T(8,128)(2,1)S(1)} %fusion.20), channel_id=1, source_target_pairs={{0,2},{8,10},{16,18},{24,26},{1,3},{9,11},{17,19},{25,27},{2,0},{1... | collective-permute-start | bytes 479240 | tf_op jit(solution)/shard_map/c_back/ppermute | solution.py:714
  434.2 14.4 %collective-permute-start.40 = (bf16[2,224,768]{2,1,0:T(8,128)(2,1)S(1)}, bf16[2,224,768]{2,1,0:T(8,128)(2,1)S(1)}, u32[]{:S(2)}, u32[]{:S(2)}) collective-permute-start(bf16[2,224,768]{2,1,0:T(8,128)(2,1)S(1)} %maximum_add_fusion.6), channel_id=1, source_target_pairs={{0,16},{8,24},{16,0},{24,8},{1,17},{9,25},{17,1},{25,9},{2,18},{10... | collective-permute-start | bytes 2064392 | tf_op jit(solution)/shard_map/s_heads/ppermute | solution.py:714
  440.5 39.1 %collective-permute-start.59 = (bf16[416,768]{1,0:T(8,128)(2,1)S(1)}, bf16[416,768]{1,0:T(8,128)(2,1)S(1)}, u32[]{:S(2)}, u32[]{:S(2)}) collective-permute-start(bf16[416,768]{1,0:T(8,128)(2,1)S(1)} %pad_maximum_fusion.4), channel_id=1, source_target_pairs={{0,1},{8,9},{16,17},{24,25},{1,0},{9,8},{17,16},{25,24},{2,3},{10,... | collective-permute-start | bytes 1916936 | tf_op jit(solution)/shard_map/c_far/ppermute | solution.py:714
  444.9 15.0 %collective-permute-start.37 = (bf16[2,192,768]{2,1,0:T(8,128)(2,1)S(1)}, bf16[2,192,768]{2,1,0:T(8,128)(2,1)S(1)}, u32[]{:S(2)}, u32[]{:S(2)}) collective-permute-start(bf16[2,192,768]{2,1,0:T(8,128)(2,1)S(1)} %maximum_add_fusion.11), channel_id=1, source_target_pairs={{0,8},{8,0},{16,24},{24,16},{1,9},{9,1},{17,25},{25,17},{2,10},{10... | collective-permute-start | bytes 1769480 | tf_op jit(solution)/shard_map/s_heads/ppermute | solution.py:714
  445.1 24.5 %collective-permute-start.32 = (bf16[272,768]{1,0:T(8,128)(2,1)S(1)}, bf16[272,768]{1,0:T(8,128)(2,1)S(1)}, u32[]{:S(2)}, u32[]{:S(2)}) collective-permute-start(bf16[272,768]{1,0:T(8,128)(2,1)S(1)} %get-tuple-element.177), channel_id=1, source_target_pairs={{0,0},{8,1},{16,16},{24,17},{1,8},{9,9},{17,24},{25,25},{2,2},{10,... | collective-permute-start | bytes 1253384 | tf_op jit(solution)/shard_map/in_a/ppermute | solution.py:714
  448.5 21.1 %collective-permute-start.33 = (bf16[272,768]{1,0:T(8,128)(2,1)S(1)}, bf16[272,768]{1,0:T(8,128)(2,1)S(1)}, u32[]{:S(2)}, u32[]{:S(2)}) collective-permute-start(bf16[272,768]{1,0:T(8,128)(2,1)S(1)} %get-tuple-element.178), channel_id=1, source_target_pairs={{0,8},{8,9},{16,24},{24,25},{1,0},{9,1},{17,16},{25,17},{2,10},{10... | collective-permute-start | bytes 1253384 | tf_op jit(solution)/shard_map/in_b/ppermute | solution.py:714
  448.8 27.4 %collective-permute-start.41 = (bf16[224,768]{1,0:T(8,128)(2,1)S(1)}, bf16[224,768]{1,0:T(8,128)(2,1)S(1)}, u32[]{:S(2)}, u32[]{:S(2)}) collective-permute-start(bf16[224,768]{1,0:T(8,128)(2,1)S(1)} %fusion.6), channel_id=1, source_target_pairs={{0,8},{8,0},{16,24},{24,16},{1,9},{9,1},{17,25},{25,17},{2,10},{10... | collective-permute-start | bytes 1032200 | tf_op jit(solution)/shard_map/s_heads_2/ppermute | solution.py:714
  460.9 15.4 %collective-permute-start.38 = (bf16[192,768]{1,0:T(8,128)(2,1)S(1)}, bf16[192,768]{1,0:T(8,128)(2,1)S(1)}, u32[]{:S(2)}, u32[]{:S(2)}) collective-permute-start(bf16[192,768]{1,0:T(8,128)(2,1)S(1)} %fusion.27), channel_id=1, source_target_pairs={{0,16},{8,24},{16,0},{24,8},{1,17},{9,25},{17,1},{25,9},{2,18},{10... | collective-permute-start | bytes 884744 | tf_op jit(solution)/shard_map/s_heads_2/ppermute | solution.py:714
  479.4 13.9 %collective-permute-start.44 = (bf16[104,768]{1,0:T(8,128)(2,1)S(1)}, bf16[104,768]{1,0:T(8,128)(2,1)S(1)}, u32[]{:S(2)}, u32[]{:S(2)}) collective-permute-start(bf16[104,768]{1,0:T(8,128)(2,1)S(1)} %get-tuple-element.159), channel_id=1, source_target_pairs={{0,6},{8,14},{16,22},{24,30},{1,7},{9,15},{17,23},{25,31},{2,4},{1... | collective-permute-start | bytes 479240 | tf_op jit(solution)/shard_map/s_depth/ppermute | solution.py:714
  494.8 11.4 %collective-permute-start.46 = (bf16[104,768]{1,0:T(8,128)(2,1)S(1)}, bf16[104,768]{1,0:T(8,128)(2,1)S(1)}, u32[]{:S(2)}, u32[]{:S(2)}) collective-permute-start(bf16[104,768]{1,0:T(8,128)(2,1)S(1)} %fusion.23), channel_id=1, source_target_pairs={{0,4},{8,12},{16,20},{24,28},{1,5},{9,13},{17,21},{25,29},{2,6},{1... | collective-permute-start | bytes 479240 | tf_op jit(solution)/shard_map/s_back/ppermute | solution.py:714
  494.8 11.4 %collective-permute-start.47 = (bf16[104,768]{1,0:T(8,128)(2,1)S(1)}, bf16[104,768]{1,0:T(8,128)(2,1)S(1)}, u32[]{:S(2)}, u32[]{:S(2)}) collective-permute-start(bf16[104,768]{1,0:T(8,128)(2,1)S(1)} %fusion.23), channel_id=1, source_target_pairs={{0,2},{8,10},{16,18},{24,26},{1,3},{9,11},{17,19},{25,27},{2,0},{1... | collective-permute-start | bytes 479240 | tf_op jit(solution)/shard_map/s_back/ppermute | solution.py:714
  (94 other events, 698.5 us)
Sparse Core Ops, SparseCore 0:
  287.2 54.8 all-gather.3

commit v2 on v1

v2 whole, which is shorter than its diff:
```python
import jax
import jax.numpy as jnp
from jax import lax
from jax.experimental import pallas as pl
from jax.experimental.pallas import tpu as pltpu
from jax.sharding import PartitionSpec as P

BF = jnp.bfloat16
F32 = jnp.float32
HEAD = 64
PAIR = 128
EPS = 1e-05
ROW = 1088
CHUNK = 272
OWN = 544
ENC = 1024
HALF_ENC = 512
D = 768
GROUP = 192
PIECE = 96
BIAS_ROWS = 16
FF = 3072
MIB = 1 << 20


def nn(a, b):
    return jnp.dot(a, b, preferred_element_type=F32)


def nt(a, b):
    return lax.dot_general(a, b, (((1,), (1,)), ((), ())), preferred_element_type=F32)


def tn(a, b):
    return lax.dot_general(a, b, (((0,), (0,)), ((), ())), preferred_element_type=F32)


def lane_ids(shape):
    return lax.broadcasted_iota(jnp.int32, shape, len(shape) - 1)


def pair_lanes(p):
    return pl.ds(pl.multiple_of(p * PAIR, PAIR), PAIR)


def normalize(total):
    center = total - jnp.mean(total, axis=-1, keepdims=True)
    scale = lax.rsqrt(jnp.mean(center * center, axis=-1, keepdims=True) + EPS)
    return center * scale, scale


def norm_back(grad, hat, scale, gain):
    scaled = grad * gain
    inner = scaled - jnp.mean(scaled, axis=-1, keepdims=True)
    return scale * (inner - hat * jnp.mean(scaled * hat, axis=-1, keepdims=True))


def column(values):
    return jnp.sum(values.astype(F32), axis=0, keepdims=True)


def pick_lane(ref, rows, lane):
    block = ref[rows, :]
    return jnp.sum(jnp.where(lane_ids(block.shape) == lane, block, 0.0), axis=-1, keepdims=True)


def start(copies):
    for one in copies:
        one.start()


def finish(copies):
    for one in copies:
        one.wait()


def by_core(core, body):
    for value in (0, 1):

        @pl.when(core == value)
        def _():
            body(value)


class Late:
    def __init__(self, source, held, sem):
        self.copy = pltpu.make_async_copy(source, held, sem)
        self.copy.start()
        self.held = held
        self.waited = False

    def get(self):
        if not self.waited:
            self.copy.wait()
            self.waited = True
        return self.held


class Early:
    def __init__(self, held, target, sem):
        self.copy = pltpu.make_async_copy(held, target, sem)
        self.held = held
        self.sent = False

    def send(self):
        self.copy.start()
        self.sent = True


def call(kernel, ins, outs, scratch, name, pins=()):
    vmem, anywhere = pl.BlockSpec(memory_space=pltpu.VMEM), pl.BlockSpec(memory_space=pltpu.HBM)
    smem = pl.BlockSpec(memory_space=pltpu.SMEM)
    specs = {"v": vmem, "a": anywhere, "l": anywhere, "e": anywhere, "s": smem}
    late = [(n, x) for n, (x, kind) in enumerate(ins) if kind == "l"]
    early = [(n, out) for n, out in enumerate(outs) if out[2] == "e"]
    first = len(ins)
    last = first + len(pins)
    end = last + len(outs)

    def body(*refs):
        took, gave, rest = list(refs[:first]), list(refs[last:end]), list(refs[end + 1 :])
        own, rest = rest[: len(scratch)], rest[len(scratch) :]
        for n, (at, _) in enumerate(late):
            took[at] = Late(took[at], rest[n], rest[-1].at[n])
        rest = rest[len(late) :]
        for n, (at, _) in enumerate(early):
            gave[at] = Early(rest[n], gave[at], rest[-1].at[len(late) + n])
        kernel(*took, *gave, *own)
        refs[end][...] = jnp.zeros((8, 128), F32)
        for at, _ in late:
            took[at].get()
        for at, _ in early:
            if not gave[at].sent:
                gave[at].send()
        for at, _ in early:
            gave[at].copy.wait()

    extra = [pltpu.VMEM(x.shape, x.dtype) for _, x in late]
    extra += [pltpu.VMEM(out[0], out[1]) for _, out in early]
    extra += [pltpu.SemaphoreType.DMA((max(len(late) + len(early), 1),))]
    return pl.pallas_call(
        body,
        in_specs=[specs[kind] for _, kind in ins] + [anywhere] * len(pins),
        out_specs=[specs[out[2]] for out in outs] + [vmem],
        out_shape=[jax.ShapeDtypeStruct(out[0], out[1]) for out in outs]
        + [jax.ShapeDtypeStruct((8, 128), F32)],
        scratch_shapes=list(scratch) + extra,
        compiler_params=pltpu.CompilerParams(vmem_limit_bytes=58 * MIB),
        cost_estimate=pl.CostEstimate(flops=1000, bytes_accessed=1000, transcendentals=0),
        name=name,
    )(*[x for x, _ in ins], *pins)


def after(value, zero):
    return value + zero[0, 0].astype(value.dtype)


def weight_copies(w, slot, core, own, near, far, dst, sems):
    copies = [pltpu.make_async_copy(own[w], dst.at[pl.ds(0, GROUP)], sems.at[slot, 0])]
    rows = pl.ds(w * PIECE, PIECE)
    for i in (1, 2, 3):
        for at, which, refs in ((i, core, near), (3 + i, 1 - core, far)):
            to = pl.multiple_of(GROUP * i + PIECE * which, PIECE)
            copies.append(
                pltpu.make_async_copy(
                    refs[i - 1].at[rows], dst.at[pl.ds(to, PIECE)], sems.at[slot, at]
                )
            )
    return copies


def bias_copies(near, lines, sems):
    return [
        pltpu.make_async_copy(ref.at[pl.ds(ref.shape[0] - 16, 16)], lines.at[i], sems.at[i])
        for i, ref in enumerate(near)
    ]


def gathered_bias(own_line, lines, which):
    parts = [own_line]
    for i in range(3):
        split = lines[i, 3 * which : 3 * which + 3, :GROUP].astype(F32)
        parts.append(split[0:1] + split[1:2] + split[2:3])
    return jnp.concatenate(parts, axis=1)


def put_rows(target, at, block):
    target[at : at + block.shape[0], :] = block


def store_pieces(core, block, places, own, snd):
    def put(value):
        for g, at in enumerate(places):
            for half in (0, 1):
                row = g * GROUP + half * PIECE
                put_rows(own if half == value else snd, at, block[row : row + PIECE])

    by_core(core, put)


def store_bias(row, places, own, snd):
    for i, at in enumerate(places):
        one = jnp.concatenate(
            [row[:, i * GROUP : (i + 1) * GROUP], jnp.zeros((1, D - GROUP), F32)], axis=1
        )
        block = jnp.concatenate([one, jnp.zeros((BIAS_ROWS - 1, D), F32)], axis=0).astype(BF)
        put_rows(own, at + PIECE, block)
        put_rows(snd, at + PIECE, block)


def forward_heads(q2, keys, values, bias, row_stats, p):
    lane = lane_ids(q2.shape)
    outs = []
    for t in (0, 1):
        query = jnp.where((lane // HEAD) == t, q2, jnp.zeros_like(q2))
        scores = nt(query, keys)
        if bias is not None:
            scores = scores + bias
        highest = jnp.max(scores, axis=-1, keepdims=True)
        raised = jnp.exp(scores - highest)
        total = jnp.sum(raised, axis=-1, keepdims=True)
        outs.append(nn(raised.astype(BF), values) / total)
        row_stats = jnp.where(
            lane_ids(row_stats.shape) == 2 * p + t, highest + jnp.log(total), row_stats
        )
    return jnp.where((lane // HEAD) == 0, outs[0], outs[1]).astype(BF), row_stats


def backward_heads(q2, g2, o2, keys, values, bias, stats, p):
    lane = lane_ids(q2.shape)
    key_lane = lane_ids(keys.shape)
    product = g2.astype(F32) * o2.astype(F32)
    zero = jnp.zeros_like(q2)
    grad_q = grad_k = grad_v = 0.0
    for t in (0, 1):
        mine = (lane // HEAD) == t
        query = jnp.where(mine, q2, zero)
        grad = jnp.where(mine, g2, zero)
        inner = jnp.sum(jnp.where(mine, product, 0.0), axis=-1, keepdims=True)
        lse = jnp.sum(
            jnp.where(lane_ids(stats.shape) == 2 * p + t, stats, 0.0), axis=-1, keepdims=True
        )
        scores = nt(query, keys)
        if bias is not None:
            scores = scores + bias
        shares = jnp.exp(scores - lse)
        grad_shares = nt(grad, values)
        grad_scores = (shares * (grad_shares - inner)).astype(BF)
        grad_v = grad_v + tn(shares.astype(BF), grad)
        grad_k = grad_k + tn(grad_scores, query)
        grad_q = grad_q + nn(
            grad_scores, jnp.where((key_lane // HEAD) == t, keys, jnp.zeros_like(keys))
        )
    return grad_q, grad_k, grad_v


def document_ends(xa, place):
    pair_at = place[1] // 2
    lengths = jnp.where(
        pair_at == 0,
        xa[0:1, :8] * 16.0 + xa[2:3, :8],
        xa[1:2, :8] * 16.0
        + xa[3:4, :8],
    )
    ends, total = [], 0.0
    for d in range(8):
        total = total + lengths[:, d : d + 1]
        ends.append(total)
    return ends


def mask_bias(ends, chunk, width):
    qpos = chunk * CHUNK + lax.broadcasted_iota(jnp.int32, (CHUNK, 1), 0)
    kpos = lax.broadcasted_iota(jnp.int32, (1, width), 1)
    qat, kat = qpos.astype(F32), kpos.astype(F32)
    qseg = jnp.zeros((CHUNK, 1), F32)
    kseg = jnp.zeros((1, width), F32)
    for end in ends:
        qseg = qseg + jnp.where(qat >= end, 1.0, 0.0)
        kseg = kseg + jnp.where(kat >= end, 1.0, 0.0)
    return jnp.where((qseg == kseg) & (kpos <= qpos), 0.0, -1000000000.0)


def chunk_of(core, which):
    return (2 * core, 3 - 2 * core, 2 - 2 * core, 1 + 2 * core)[which]


def chunk_rows(core, which):
    return pl.ds(pl.multiple_of(chunk_of(core, which) * CHUNK, 16), CHUNK)


def key_counts(core):
    return ((0, 1), (1, 4)) if core == 0 else ((0, 3), (1, 2))


def prepare(
    place, x, lengths, wq, wk, wv, qbias, vbias, so, cwq, cwk, cwv, cwo, cqbias, cvbias, out_grad,
    xa, xb, mine, mine_cross, ga, gb,
):
    core = place[0]
    ga[...] = out_grad[0:CHUNK, :]
    gb[...] = out_grad[CHUNK:OWN, :]
    xa[0:CHUNK, :] = x[0:CHUNK, :]
    xa[CHUNK : CHUNK + 16, :] = jnp.zeros((16, D), BF)
    xa[CHUNK : CHUNK + 16, 0:128] = lengths[...]
    xb[...] = x[CHUNK:OWN, :]
    prepare_weights(core, (wq, wk, wv), qbias, vbias, mine)
    prepare_weights(core, (cwq, cwk, cwv, cwo, so), cqbias, cvbias, mine_cross)


def prepare_weights(core, weights, qbias, vbias, mine):
    half = pl.ds(pl.multiple_of(core * PIECE, PIECE), PIECE)
    for w, one in enumerate(weights):
        mine[w * PIECE : (w + 1) * PIECE, :] = one[half, :]
    rows = []
    for one in (qbias[...], vbias[...]):
        for _ in range(3):
            top = one.astype(BF).astype(F32)
            rows.append(top)
            one = one - top
    rows = jnp.concatenate(rows + [jnp.zeros((10, GROUP), F32)], axis=0)
    at = len(weights) * PIECE
    mine[at : at + 16, :] = jnp.concatenate(
        [rows, jnp.zeros((16, D - GROUP), F32)], axis=1
    ).astype(BF)


def gate(*refs):
    pass


def row_copies(core, xs, full, sems):
    return [
        pltpu.make_async_copy(
            x.at[pl.ds(0, CHUNK)], full.at[chunk_rows(core, which)], sems.at[which]
        )
        for which, x in enumerate(xs)
    ]


def self_forward(
    place, xa, xb, ya, yb, w0, w1, w2, n1, n2, n3, f1, f2, f3, qbias, vbias,
    q_out, k_out, v_out, att, stats,
    wq, wk, wv, full, bias, lines, sems, line_sems, row_sems,
):
    core = place[0]
    near, far = (n1, n2, n3), (f1, f2, f3)
    sets = [
        weight_copies(w, w, core, (w0, w1, w2), near, far, dst, sems)
        for w, dst in enumerate((wq, wk, wv))
    ]
    held = bias_copies(near, lines, line_sems)
    rows = row_copies(core, (xa, xb, ya, yb), full, row_sems)
    start(rows)
    start(held)
    for one in sets:
        start(one)
    finish(rows[:1])
    tail = pltpu.make_async_copy(xa.at[pl.ds(CHUNK, 16)], lines.at[3], line_sems.at[3])
    tail.start()
    tail.wait()
    ends = document_ends(lines[3].astype(F32), place)
    for slot in (0, 1):
        bias[slot] = mask_bias(ends, chunk_of(core, slot), ROW)
    finish(rows[1:])
    finish(held)
    for one in sets:
        finish(one)
    line = gathered_bias(qbias[...], lines, 0)
    k_out.held[...] = nt(full[...], wk[...]).astype(BF)
    k_out.send()
    for which in (0, 1):
        q_out.held[which * CHUNK : (which + 1) * CHUNK, :] = (
            (nt(full[chunk_rows(core, which), :], wq[...]) + line) * 0.125
        ).astype(BF)
    q_out.send()
    line = gathered_bias(vbias[...], lines, 1)
    v_out.held[...] = (nt(full[...], wv[...]) + line).astype(BF)
    v_out.send()
    q, k, v = q_out.held, k_out.held, v_out.held
    stats[...] = jnp.zeros_like(stats)

    def attend(value):
        def pair(p, carry):
            lanes = pair_lanes(p)
            for slot, count in key_counts(value):
                rows = pl.ds(slot * CHUNK, CHUNK)
                width = count * CHUNK
                out, now = forward_heads(
                    q[rows, lanes], k[0:width, lanes], v[0:width, lanes],
                    bias[slot, :, 0:width], stats[rows, :], p,
                )
                att[rows, lanes] = out
                stats[rows, :] = now
            return carry

        lax.fori_loop(0, 6, pair, 0)

    by_core(core, attend)


def cross_forward(
    place, xa, xb, self_att, self_bias, gain1, shift1, ea, eb, w0, w1, w2, w3, w4, n1, n2, n3,
    f1, f2, f3, qbias, vbias, obias,
    hat1, scale1, q_out, k_out, v_out, att, stats, hat_out,
    wq, wk, wv, wo, full, lines, sems, line_sems, row_sems, self_wo, self_sems,
):
    core = place[0]
    near, far = (n1, n2, n3), (f1, f2, f3)
    rows = [
        pltpu.make_async_copy(e, full.at[pl.ds(i * HALF_ENC, HALF_ENC)], row_sems.at[i])
        for i, e in enumerate((ea, eb))
    ]
    held = bias_copies(near, lines, line_sems)
    sets = [
        weight_copies(w, w, core, (w0, w1, w2, w3), near, far, dst, sems)
        for w, dst in enumerate((wq, wk, wv, wo))
    ]
    self_set = weight_copies(
        4, 0, core, (None, None, None, None, w4), near, far, self_wo, self_sems
    )
    start(self_set)
    start(held)
    start(sets[0])
    start(rows)
    for one in sets[1:]:
        start(one)
    finish(self_set)
    product = nn(self_att[...], self_wo[...]) + self_bias[...]
    for which, x in enumerate((xa, xb)):
        part = slice(which * CHUNK, (which + 1) * CHUNK)
        hat, scale = normalize(x[0:CHUNK, :].astype(F32) + product[part])
        hat1.held[part, :] = hat
        scale1[part, :] = jnp.broadcast_to(scale, (CHUNK, 128))
    hat1.send()
    hidden = (hat1.held[...] * gain1[...] + shift1[...]).astype(BF)
    finish(held)
    finish(sets[0])
    line = gathered_bias(qbias[...], lines, 0)
    q_out.held[...] = ((nt(hidden, wq[...]) + line) * 0.125).astype(BF)
    q_out.send()
    finish(rows)
    finish(sets[1])
    k_out.held[...] = nt(full[...], wk[...]).astype(BF)
    k_out.send()
    finish(sets[2])
    line = gathered_bias(vbias[...], lines, 1)
    v_out.held[...] = (nt(full[...], wv[...]) + line).astype(BF)
    v_out.send()
    finish(sets[3])
    q, k, v = q_out.held, k_out.held, v_out.held
    stats[...] = jnp.zeros_like(stats)

    def pair(p, carry):
        lanes = pair_lanes(p)
        out, now = forward_heads(q[:, lanes], k[:, lanes], v[:, lanes], None, stats[...], p)
        att[:, lanes] = out
        stats[...] = now
        return carry

    lax.fori_loop(0, 6, pair, 0)
    hidden = hat1.held[...] * gain1[...] + shift1[...]
    hat, scale = normalize(hidden + (nn(att[...], wo[...]) + obias[...]))
    hat_out[...] = hat
    stats[...] = jnp.where(lane_ids(stats.shape) == 12, scale, stats[...])


FF_STEP = 512
FF_BLOCK = 768


def gelu_parts(u):
    size = jnp.abs(u)
    t = 1.0 / (1.0 + (0.3275911 * 0.7071067811865476) * size)
    poly = t * (
        0.254829592
        + t * (-0.284496736 + t * (1.421413741 + t * (-1.453152027 + t * 1.061405429)))
    )
    bell = jnp.exp(-0.5 * u * u)
    tail = 0.5 * poly * bell
    phi = jnp.where(u >= 0.0, 1.0 - tail, tail)
    return u * phi, phi + u * bell * 0.3989422804014327


def feed_forward(
    place, hat2, stats, gain2, shift2, up_hbm, up_bias, down_hbm, down_bias, gain3, shift3,
    ga, gb,
    out_a, out_b, dsecond, left, right, vec, upb,
    up, down, active, slope, hid, total, third, grads, sems, left_sems, right_sems,
):
    steps = FF // FF_STEP
    ups = [
        pltpu.make_async_copy(
            up_hbm.at[:, pl.ds(i * FF_STEP, FF_STEP)],
            up.at[:, pl.ds(i * FF_STEP, FF_STEP)],
            sems.at[0, i],
        )
        for i in range(steps)
    ]
    downs = [
        pltpu.make_async_copy(
            down_hbm.at[pl.ds(i * FF_STEP, FF_STEP)],
            down.at[pl.ds(i * FF_STEP, FF_STEP)],
            sems.at[1, i],
        )
        for i in range(steps)
    ]
    for i in range(steps):
        ups[i].start()
        downs[i].start()
    second = hat2[...] * gain2[...] + shift2[...]
    hid[...] = second.astype(BF)
    to_right = [
        pltpu.make_async_copy(ref, right.at[i], right_sems.at[i]) for i, ref in enumerate((hid, third))
    ]
    to_right[0].start()
    total[...] = second + down_bias[...]
    for i in range(steps):
        cols = pl.ds(i * FF_STEP, FF_STEP)
        ups[i].wait()
        u = nn(hid[...], up[:, cols]) + up_bias[:, cols]
        act, slo = gelu_parts(u)
        active[:, cols] = act.astype(BF)
        slope[:, cols] = slo
        downs[i].wait()
        total[...] += nn(active[:, cols], down[cols, :])
    to_left = [
        pltpu.make_async_copy(ref, left.at[i], left_sems.at[i])
        for i, ref in enumerate((grads, active))
    ]
    to_left[1].start()
    hat3, scale3 = normalize(total[...])
    out = (hat3 * gain3[...] + shift3[...]).astype(BF)
    out_a[...] = out[0:CHUNK]
    out_b[...] = out[CHUNK:OWN]
    grad = jnp.concatenate([ga.get()[...], gb.get()[...]], axis=0).astype(F32)
    vec[0:1, :] = column(grad * hat3)
    vec[1:2, :] = column(grad)
    dthird = norm_back(grad, hat3, scale3, gain3[...])
    total[...] = dthird
    third[...] = dthird.astype(BF)
    to_right[1].start()
    vec[2:3, :] = column(third[...])
    for i in range(FF // FF_BLOCK):
        cols = pl.ds(i * FF_BLOCK, FF_BLOCK)
        du = (nt(third[...], down[cols, :]) * slope[:, cols]).astype(BF)
        grads[:, cols] = du
        upb[:, cols] = column(du)
        total[...] += nt(du, up[:, cols])
    to_left[0].start()
    grad = total[...]
    hat = hat2[...]
    scale = pick_lane(stats, slice(None), 12)
    vec[3:4, :] = column(grad * hat)
    vec[4:5, :] = column(grad)
    dsec = norm_back(grad, hat, scale, gain2[...])
    dsecond[...] = dsec
    vec[5:6, :] = column(dsec.astype(BF))
    vec[6:8, :] = jnp.zeros((2, D), F32)
    finish(to_left)
    finish(to_right)


def ff_weight_grads(place, left, right, pins, out, held, left_held, right_held, sems):
    which = place[3]
    copies = [pltpu.make_async_copy(right.at[which], right_held, sems.at[0])]
    for i in range(4):
        cols = pl.ds(pl.multiple_of((place[1] ^ i) * D, D), D)
        copies.append(
            pltpu.make_async_copy(left.at[which, :, cols], left_held.at[i], sems.at[1 + i])
        )
    start(copies)
    copies[0].wait()
    outs = []
    for i in range(4):
        copies[1 + i].wait()
        rows = pl.ds(i * D, D)
        held[rows, :] = tn(left_held[i], right_held[...]).astype(BF)
        outs.append(pltpu.make_async_copy(held.at[rows], out.at[rows], sems.at[5 + i]))
        outs[i].start()
    finish(outs)


def out_grads(core, att, low, wo, grad, places, own, snd):
    store_pieces(core, tn(att[...], low[...]).astype(BF), places, own, snd)
    store_bias(jnp.zeros((1, D), F32), places, own, snd)
    grad[...] = nt(low[...], wo[...]).astype(BF)


def weight_grads(core, dq, dk, dv, queries, keys, places, own, snd):
    store_pieces(core, tn(dq[...], queries).astype(BF), places[0], own, snd)
    store_pieces(core, tn(dk[...], keys).astype(BF), places[1], own, snd)
    store_pieces(core, tn(dv[...], keys).astype(BF), places[2], own, snd)
    store_bias(column(dq[...]), places[0], own, snd)
    store_bias(jnp.zeros((1, dk.shape[1]), F32), places[1], own, snd)
    store_bias(column(dv[...]), places[2], own, snd)


def cross_part(core, first, grad, att, q, k, v, stats, queries, full, sets, places, own, snd, scratch):
    wq, wk, wv, dq, dk, dv = scratch
    q, k, v = q.get(), k.get(), v.get()

    def pair(p, carry):
        lanes = pair_lanes(first + p)
        out = pair_lanes(p)
        gq, gk, gv = backward_heads(
            q[:, lanes], grad[:, lanes], att[:, lanes], k[:, lanes], v[:, lanes],
            None, stats[...], first + p,
        )
        dq[:, out] = (gq * 0.125).astype(BF)
        dk[:, out] = gk.astype(BF)
        dv[:, out] = gv.astype(BF)
        return carry

    lax.fori_loop(0, 3, pair, 0)
    weight_grads(core, dq, dk, dv, queries(), full[...], places, own.held, snd.held)
    own.send()
    for one in sets:
        finish(one)
    return nn(dk[...], wk[...]) + nn(dv[...], wv[...]), nn(dq[...], wq[...])


def cross_backward_a(
    place, dsecond, att, q, k, v, stats, hat1, gain1, shift1, ea, eb,
    w0, w1, w2, w3, n1, n2, n3, f1, f2, f3,
    enc_out, dfirst, grad, own, snd,
    wq, wk, wv, wo, dq, dk, dv, low, full, sems, row_sems,
):
    core = place[0]
    near, far, ws = (n1, n2, n3), (f1, f2, f3), (w0, w1, w2, w3)
    sets = [weight_copies(3, 3, core, ws, near, far, wo, sems)] + [
        half_weight_copies(w, w, core, ws, near, far, 1, dst, sems)
        for w, dst in enumerate((wq, wk, wv))
    ]
    rows = [
        pltpu.make_async_copy(e, full.at[pl.ds(i * HALF_ENC, HALF_ENC)], row_sems.at[i])
        for i, e in enumerate((ea, eb))
    ]
    start(sets[0])
    start(rows)
    for one in sets[1:]:
        start(one)
    low[...] = dsecond[...].astype(BF)
    finish(sets[0])
    size = own.held.shape[0] // 10
    places = [[(4 * g + w) * size for g in (0, 1)] for w in range(3)]
    places_o = [8 * size, 9 * size, 3 * size, 7 * size]
    out_grads(core, att, low, wo, grad, places_o, own.held, snd.held)
    finish(rows)

    def queries():
        return (hat1.get()[...] * gain1[...] + shift1[...]).astype(BF)

    enc, mine = cross_part(
        core, 3, grad, att, q, k, v, stats, queries, full, sets[1:], places, own, snd,
        (wq, wk, wv, dq, dk, dv),
    )
    snd.send()
    enc_out[...] = enc
    dfirst[...] = dsecond[...] + mine


def cross_backward_b(
    place, enc_a, dfirst_a, grad, att, q, k, v, stats, hat1, scale1, gain1, shift1, ea, eb,
    vec_a, upb, w0, w1, w2, n1, n2, n3, f1, f2, f3,
    dfirst, enc_own, own, snd, vec,
    wq, wk, wv, dq, dk, dv, full, sems, row_sems,
):
    core = place[0]
    near, far, ws = (n1, n2, n3), (f1, f2, f3), (w0, w1, w2)
    sets = [
        half_weight_copies(w, w, core, ws, near, far, 0, dst, sems)
        for w, dst in enumerate((wq, wk, wv))
    ]
    rows = [
        pltpu.make_async_copy(e, full.at[pl.ds(i * HALF_ENC, HALF_ENC)], row_sems.at[i])
        for i, e in enumerate((ea, eb))
    ]
    start(rows)
    for one in sets:
        start(one)
    finish(rows)
    size = own.held.shape[0] // 6
    places = [[(3 * g + w) * size for g in (0, 1)] for w in range(3)]

    def queries():
        return (hat1.get()[...] * gain1[...] + shift1[...]).astype(BF)

    enc, mine = cross_part(
        core, 0, grad, att, q, k, v, stats, queries, full, sets, places, own, snd,
        (wq, wk, wv, dq, dk, dv),
    )
    enc = enc + enc_a.get()[...]
    enc_own.held[...] = enc[0:HALF_ENC]
    put_rows(snd.held, 6 * size, enc[HALF_ENC:ENC].astype(BF))
    snd.send()
    enc_own.send()
    total = dfirst_a.get()[...] + mine
    hat = hat1.get()[...]
    vec[0:6, :] = vec_a[0:6, :]
    vec[6:7, :] = column(total * hat)
    vec[7:8, :] = column(total)
    dfi = norm_back(total, hat, scale1[:, 0:1], gain1[...])
    dfirst[...] = dfi
    vec[8:9, :] = column(dfi.astype(BF))
    for n in range(4):
        vec[9 + n : 10 + n, :] = upb[:, n * D : (n + 1) * D]
    vec[13:16, :] = jnp.zeros((3, D), F32)


def self_part(core, first, ends, grad, att, q, k, v, stats, full, sets, places, own, snd, scratch):
    wq, wk, wv, dq, dk, dv, bias, sum_k, sum_v = scratch
    for slot in (0, 1):
        bias[slot] = mask_bias(ends, chunk_of(core, slot), ROW)
    q, k, v = q.get(), k.get(), v.get()

    def attend(value):
        def pair(p, carry):
            lanes = pair_lanes(first + p)
            out = pair_lanes(p)
            sum_k[...] = jnp.zeros_like(sum_k)
            sum_v[...] = jnp.zeros_like(sum_v)
            for slot, count in key_counts(value):
                rows = pl.ds(slot * CHUNK, CHUNK)
                width = count * CHUNK
                gq, gk, gv = backward_heads(
                    q[rows, lanes], grad[rows, lanes], att[rows, lanes],
                    k[0:width, lanes], v[0:width, lanes],
                    bias[slot, :, 0:width], stats[rows, :], first + p,
                )
                dq[rows, out] = (gq * 0.125).astype(BF)
                sum_k[0:width, :] += gk
                sum_v[0:width, :] += gv
            dk[:, out] = sum_k[...].astype(BF)
            dv[:, out] = sum_v[...].astype(BF)
            return carry

        lax.fori_loop(0, 3, pair, 0)

    by_core(core, attend)
    queries = jnp.concatenate([full[chunk_rows(core, n), :] for n in (0, 1)], axis=0)
    weight_grads(core, dq, dk, dv, queries, full[...], places, own.held, snd.held)
    own.send()
    for one in sets:
        finish(one)
    sum_all = nn(dk[...], wk[...]) + nn(dv[...], wv[...])
    return sum_all, nn(dq[...], wq[...])


def half_weight_copies(w, slot, core, own, near, far, half, dst, sems):
    copies = []
    rows = pl.ds(w * PIECE, PIECE)
    for n in (0, 1):
        i = 2 * half + n
        if i == 0:
            copies.append(
                pltpu.make_async_copy(own[w], dst.at[pl.ds(0, GROUP)], sems.at[slot, 0])
            )
            continue
        for at, which, refs in ((i, core, near), (3 + i, 1 - core, far)):
            to = pl.multiple_of(GROUP * n + PIECE * which, PIECE)
            copies.append(
                pltpu.make_async_copy(
                    refs[i - 1].at[rows], dst.at[pl.ds(to, PIECE)], sems.at[slot, at]
                )
            )
    return copies


def self_backward_a(
    place, dfirst, att, q, k, v, stats, xa, xb, ya, yb, w0, w1, w2, w3, n1, n2, n3, f1, f2, f3,
    m1, m2, m3, g1, g2, g3,
    sum_out, in_own, grad, own, snd,
    wq, wk, wv, wo, dq, dk, dv, low, bias, sum_k, sum_v, full, lines, sems, row_sems,
):
    core = place[0]
    near, far, ws = (n1, n2, n3), (f1, f2, f3), (w0, w1, w2)
    self_set = (None, None, None, None, w3)
    sets = [weight_copies(4, 3, core, self_set, (m1, m2, m3), (g1, g2, g3), wo, sems)] + [
        half_weight_copies(w, w, core, ws, near, far, 1, dst, sems)
        for w, dst in enumerate((wq, wk, wv))
    ]
    tail = pltpu.make_async_copy(xa.at[pl.ds(CHUNK, 16)], lines, row_sems.at[4])
    rows = row_copies(core, (xa, xb, ya, yb), full, row_sems)
    start(sets[0])
    tail.start()
    start(rows)
    for one in sets[1:]:
        start(one)
    low[...] = dfirst[...].astype(BF)
    finish(sets[0])
    size = own.held.shape[0] // 10
    places = [[(4 * g + w) * size for g in (0, 1)] for w in range(3)]
    places_o = [8 * size, 9 * size, 3 * size, 7 * size]
    out_grads(core, att, low, wo, grad, places_o, own.held, snd.held)
    tail.wait()
    finish(rows)
    sum_all, mine = self_part(
        core, 3, document_ends(lines[...].astype(F32), place), grad, att, q, k, v, stats, full,
        sets[1:], places, own, snd, (wq, wk, wv, dq, dk, dv, bias, sum_k, sum_v),
    )
    snd.send()
    sum_out[...] = sum_all
    in_own[...] = mine + dfirst[...]


def self_backward_b(
    place, grad, sum_a, in_own_a, att, q, k, v, stats, xa, xb, ya, yb,
    w0, w1, w2, n1, n2, n3, f1, f2, f3,
    in_own, own, snd,
    wq, wk, wv, dq, dk, dv, bias, sum_k, sum_v, full, total, lines, sems, row_sems,
):
    core = place[0]
    size = own.held.shape[0] // 6
    places = [[(3 * g + w) * size for g in (0, 1)] for w in range(3)]
    near, far, ws = (n1, n2, n3), (f1, f2, f3), (w0, w1, w2)
    sets = [
        half_weight_copies(w, w, core, ws, near, far, 0, dst, sems)
        for w, dst in enumerate((wq, wk, wv))
    ]
    tail = pltpu.make_async_copy(xa.at[pl.ds(CHUNK, 16)], lines, row_sems.at[4])
    rows = row_copies(core, (xa, xb, ya, yb), full, row_sems)
    tail.start()
    start(rows)
    for one in sets:
        start(one)
    tail.wait()
    finish(rows)
    sum_all, mine = self_part(
        core, 0, document_ends(lines[...].astype(F32), place), grad, att, q, k, v, stats, full,
        sets, places, own, snd, (wq, wk, wv, dq, dk, dv, bias, sum_k, sum_v),
    )
    total[...] = sum_all + sum_a.get()[...]
    mine = mine + in_own_a.get()[...]
    for n in (0, 1):
        in_own[n] = mine[n * CHUNK : (n + 1) * CHUNK] + total[chunk_rows(core, n), :]
        put_rows(snd.held, 6 * size + n * CHUNK, total[chunk_rows(core, 2 + n), :].astype(BF))
    snd.send()


def add_jobs(jobs, ins, store, held, sems):
    copies, at = [], 0
    for _, rows, sources in jobs:
        mine = []
        for operand, row in sources:
            mine.append(
                (
                    pltpu.make_async_copy(
                        ins[operand].at[pl.ds(row, rows)], held.at[pl.ds(at, rows)],
                        sems.at[len(copies) * 8 + len(mine)],
                    ),
                    at,
                )
            )
            at += rows
        copies.append(mine)
    for mine in copies:
        for copy, _ in mine:
            copy.start()
    for (place, rows, _), mine in zip(jobs, copies):
        total = 0.0
        for copy, row in mine:
            copy.wait()
            total = total + held[row : row + rows, :].astype(F32)
        store(place, total)


def job_rows(jobs):
    return sum(rows * len(sources) for _, rows, sources in jobs)


def add_call(name, place, arrays, outs, jobs, pins=()):
    count = len(arrays)

    def kernel(place, *refs):
        ins, targets = refs[:count], refs[count : count + len(outs)]
        held, out_held, sems, out_sems = refs[count + len(outs) :]
        copies = []

        def store(where, total):
            at = sum(outs[: where[0]]) + where[1]
            put_rows(out_held, at, total.astype(BF))
            rows = pl.ds(at, total.shape[0])
            copies.append(
                pltpu.make_async_copy(
                    out_held.at[rows],
                    targets[where[0]].at[pl.ds(where[1], total.shape[0])],
                    out_sems.at[len(copies)],
                )
            )
            copies[-1].start()

        add_jobs(jobs, ins, store, held, sems)
        finish(copies)

    dma = pltpu.SemaphoreType.DMA
    return call(
        kernel, [(place, "s")] + [(one, "a") for one in arrays],
        [((rows, D), BF, "a") for rows in outs],
        [
            pltpu.VMEM((job_rows(jobs), D), BF), pltpu.VMEM((sum(outs), D), BF),
            dma((8 * len(jobs),)), dma((len(jobs),)),
        ],
        name, pins=pins,
    )


def total_call(name, place, arrays, total_rows, jobs, groups, depth, pins=()):
    count = len(arrays)
    size = total_rows // groups // depth

    def kernel(place, *refs):
        mine, parts = refs[count], refs[count + 1 : count + depth]
        held, total, sems = refs[count + depth :]

        def store(row, value):
            put_rows(total, row, value)

        add_jobs(jobs, refs[:count], store, held, sems)
        for d in range(depth):
            for g in range(groups):
                at = pl.multiple_of(
                    g * (total_rows // groups) + (place[2] ^ d) * size, 8
                )
                block = total[pl.ds(at, size), :]
                if d == 0:
                    put_rows(mine, g * size, block)
                else:
                    put_rows(parts[d - 1], g * size, block.astype(BF))

    return call(
        kernel, [(place, "s")] + [(one, "a") for one in arrays],
        [((groups * size, D), F32, "v")] + [((groups * size, D), BF, "v")] * (depth - 1),
        [
            pltpu.VMEM((job_rows(jobs), D), BF), pltpu.VMEM((total_rows, D), F32),
            pltpu.SemaphoreType.DMA((8 * len(jobs),)),
        ],
        name, pins=pins,
    )


def spread(depth, groups):
    def kernel(place, own, other, *refs):
        outs, biases, total = refs[: 4 * groups], refs[4 * groups : -1], refs[-1]
        core, k = place[0], place[2]
        size = own.shape[0] // depth // groups
        for which, ref in enumerate((own, other)):
            for d in range(depth):
                for g in range(groups):
                    at = pl.multiple_of(g * depth * size + (k ^ d) * size, 8)
                    row = (d * groups + g) * size
                    total[which, pl.ds(at, size), :] = ref[row : row + size, :].astype(F32)
        rows = depth * size // 4
        for n, out in enumerate(outs):
            for which, half in ((0, core), (1, 1 - core)):
                to = pl.ds(pl.multiple_of(half * PIECE, PIECE), PIECE)
                out[to, :] = total[which, n * rows : n * rows + PIECE, :]
        for n, bias in enumerate(biases):
            at = (4 * (n // 2) + 2 * (n % 2)) * rows + PIECE
            bias[...] = total[0, at : at + 1, :GROUP]

    return kernel


def solution(mesh):
    names = tuple(mesh.axis_names)
    heads, rows = mesh.shape["heads"], mesh.shape["rows"]
    depth = rows // 2
    piece = FF // (heads * rows)
    weight_rows = PIECE + BIAS_ROWS
    while (4 * weight_rows) % (8 * depth):
        weight_rows += BIAS_ROWS
    def send(value, where, label="moved"):
        pairs = []
        for r in range(rows):
            for h in range(heads):
                to_r, to_h = where(r, h)
                index = {"rows": (r, to_r), "heads": (h, to_h)}
                a = b = 0
                for name in names:
                    a = a * mesh.shape[name] + index[name][0]
                    b = b * mesh.shape[name] + index[name][1]
                pairs.append((a, b))
        with jax.named_scope(label):
            return lax.ppermute(value, names, pairs)

    def swap(r, h):
        return (r & ~1) | (h & 1), (h & ~1) | (r & 1)

    def swap_b(r, h):
        return (r & ~1) | (1 - (h & 1)), (h & ~1) | (r & 1)

    def swap_b_back(r, h):
        return (r & ~1) | (h & 1), (h & ~1) | (1 - (r & 1))

    def core_to(r, h):
        return r ^ 1, h

    def head_to(d):
        return lambda r, h: (r, h ^ d)

    def depth_to(d):
        return lambda r, h: (r ^ (2 * d), h)

    def shards(
        layer_input, encoder_out, doc_lengths,
        self_query, self_qbias, self_key_weight, self_value, self_vbias, self_out, self_obias,
        first_gain, first_shift,
        cross_query, cross_qbias, cross_key, cross_value, cross_vbias, cross_out, cross_obias,
        second_gain, second_shift, up_weight, up_bias, down_weight, down_bias,
        third_gain, third_shift, out_grad,
    ):
        h = lax.axis_index("heads")
        r = lax.axis_index("rows")
        core, k = r % 2, r // 2
        place = jnp.stack([core, h, k]).astype(jnp.int32)

        def line(vector):
            return vector.reshape(1, -1)

        def v(*arrays):
            return [(one, "v") for one in arrays]

        def a(*arrays):
            return [(one, "a") for one in arrays]

        def l(*arrays):
            return [(one, "l") for one in arrays]

        here = [(place, "s")]

        lengths = jnp.concatenate([doc_lengths // 16, doc_lengths % 16], axis=0).astype(BF)
        lengths = jnp.pad(lengths, ((0, 12), (0, 120)))
        self_own = [self_query.T, self_key_weight.T, self_value.T]
        cross_own = [cross_query.T, cross_key.T, cross_value.T, cross_out, self_out]
        xa, xb, mine, mine_cross, ga, gb, _ = call(
            prepare,
            here + v(layer_input, lengths, *self_own, line(self_qbias), line(self_vbias), self_out)
            + v(*cross_own[:4], line(cross_qbias), line(cross_vbias), out_grad),
            [
                ((CHUNK + 16, D), BF, "v"), ((CHUNK, D), BF, "v"),
                ((3 * PIECE + 16, D), BF, "v"), ((5 * PIECE + 16, D), BF, "v"),
                ((CHUNK, D), BF, "v"), ((CHUNK, D), BF, "v"),
            ],
            [], "prepare",
        )

        def gather_groups(mine, label):
            x, y = send(mine, head_to(1), label), send(mine, head_to(2), label)
            return [x, y, send(x, head_to(2), label + "_2")]

        self_near = gather_groups(mine, "w_self_near")
        xa = send(xa, swap, "x_a")
        xb = send(xb, swap_b, "x_b")
        ya = send(xa, core_to, "y_a")
        yb = send(xb, core_to, "y_b")
        self_far = [send(one, core_to, "w_self_far") for one in self_near]
        self_w = self_near + self_far

        def gated(values, pins, name):
            count = len(values)
            anywhere = pl.BlockSpec(memory_space=pltpu.HBM)
            return pl.pallas_call(
                gate,
                in_specs=[anywhere] * (count + len(pins)),
                out_specs=[anywhere] * count,
                out_shape=[jax.ShapeDtypeStruct(one.shape, one.dtype) for one in values],
                input_output_aliases={n: n for n in range(count)},
                name=name,
            )(*values, *pins)

        mine_cross, enc = gated([mine_cross, encoder_out], self_near + [xa, xb], "gate_near")
        cross_near = gather_groups(mine_cross, "w_cross_near")
        ea = send(enc, swap, "e_a")

        dma = pltpu.SemaphoreType.DMA
        weight = pltpu.VMEM((D, D), BF)
        half_weight = pltpu.VMEM((D // 2, D), BF)
        masks = pltpu.VMEM((2, CHUNK, ROW), F32)
        lines_bf = pltpu.VMEM((4, 16, D), BF)
        row_full = pltpu.VMEM((ROW, D), BF)
        enc_full = pltpu.VMEM((ENC, D), BF)
        tokens = (OWN, D)
        q, kk, vv, att, stats1, zero = call(
            self_forward,
            here + a(xa, xb, ya, yb) + a(*self_own, *self_w) + v(line(self_qbias), line(self_vbias)),
            [
                (tokens, BF, "e"), ((ROW, D), BF, "e"), ((ROW, D), BF, "e"), (tokens, BF, "v"),
                ((OWN, 128), F32, "v"),
            ],
            [weight] * 3 + [row_full, masks, lines_bf, dma((3, 7)), dma((4,)), dma((4,))],
            "self_forward", pins=[mine_cross, enc],
        )
        *cross_near, ea, ga, gb = gated(cross_near + [ea, ga, gb], [zero], "gate_far")
        cross_far = [send(one, core_to, "w_cross_far") for one in cross_near]
        eb = send(ea, core_to, "e_b")
        ga = send(ga, swap, "g_a")
        gb = send(gb, swap_b, "g_b")
        cross_w = cross_near + cross_far
        hat1, scale1, cq, ck, cv, catt, stats2, hat2, zero = call(
            cross_forward,
            here + v(xa, xb, att, line(self_obias), line(first_gain), line(first_shift)) + a(ea, eb)
            + a(*cross_own, *cross_w) + v(line(cross_qbias), line(cross_vbias), line(cross_obias)),
            [
                (tokens, F32, "e"), ((OWN, 128), F32, "v"),
                (tokens, BF, "e"), ((ENC, D), BF, "e"), ((ENC, D), BF, "e"), (tokens, BF, "v"),
                ((OWN, 128), F32, "v"), (tokens, F32, "v"),
            ],
            [weight] * 4 + [
                enc_full, lines_bf, dma((4, 7)), dma((4,)), dma((2,)), weight, dma((1, 7)),
            ],
            "cross_forward",
        )
        chunk = ((CHUNK, D), BF, "v")
        out_a, out_b, dsecond, left, right, vec_a, upb, zero = call(
            feed_forward,
            here + v(hat2, stats2, line(second_gain), line(second_shift)) + a(up_weight)
            + v(line(up_bias)) + a(down_weight)
            + v(line(down_bias), line(third_gain), line(third_shift)) + l(ga, gb),
            [
                chunk, chunk, (tokens, F32, "v"), ((2, OWN, FF), BF, "a"), ((2, OWN, D), BF, "a"),
                ((8, D), F32, "v"), ((1, FF), F32, "v"),
            ],
            [
                pltpu.VMEM((D, FF), BF), pltpu.VMEM((FF, D), BF), pltpu.VMEM((OWN, FF), BF),
                pltpu.VMEM((OWN, FF), F32), pltpu.VMEM(tokens, BF), pltpu.VMEM(tokens, F32),
                pltpu.VMEM(tokens, BF), pltpu.VMEM((OWN, FF), BF), dma((2, FF // FF_STEP)),
                dma((2,)), dma((2,)),
            ],
            "feed_forward",
        )
        def ff_grads(which, pins):
            grads, zero = call(
                ff_weight_grads, [(jnp.concatenate([place, which[None]]), "s")] + a(left, right, pins),
                [((FF, D), BF, "a")],
                [
                    pltpu.VMEM((FF, D), BF), pltpu.VMEM((4, OWN, D), BF), pltpu.VMEM(tokens, BF),
                    dma((9,)),
                ],
                "ff_weight_grads",
            )
            return grads

        half = D // 2

        def ff_row(g, which):
            return g * D + which * half

        def both(row):
            return [(0, row), (1, row)]

        out_a = send(out_a, swap, "out_a")
        out_b = send(out_b, swap_b_back, "out_b")
        ff_snd = ff_grads((1 - core).astype(jnp.int32), zero)
        ff_got = send(ff_snd, core_to, "ff_core")
        ff_own = ff_grads(core.astype(jnp.int32), ff_snd)
        output = jnp.concatenate([out_a, out_b], axis=0)
        ff_x, ff_y, _ = add_call(
            "ff_add_1", place, [ff_own, ff_got], [D, D],
            [
                ((0, 0), half, both(ff_row(1, 0))), ((0, half), half, both(ff_row(3, 0))),
                ((1, 0), half, both(ff_row(2, 1))), ((1, half), half, both(ff_row(3, 1))),
            ],
            pins=[out_a, out_b],
        )
        ff_gx = send(ff_x, head_to(1), "ff_heads")
        ff_gy = send(ff_y, head_to(2), "ff_heads")

        wr = weight_rows
        rows_a = [((10 * wr, D), BF, "e")] * 2
        enc_grads = [pltpu.VMEM((ENC, D // 2), BF)] * 2
        half_tokens = pltpu.VMEM((OWN, D // 2), BF)
        enc_a, dfirst, cgrad, ca_own, ca_snd, zero = call(
            cross_backward_a,
            here + v(dsecond, catt) + l(cq, ck, cv) + v(stats2) + l(hat1)
            + v(line(first_gain), line(first_shift)) + a(ea, eb) + a(*cross_own[:4], *cross_w),
            [((ENC, D), F32, "v"), (tokens, F32, "v"), (tokens, BF, "v")] + rows_a,
            [half_weight] * 3 + [weight, half_tokens] + enc_grads
            + [pltpu.VMEM(tokens, BF), enc_full, dma((4, 7)), dma((2,))],
            "cross_backward_a", pins=[ff_x, ff_y],
        )
        (ca_snd,) = gated([ca_snd], [ff_gx, ff_gy], "gate_ca")
        ca_got = send(ca_snd, core_to, "ca_core")
        ff_x2, ff_y2, _ = add_call(
            "ff_add_2", place, [ff_own, ff_got, ff_gx, ff_gy], [half, half],
            [
                ((0, 0), half, both(ff_row(2, 0)) + [(2, half)]),
                ((1, 0), half, both(ff_row(1, 1)) + [(3, half)]),
            ],
            pins=[zero],
        )
        ff_gx2 = send(ff_x2, head_to(2), "ff_heads_2")
        ff_gy2 = send(ff_y2, head_to(1), "ff_heads_2")
        c_x3, _ = add_call(
            "c_add_1", place, [ca_own, ca_got], [4 * wr], [((0, 0), 4 * wr, both(4 * wr))],
            pins=[ff_x2],
        )
        c_gx3 = send(c_x3, head_to(1), "c_heads")
        dfirst, enc_own, cb_own, cb_snd, vectors, zero = call(
            cross_backward_b,
            here + l(enc_a, dfirst) + v(cgrad, catt) + l(cq, ck, cv) + v(stats2) + l(hat1)
            + v(scale1, line(first_gain), line(first_shift)) + a(ea, eb) + v(vec_a, upb)
            + a(*cross_own[:3], *cross_w),
            [
                (tokens, F32, "v"), ((HALF_ENC, D), F32, "e"),
                ((6 * wr, D), BF, "e"), ((6 * wr + HALF_ENC, D), BF, "e"), ((16, D), F32, "v"),
            ],
            [half_weight] * 3 + [half_tokens] + enc_grads + [enc_full, dma((4, 7)), dma((2,))],
            "cross_backward_b", pins=[ff_x2, ff_y2, c_x3],
        )
        vectors = lax.all_gather(vectors, names)
        (cb_snd,) = gated([cb_snd], [ff_gx2, ff_gy2, c_gx3], "gate_cb")
        cb_got = send(cb_snd, core_to, "cb_core")

        def depth_send(parts, label):
            return [send(one, depth_to(d + 1), label) for d, one in enumerate(parts)]

        ff_mine, *ff_parts, _ = total_call(
            "ff_add_3", place, [ff_own, ff_got, ff_gx, ff_gy, ff_gx2, ff_gy2], D,
            [
                (0, half, both(ff_row(0, 0)) + [(2, 0), (4, 0)]),
                (half, half, both(ff_row(0, 1)) + [(3, 0), (5, 0)]),
            ],
            1, depth, pins=[zero],
        )
        ff_back = depth_send(ff_parts, "ff_depth")
        c_y2, c_x1, _ = add_call(
            "c_add_2", place, [ca_own, ca_got, cb_own, cb_got, c_gx3], [4 * wr, 4 * wr],
            [
                ((0, 0), 4 * wr, both(0) + [(4, 0)]),
                ((1, 0), 3 * wr, [(2, 3 * wr), (3, 3 * wr)]), ((1, 3 * wr), wr, both(9 * wr)),
            ],
            pins=[ff_parts[0]],
        )
        c_gy2 = send(c_y2, head_to(2), "c_heads_2")
        c_gx1 = send(c_x1, head_to(1), "c_heads_2")

        row_grads = [pltpu.VMEM((ROW, D // 2), BF)] * 2
        sums = [pltpu.VMEM((ROW, PAIR), F32)] * 2
        sum_a, in_own, sgrad, sa_own, sa_snd, zero = call(
            self_backward_a,
            here + v(dfirst, att) + l(q, kk, vv) + v(stats1) + a(xa, xb, ya, yb)
            + a(*self_own, self_out, *self_w, *cross_w),
            [((ROW, D), F32, "v"), (tokens, F32, "v"), (tokens, BF, "v")] + rows_a,
            [half_weight] * 3 + [weight, half_tokens] + row_grads
            + [pltpu.VMEM(tokens, BF), masks] + sums
            + [row_full, pltpu.VMEM((16, D), BF), dma((4, 7)), dma((5,))],
            "self_backward_a", pins=[*ff_parts, c_y2, c_x1],
        )
        (sa_snd,) = gated([sa_snd], [*ff_back, c_gy2, c_gx1], "gate_sa")
        sa_got = send(sa_snd, core_to, "sa_core")
        c_mine, *c_parts, _ = total_call(
            "c_add_3", place, [ca_own, ca_got, cb_own, cb_got, c_gy2, c_gx1], 4 * wr,
            [
                (0, 3 * wr, [(2, 0), (3, 0), (4, 0), (5, 0)]),
                (3 * wr, wr, [(0, 8 * wr), (1, 8 * wr), (4, 3 * wr), (5, 3 * wr)]),
            ],
            1, depth, pins=[zero],
        )
        c_depth = depth_send(c_parts, "c_depth")
        enc_sum = after((enc_own + cb_got[6 * wr :].astype(F32)).astype(BF), zero)
        encoder_g = send(enc_sum, swap, "enc_grad")
        (s_y, _) = add_call(
            "s_add_1", place, [sa_own, sa_got], [8 * wr], [((0, 0), 8 * wr, both(0))],
            pins=[c_parts[0]],
        )
        s_gy = send(s_y, head_to(2), "s_heads")
        in_own, sb_own, sb_snd, zero = call(
            self_backward_b,
            here + v(sgrad) + l(sum_a, in_own) + v(att) + l(q, kk, vv) + v(stats1)
            + a(xa, xb, ya, yb) + a(*self_own, *self_w),
            [
                ((2, CHUNK, D), F32, "v"), ((6 * wr, D), BF, "e"),
                ((6 * wr + 2 * CHUNK, D), BF, "e"),
            ],
            [half_weight] * 3 + [half_tokens] + row_grads + [masks] + sums
            + [row_full, pltpu.VMEM((ROW, D), F32), pltpu.VMEM((16, D), BF), dma((3, 7)), dma((5,))],
            "self_backward_b", pins=[*c_parts, s_y, enc_sum],
        )
        (sb_snd,) = gated([sb_snd], [*c_depth, s_gy, encoder_g], "gate_sb")
        sb_got = send(sb_snd, core_to, "sb_core")

        def depth_sum(mine, got):
            for one in got:
                mine = mine + one.astype(F32)
            return mine

        c_part = after(depth_sum(c_mine, c_depth), zero).astype(BF)
        c_back = [send(c_part, depth_to(d), "c_back") for d in range(1, depth)]
        s_x, _ = add_call(
            "s_add_2", place, [sa_own, sa_got, sb_own, sb_got, s_gy], [4 * wr],
            [
                ((0, 0), 3 * wr, [(2, 3 * wr), (3, 3 * wr), (4, 4 * wr)]),
                ((0, 3 * wr), wr, both(9 * wr) + [(4, 7 * wr)]),
            ],
            pins=[c_part],
        )
        s_gx = send(s_x, head_to(1), "s_heads_2")
        in_sum = (in_own + sb_got[6 * wr :].reshape(2, CHUNK, D).astype(F32)).astype(BF)
        in_a = send(in_sum[0], swap, "in_a")
        in_b = send(in_sum[1], swap_b_back, "in_b")
        s_mine, *s_parts, _ = total_call(
            "s_add_3", place, [sa_own, sa_got, sb_own, sb_got, s_gy, s_gx], 4 * wr,
            [
                (0, 3 * wr, [(2, 0), (3, 0), (4, 0), (5, 0)]),
                (3 * wr, wr, [(0, 8 * wr), (1, 8 * wr), (4, 3 * wr), (5, 3 * wr)]),
            ],
            1, depth, pins=c_back,
        )
        s_depth = depth_send(s_parts, "s_depth")

        def whole_grads(part, back, label):
            own = jnp.concatenate([part] + back, axis=0)
            other = send(own, core_to, label + "_far")
            *grads, qbias, vbias, _ = call(
                spread(depth, 1), here + v(own, other),
                [((GROUP, D), F32, "v")] * 4 + [((1, GROUP), F32, "v")] * 2,
                [pltpu.VMEM((2, 4 * wr, D), F32)], label + "_spread",
            )
            return grads, qbias[0], vbias[0]

        (cq_g, ck_g, cv_g, co_g), cqb, cvb = whole_grads(c_part, c_back, "c")
        (s_part,) = gated([depth_sum(s_mine, s_depth).astype(BF)], [in_a, in_b, cq_g], "gate_back")
        s_back = [send(s_part, depth_to(d), "s_back") for d in range(1, depth)]
        (sq_g, sk_g, sv_g, so_g), sqb, svb = whole_grads(s_part, s_back, "s")
        input_g = jnp.concatenate([in_a, in_b], axis=0)

        ff = depth_sum(ff_mine, ff_back).reshape(2, piece, D)
        ff_here = lax.dynamic_index_in_dim(ff, core, 0, keepdims=False)
        ff_there = send(lax.dynamic_index_in_dim(ff, 1 - core, 0, keepdims=False), core_to, "ff_last")
        upweight_g = jnp.where(core == 0, ff_here, ff_there).T
        downweight_g = jnp.where(core == 0, ff_there, ff_here)

        vectors = jnp.sum(vectors, axis=0)
        ff_at = (h * rows + r) * piece
        upbias_g = lax.dynamic_slice_in_dim(vectors[9:13].reshape(FF), ff_at, piece)
        return (
            output, input_g, encoder_g,
            sq_g.T, sqb, sk_g.T, sv_g.T, svb, so_g, vectors[8], vectors[6], vectors[7],
            cq_g.T, cqb, ck_g.T, cv_g.T, cvb, co_g, vectors[5],
            vectors[3], vectors[4], upweight_g, upbias_g, downweight_g, vectors[2],
            vectors[0], vectors[1],
        )

    rowed, headed = P(("rows", "heads"), None), P(None, "heads")
    by_head, by_head_rows, whole = P("heads"), P("heads", None), P()
    ffed = ("heads", "rows")
    return jax.shard_map(
        shards,
        mesh=mesh,
        in_specs=(
            rowed, rowed, P("rows", None),
            headed, by_head, headed, headed, by_head, by_head_rows, whole, whole, whole,
            headed, by_head, headed, headed, by_head, by_head_rows, whole, whole, whole,
            whole, whole, whole, whole, whole, whole, rowed,
        ),
        out_specs=(
            rowed, rowed, rowed,
            headed, by_head, headed, headed, by_head, by_head_rows, whole, whole, whole,
            headed, by_head, headed, headed, by_head, by_head_rows, whole, whole, whole,
            P(None, ffed), P(ffed), P(ffed, None), whole, whole, whole,
        ),
        check_vma=False,
    )
```

time: 531 us -> 456 us (0.86)
  other arithmetic: 71.5 us -> 16.7 us
  waiting for transfers between devices: 121 us -> 71.5 us
  Pallas kernels: 204 us -> 246 us
  starting transfers between devices: 75.1 us -> 65.1 us
    ppermute x63 -> x57, waiting for transfers between devices: 121 us -> 71.5 us  [send(): return lax.ppermute(value, names, pairs)]
    pallas_call x9 -> x28, Pallas kernels: 204 us -> 246 us  [the longest x21 246 us: call(): pl.pallas_call(body, in_specs=[specs[kind] for _, kind in ins] + [anywher...]
    add x24 -> x1, other arithmetic: 28.9 us -> 1.97 us  [after(): return value + zero[0, 0].astype(value.dtype)]
    add x12 -> x1, other arithmetic: 12.4 us -> 1.3 us  [depth_sum(): mine = mine + one.astype(F32)]
    ppermute x63 -> x57, starting transfers between devices: 75.1 us -> 65 us  [send(): return lax.ppermute(value, names, pairs)]
    another operation x13 -> x3, other arithmetic: 7.8 us -> 1.27 us
    unnamed x165 -> x168, local copies, waits for them, and re-layouts: 17.8 us -> 24.3 us
    convert_element_type x15 -> x3, other arithmetic: 10.1 us -> 3.97 us  [the longest x1 1.94 us: shards(): depth_sum(s_mine, s_depth).astype(BF)]
  transfers between devices with their start and end apart: 64 -> 58, of which waited for: 21 -> 17; matrix products, arithmetic and copies ran while one was open for 17% -> 5% of each run, Pallas kernels for 31% -> 42%
where the time goes in v2:
time: 456 us; the launch traced here: 447 us
  Pallas kernels  246 us (54%)
  waiting for transfers between devices  71.5 us (16%)
  starting transfers between devices  65.1 us (14%)
  local copies, waits for them, and re-layouts  32.8 us (7%)
  other arithmetic  16.7 us (4%)
  between operations  15.4 us (3%)
    pallas_call x21, Pallas kernels, call(): pl.pallas_call(body, in_specs=[specs[kind] for _, kind in ins] + [anywher...  246 us
    ppermute x57, waiting for transfers between devices, send(): return lax.ppermute(value, names, pairs)  71.5 us
    ppermute x57, starting transfers between devices, send(): return lax.ppermute(value, names, pairs)  65 us
    unnamed x168, local copies, waits for them, and re-layouts  24.3 us
  transfers between devices with their start and end apart: 58, of which 17 were waited for; matrix products, arithmetic and copies ran while one was open for 5% of the time, Pallas kernels for 42%

profile of v2, /device:TPU:9, one launch (start us, length us, event | category | flops | bytes accessed | tf_op | source)
XLA Modules:
  0.0 447.4 jit_solution(17043846218108481723)
XLA Ops:
  7.2 2.1 copy.83.refs_1_
  11.2 3.8 prepare.1
  17.5 9.3 %collective-permute-done.4.refs_2_.refs_8_.refs_15_.refs_16_ = bf16[304,768]{1,0:T(8,128)(2,1)S(1)} collective-permute-done((bf16[304,768]{1,0:T(8,128)(2,1)}, bf16[304,768]{1,0:T(8,128)(2,1)S(1)}, u32[]{:S(2)}, u32[]{:S(2)}) %collective-permute-start.4) | collective-permute-done | bytes 466976 | tf_op jit(solution)/shard_map/w_self_near/ppermute | solution.py:985
  28.1 4.8 %collective-permute-start = (bf16[288,768]{1,0:T(8,128)(2,1)}, bf16[288,768]{1,0:T(8,128)(2,1)S(1)}, u32[]{:S(2)}, u32[]{:S(2)}) collective-permute-start(bf16[288,768]{1,0:T(8,128)(2,1)} %get-tuple-element.120), channel_id=1, source_target_pairs={{0,0},{8,1},{16,16},{24,17},{1,8},{9,9},{17,24},{25,25},{2,2},{10,... | collective-permute-start | bytes 1327112 | tf_op jit(solution)/shard_map/x_a/ppermute | solution.py:985
  32.9 10.0 %collective-permute-done.1.refs_6_.refs_2_.refs_8_.refs_10_ = bf16[272,768]{1,0:T(8,128)(2,1)S(1)} collective-permute-done((bf16[272,768]{1,0:T(8,128)(2,1)}, bf16[272,768]{1,0:T(8,128)(2,1)S(1)}, u32[]{:S(2)}, u32[]{:S(2)}) %collective-permute-start.1) | collective-permute-done | bytes 417824 | tf_op jit(solution)/shard_map/x_b/ppermute | solution.py:985
  46.5 3.1 collective-permute-start.13
  49.8 13.0 %collective-permute-done.10.refs_0_ = bf16[496,768]{1,0:T(8,128)(2,1)S(1)} collective-permute-done((bf16[496,768]{1,0:T(8,128)(2,1)}, bf16[496,768]{1,0:T(8,128)(2,1)S(1)}, u32[]{:S(2)}, u32[]{:S(2)}) %collective-permute-start.10) | collective-permute-done | bytes 761888 | tf_op jit(solution)/shard_map/w_cross_near/ppermute | solution.py:985
  67.9 20.4 %self_forward.1 = (bf16[544,768]{1,0:T(8,128)(2,1)}, bf16[1088,768]{1,0:T(8,128)(2,1)}, bf16[1088,768]{1,0:T(8,128)(2,1)}, bf16[544,768]{1,0:T(8,128)(2,1)}, f32[544,128]{1,0:T(8,128)}, /*index=5*/f32[8,128]{1,0:T(8,128)}) custom-call(s32[3]{0:T(128)} %pad_add_fusion.refs_0_, bf16[288,768]{1,0:T(8,128)(2,1)} %copy-done.12, bf16[272,768]{1,0:T(8,128)(2,1)} %copy-done.16, ...), custom_call_target="tpu_custom_call" | custom-call | flops 1000 | bytes 1000 | tf_op jit(solution)/shard_map/self_forward/pallas_call | solution.py:141
  90.2 2.4 collective-permute-start.15
  93.2 3.6 collective-permute-start.18
  104.0 27.1 %cross_forward.1 = (f32[544,768]{1,0:T(8,128)}, f32[544,128]{1,0:T(8,128)}, bf16[544,768]{1,0:T(8,128)(2,1)}, bf16[1024,768]{1,0:T(8,128)(2,1)}, bf16[1024,768]{...) custom-call(s32[3]{0:T(128)} %pad_add_fusion.refs_0_, ...), custom_call_target="tpu_custom_call" | custom-call | flops 1000 | bytes 1000 | tf_op jit(solution)/shard_map/cross_forward/pallas_call | solution.py:141
  132.1 26.1 %feed_forward.1 = (bf16[272,768]{1,0:T(8,128)(2,1)}, bf16[272,768]{1,0:T(8,128)(2,1)}, f32[544,768]{1,0:T(8,128)}, bf16[2,544,3072]{2,1,0:T(8,128)(2,1)}, bf16[2...) custom-call(s32[3]{0:T(128)} %pad_add_fusion.refs_0_, ...), custom_call_target="tpu_custom_call" | custom-call | flops 1000 | bytes 1000 | tf_op jit(solution)/shard_map/feed_forward/pallas_call | solution.py:141
  158.2 9.4 %ff_weight_grads.2 = (bf16[3072,768]{1,0:T(8,128)(2,1)}, f32[8,128]{1,0:T(8,128)}) custom-call(s32[4]{0:T(128)} %get-tuple-element.222.refs_0_, bf16[2,544,3072]{2,1,0:T(8,128)(2,1)} %get-tuple-element.146.refs_1_, bf16[2,544,768]{2,1,0:T(8,128)(2,1)} %get-tuple-element.147.refs_2_, f32[8,128]{1,0:T(8,128)} %get-tuple-element.148.refs_3_), custom_call_target="tpu_custom_call" | custom-call | flops 1000 | bytes 1000 | tf_op jit(solution)/shard_map/ff_weight_grads/pallas_call | solution.py:141
  168.1 2.9 collective-permute-start.20
  171.6 9.4 %ff_weight_grads.3 = (bf16[3072,768]{1,0:T(8,128)(2,1)}, f32[8,128]{1,0:T(8,128)}) custom-call(s32[4]{0:T(128)} %pad_add_fusion.1.refs_0_, bf16[2,544,3072]{2,1,0:T(8,128)(2,1)} %get-tuple-element.146.refs_1_, bf16[2,544,768]{2,1,0:T(8,128)(2,1)} %get-tuple-element.147.refs_2_, bf16[3072,768]{1,0:T(8,128)(2,1)} %get-tuple-element.149.refs_3_), custom_call_target="tpu_custom_call" | custom-call | flops 1000 | bytes 1000 | tf_op jit(solution)/shard_map/ff_weight_grads/pallas_call | solution.py:141
  184.4 5.0 %ff_add_1.1 = (bf16[768,768]{1,0:T(8,128)(2,1)}, bf16[768,768]{1,0:T(8,128)(2,1)}, f32[8,128]{1,0:T(8,128)}) custom-call(s32[3]{0:T(128)} %pad_add_fusion.refs_0_, bf16[3072,768]{1,0:T(8,128)(2,1)} %get-tuple-element.150.refs_1_, bf16[3072,768]{1,0:T(8,128)(2,1)} %copy-done, bf16[272,768]{1,0:T(8,128)(2,1)} %copy-done.36, bf16[272,768]{1,0:T(8,128)(2,1)} %copy-done.38), custom_call_target="tpu_custom_call" | custom-call | flops 1000 | bytes 1000 | tf_op jit(solution)/shard_map/ff_add_1/pallas_call | solution.py:141
  191.2 24.8 %cross_backward_a.1 = (f32[1024,768]{1,0:T(8,128)}, f32[544,768]{1,0:T(8,128)}, bf16[544,768]{1,0:T(8,128)(2,1)}, bf16[1120,768]{1,0:T(8,128)(2,1)}, bf16[1120,768]{1,0:T(8,128)(2,1)}, /*index=5*/f32[8,128]{1,0:T(8,128)}) custom-call(s32[3]{0:T(128)} %pad_add_fusion.refs_0_, f32[544,768]{1,0:T(8,128)} %get-tuple-element.140.refs_1_, ...), custom_call_target="tpu_custom_call" | custom-call | flops 1000 | bytes 1000 | tf_op jit(solution)/shard_map/cross_backward_a/pallas_call | solution.py:141
  219.7 4.3 ff_add_2.1
  225.2 3.7 c_add_1.1
  231.7 26.4 %cross_backward_b.1 = (f32[544,768]{1,0:T(8,128)}, f32[512,768]{1,0:T(8,128)}, bf16[672,768]{1,0:T(8,128)(2,1)}, bf16[1184,768]{1,0:T(8,128)(2,1)}, f32[16,768]{1,0:T(8,128)}, /*index=5*/f32[8,128]{1,0:T(8,128)}) custom-call(s32[3]{0:T(128)} %pad_add_fusion.refs_0_, f32[1024,768]{1,0:T(8,128)} %get-tuple-element.153.refs_1_, ...), custom_call_target="tpu_custom_call" | custom-call | flops 1000 | bytes 1000 | tf_op jit(solution)/shard_map/cross_backward_b/pallas_call | solution.py:141
  260.7 4.4 ff_add_3.1
  266.4 4.4 c_add_2.1
  273.2 2.3 collective-permute-start.33
  275.7 26.8 %self_backward_a.1 = (f32[1088,768]{1,0:T(8,128)}, f32[544,768]{1,0:T(8,128)}, bf16[544,768]{1,0:T(8,128)(2,1)}, bf16[1120,768]{1,0:T(8,128)(2,1)}, bf16[1120,768]{1,0:T(8,128)(2,1)}, /*index=5*/f32[8,128]{1,0:T(8,128)}) custom-call(s32[3]{0:T(128)} %pad_add_fusion.refs_0_, f32[544,768]{1,0:T(8,128)} %get-tuple-element.165.refs_1_, ...), custom_call_target="tpu_custom_call" | custom-call | flops 1000 | bytes 1000 | tf_op jit(solution)/shard_map/self_backward_a/pallas_call | solution.py:141
  303.9 3.5 c_add_3.1
  308.9 4.5 %s_add_1.1 = (bf16[896,768]{1,0:T(8,128)(2,1)}, f32[8,128]{1,0:T(8,128)}) custom-call(s32[3]{0:T(128)} %pad_add_fusion.refs_0_, bf16[1120,768]{1,0:T(8,128)(2,1)} %get-tuple-element.185.refs_1_, bf16[1120,768]{1,0:T(8,128)(2,1)} %copy-done.5, bf16[112,768]{1,0:T(8,128)(2,1)} %get-tuple-element.182.refs_3_.refs_22_), custom_call_target="tpu_custom_call" | custom-call | flops 1000 | bytes 1000 | tf_op jit(solution)/shard_map/s_add_1/pallas_call | solution.py:141
  314.3 2.0 fusion.1.refs_26_
  316.3 2.7 collective-permute-start.40
  320.2 2.2 collective-permute-start.37
  322.7 28.7 %self_backward_b.1 = (f32[2,272,768]{2,1,0:T(8,128)}, bf16[672,768]{1,0:T(8,128)(2,1)}, bf16[1216,768]{1,0:T(8,128)(2,1)}, f32[8,128]{1,0:T(8,128)}) custom-call(s32[3]{0:T(128)} %pad_add_fusion.refs_0_, bf16[544,768]{1,0:T(8,128)(2,1)} %get-tuple-element.178.refs_1_, f32[1088,768]{1,0:T(8,128)} %get-tuple-element.179.refs_2_, ...), custom_call_target="tpu_custom_call" | custom-call | flops 1000 | bytes 1000 | tf_op jit(solution)/shard_map/self_backward_b/pallas_call | solution.py:141
  354.2 1.8 add_convert_fusion.2.refs_6_
  357.3 2.1 collective-permute-start.46
  360.9 3.7 s_add_2.1
  364.8 5.9 %collective-permute-done.46.refs_8_ = bf16[112,768]{1,0:T(8,128)(2,1)S(1)} collective-permute-done((bf16[112,768]{1,0:T(8,128)(2,1)S(1)}, bf16[112,768]{1,0:T(8,128)(2,1)S(1)}, u32[]{:S(2)}, u32[]{:S(2)}) %collective-permute-start.46) | collective-permute-done | bytes 172064 | tf_op jit(solution)/shard_map/c_back/ppermute | solution.py:985
  370.7 4.9 %collective-permute-done.47.refs_9_ = bf16[112,768]{1,0:T(8,128)(2,1)S(1)} collective-permute-done((bf16[112,768]{1,0:T(8,128)(2,1)S(1)}, bf16[112,768]{1,0:T(8,128)(2,1)S(1)}, u32[]{:S(2)}, u32[]{:S(2)}) %collective-permute-start.47) | collective-permute-done | bytes 172064 | tf_op jit(solution)/shard_map/c_back/ppermute | solution.py:985
  378.3 2.5 collective-permute-done.44.refs_6_
  381.7 3.5 s_add_3.1
  386.2 2.1 collective-permute-start.49
  388.6 4.7 %collective-permute-start.42 = (bf16[272,768]{1,0:T(8,128)(2,1)S(1)}, bf16[272,768]{1,0:T(8,128)(2,1)S(1)}, u32[]{:S(2)}, u32[]{:S(2)}) collective-permute-start(bf16[272,768]{1,0:T(8,128)(2,1)S(1)} %get-tuple-element.226), channel_id=1, source_target_pairs={{0,0},{8,1},{16,16},{24,17},{1,8},{9,9},{17,24},{25,25},{2,2},{10,... | collective-permute-start | bytes 1253384 | tf_op jit(solution)/shard_map/in_a/ppermute | solution.py:985
  394.1 3.0 c_spread.1
  397.1 6.8 %collective-permute-done.50 = bf16[112,768]{1,0:T(8,128)(2,1)} collective-permute-done((bf16[112,768]{1,0:T(8,128)(2,1)}, bf16[112,768]{1,0:T(8,128)(2,1)}, u32[]{:S(2)}, u32[]{:S(2)}) %collective-permute-start.50) | collective-permute-done | bytes 172064 | tf_op jit(solution)/shard_map/s_depth/ppermute | solution.py:985
  403.9 1.9 add_convert_fusion.1.refs_0_
  406.7 2.9 collective-permute-start.53
  411.0 3.2 collective-permute-start.56
  414.3 9.6 %collective-permute-done.53 = bf16[112,768]{1,0:T(8,128)(2,1)S(1)} collective-permute-done((bf16[112,768]{1,0:T(8,128)(2,1)}, bf16[112,768]{1,0:T(8,128)(2,1)S(1)}, u32[]{:S(2)}, u32[]{:S(2)}) %collective-permute-start.53) | collective-permute-done | bytes 172064 | tf_op jit(solution)/shard_map/s_back/ppermute | solution.py:985
  423.9 3.7 collective-permute-done.54
  430.0 1.9 bitcast_select_fusion
  436.5 3.0 s_spread.1
  (301 shorter events, 71.7 us)
Async XLA Ops:
  7.2 424.7 %all-gather.3.cloned.1.call-start = ((), (), s32[]{:S(2)}) async-start(), calls=%async_computation | async-start | bytes 1622016 | tf_op jit(solution)/shard_map/all_gather | solution.py:1211
  15.0 11.8 %collective-permute-start.4 = (bf16[304,768]{1,0:T(8,128)(2,1)}, bf16[304,768]{1,0:T(8,128)(2,1)S(1)}, u32[]{:S(2)}, u32[]{:S(2)}) collective-permute-start(bf16[304,768]{1,0:T(8,128)(2,1)} %get-tuple-element.122), channel_id=1, source_target_pairs={{0,8},{8,0},{16,24},{24,16},{1,9},{9,1},{17,25},{25,17},{2,10},{10... | collective-permute-start | bytes 1400840 | tf_op jit(solution)/shard_map/w_self_near/ppermute | solution.py:985
  16.3 26.7 %collective-permute-start.5 = (bf16[304,768]{1,0:T(8,128)(2,1)}, bf16[304,768]{1,0:T(8,128)(2,1)S(1)}, u32[]{:S(2)}, u32[]{:S(2)}) collective-permute-start(bf16[304,768]{1,0:T(8,128)(2,1)} %get-tuple-element.122), channel_id=1, source_target_pairs={{0,16},{8,24},{16,0},{24,8},{1,17},{9,25},{17,1},{25,9},{2,18},{10... | collective-permute-start | bytes 1400840 | tf_op jit(solution)/shard_map/w_self_near/ppermute | solution.py:985
  26.9 16.1 %collective-permute-start.6 = (bf16[304,768]{1,0:T(8,128)(2,1)S(1)}, bf16[304,768]{1,0:T(8,128)(2,1)S(1)}, u32[]{:S(2)}, u32[]{:S(2)}) collective-permute-start(bf16[304,768]{1,0:T(8,128)(2,1)S(1)} %collective-permute-done.4.refs_2_.refs_8_.refs_15_.refs_16_), channel_id=1, source_target_pairs={{0,16},{8,24},{16,0},{24,8},{1,17},{9,25},{17,1},{25,9},{2,18},{10... | collective-permute-start | bytes 1400840 | tf_op jit(solution)/shard_map/w_self_near_2/ppermute | solution.py:985
  28.1 14.9 %collective-permute-start = (bf16[288,768]{1,0:T(8,128)(2,1)}, bf16[288,768]{1,0:T(8,128)(2,1)S(1)}, u32[]{:S(2)}, u32[]{:S(2)}) collective-permute-start(bf16[288,768]{1,0:T(8,128)(2,1)} %get-tuple-element.120), channel_id=1, source_target_pairs={{0,0},{8,1},{16,16},{24,17},{1,8},{9,9},{17,24},{25,25},{2,2},{10,... | collective-permute-start | bytes 1327112 | tf_op jit(solution)/shard_map/x_a/ppermute | solution.py:985
  32.9 10.0 %collective-permute-start.1 = (bf16[272,768]{1,0:T(8,128)(2,1)}, bf16[272,768]{1,0:T(8,128)(2,1)S(1)}, u32[]{:S(2)}, u32[]{:S(2)}) collective-permute-start(bf16[272,768]{1,0:T(8,128)(2,1)} %get-tuple-element.121), channel_id=1, source_target_pairs={{0,1},{8,0},{16,17},{24,16},{1,9},{9,8},{17,25},{25,24},{2,3},{10,... | collective-permute-start | bytes 1253384 | tf_op jit(solution)/shard_map/x_b/ppermute | solution.py:985
  44.1 18.7 %collective-permute-start.10 = (bf16[496,768]{1,0:T(8,128)(2,1)}, bf16[496,768]{1,0:T(8,128)(2,1)S(1)}, u32[]{:S(2)}, u32[]{:S(2)}) collective-permute-start(bf16[496,768]{1,0:T(8,128)(2,1)} %get-tuple-element.124.refs_16_), channel_id=1, source_target_pairs={{0,8},{8,0},{16,24},{24,16},{1,9},{9,1},{17,25},{25,17},{2,10},{10... | collective-permute-start | bytes 2285576 | tf_op jit(solution)/shard_map/w_cross_near/ppermute | solution.py:985
  46.0 18.7 %collective-permute-start.7 = (bf16[304,768]{1,0:T(8,128)(2,1)}, bf16[304,768]{1,0:T(8,128)(2,1)S(1)}, u32[]{:S(2)}, u32[]{:S(2)}) collective-permute-start(bf16[304,768]{1,0:T(8,128)(2,1)} %copy-done.17), channel_id=1, source_target_pairs={{0,1},{8,9},{16,17},{24,25},{1,0},{9,8},{17,16},{25,24},{2,3},{10,... | collective-permute-start | bytes 1400840 | tf_op jit(solution)/shard_map/w_self_far/ppermute | solution.py:985
  46.5 16.6 %collective-permute-start.2 = (bf16[288,768]{1,0:T(8,128)(2,1)}, bf16[288,768]{1,0:T(8,128)(2,1)S(1)}, u32[]{:S(2)}, u32[]{:S(2)}) collective-permute-start(bf16[288,768]{1,0:T(8,128)(2,1)} %copy-done.12), channel_id=1, source_target_pairs={{0,1},{8,9},{16,17},{24,25},{1,0},{9,8},{17,16},{25,24},{2,3},{10,... | collective-permute-start | bytes 1327112 | tf_op jit(solution)/shard_map/y_a/ppermute | solution.py:985
  46.5 41.9 %collective-permute-start.13 = (bf16[512,768]{1,0:T(8,128)(2,1)}, bf16[512,768]{1,0:T(8,128)(2,1)S(1)}, u32[]{:S(2)}, u32[]{:S(2)}) collective-permute-start(bf16[512,768]{1,0:T(8,128)(2,1)} %get-tuple-element.125.refs_17_), channel_id=1, source_target_pairs={{0,0},{8,1},{16,16},{24,17},{1,8},{9,9},{17,24},{25,25},{2,2},{10,... | collective-permute-start | bytes 2359304 | tf_op jit(solution)/shard_map/e_a/ppermute | solution.py:985
  49.5 38.8 %collective-permute-start.11 = (bf16[496,768]{1,0:T(8,128)(2,1)}, bf16[496,768]{1,0:T(8,128)(2,1)S(1)}, u32[]{:S(2)}, u32[]{:S(2)}) collective-permute-start(bf16[496,768]{1,0:T(8,128)(2,1)} %get-tuple-element.124.refs_16_), channel_id=1, source_target_pairs={{0,16},{8,24},{16,0},{24,8},{1,17},{9,25},{17,1},{25,9},{2,18},{10... | collective-permute-start | bytes 2285576 | tf_op jit(solution)/shard_map/w_cross_near/ppermute | solution.py:985
  62.8 25.6 %collective-permute-start.12 = (bf16[496,768]{1,0:T(8,128)(2,1)S(1)}, bf16[496,768]{1,0:T(8,128)(2,1)S(1)}, u32[]{:S(2)}, u32[]{:S(2)}) collective-permute-start(bf16[496,768]{1,0:T(8,128)(2,1)S(1)} %collective-permute-done.10.refs_0_), channel_id=1, source_target_pairs={{0,16},{8,24},{16,0},{24,8},{1,17},{9,25},{17,1},{25,9},{2,18},{10... | collective-permute-start | bytes 2285576 | tf_op jit(solution)/shard_map/w_cross_near_2/ppermute | solution.py:985
  92.6 10.2 %collective-permute-start.14 = (bf16[512,768]{1,0:T(8,128)(2,1)}, bf16[512,768]{1,0:T(8,128)(2,1)}, u32[]{:S(2)}, u32[]{:S(2)}) collective-permute-start(bf16[512,768]{1,0:T(8,128)(2,1)} %get-tuple-element.130.refs_7_.refs_10_.refs_13_), channel_id=1, source_target_pairs={{0,1},{8,9},{16,17},{24,25},{1,0},{9,8},{17,16},{25,24},{2,3},{10,... | collective-permute-start | bytes 2359304 | tf_op jit(solution)/shard_map/e_b/ppermute | solution.py:985
  92.7 10.1 %collective-permute-start.16 = (bf16[496,768]{1,0:T(8,128)(2,1)}, bf16[496,768]{1,0:T(8,128)(2,1)S(1)}, u32[]{:S(2)}, u32[]{:S(2)}) collective-permute-start(bf16[496,768]{1,0:T(8,128)(2,1)} %get-tuple-element.132.refs_15_.refs_17_.refs_21_.refs_22_), channel_id=1, source_target_pairs={{0,1},{8,9},{16,17},{24,25},{1,0},{9,8},{17,16},{25,24},{2,3},{10,... | collective-permute-start | bytes 2285576 | tf_op jit(solution)/shard_map/w_cross_far/ppermute | solution.py:985
  93.1 9.7 %collective-permute-start.17 = (bf16[496,768]{1,0:T(8,128)(2,1)}, bf16[496,768]{1,0:T(8,128)(2,1)S(1)}, u32[]{:S(2)}, u32[]{:S(2)}) collective-permute-start(bf16[496,768]{1,0:T(8,128)(2,1)} %get-tuple-element.133.refs_16_.refs_18_.refs_22_.refs_23_), channel_id=1, source_target_pairs={{0,1},{8,9},{16,17},{24,25},{1,0},{9,8},{17,16},{25,24},{2,3},{10,... | collective-permute-start | bytes 2285576 | tf_op jit(solution)/shard_map/w_cross_far/ppermute | solution.py:985
  93.2 37.9 %collective-permute-start.18 = (bf16[272,768]{1,0:T(8,128)(2,1)}, bf16[272,768]{1,0:T(8,128)(2,1)S(1)}, u32[]{:S(2)}, u32[]{:S(2)}) collective-permute-start(bf16[272,768]{1,0:T(8,128)(2,1)} %get-tuple-element.136), channel_id=1, source_target_pairs={{0,0},{8,1},{16,16},{24,17},{1,8},{9,9},{17,24},{25,25},{2,2},{10,... | collective-permute-start | bytes 1253384 | tf_op jit(solution)/shard_map/g_a/ppermute | solution.py:985
  96.9 34.3 %collective-permute-start.19 = (bf16[272,768]{1,0:T(8,128)(2,1)}, bf16[272,768]{1,0:T(8,128)(2,1)S(1)}, u32[]{:S(2)}, u32[]{:S(2)}) collective-permute-start(bf16[272,768]{1,0:T(8,128)(2,1)} %get-tuple-element.137), channel_id=1, source_target_pairs={{0,1},{8,0},{16,17},{24,16},{1,9},{9,8},{17,25},{25,24},{2,3},{10,... | collective-permute-start | bytes 1253384 | tf_op jit(solution)/shard_map/g_b/ppermute | solution.py:985
  167.6 14.5 %collective-permute-start.22 = (bf16[3072,768]{1,0:T(8,128)(2,1)}, bf16[3072,768]{1,0:T(8,128)(2,1)S(1)}, u32[]{:S(2)}, u32[]{:S(2)}) collective-permute-start(bf16[3072,768]{1,0:T(8,128)(2,1)} %get-tuple-element.149.refs_3_), channel_id=1, source_target_pairs={{0,1},{8,9},{16,17},{24,25},{1,0},{9,8},{17,16},{25,24},{2,3},{10,... | collective-permute-start | bytes 14155784 | tf_op jit(solution)/shard_map/ff_core/ppermute | solution.py:985
  168.1 13.7 %collective-permute-start.20 = (bf16[272,768]{1,0:T(8,128)(2,1)}, bf16[272,768]{1,0:T(8,128)(2,1)S(1)}, u32[]{:S(2)}, u32[]{:S(2)}) collective-permute-start(bf16[272,768]{1,0:T(8,128)(2,1)} %get-tuple-element.138), channel_id=1, source_target_pairs={{0,0},{8,1},{16,16},{24,17},{1,8},{9,9},{17,24},{25,25},{2,2},{10,... | collective-permute-start | bytes 1253384 | tf_op jit(solution)/shard_map/out_a/ppermute | solution.py:985
  171.0 11.2 %collective-permute-start.21 = (bf16[272,768]{1,0:T(8,128)(2,1)}, bf16[272,768]{1,0:T(8,128)(2,1)S(1)}, u32[]{:S(2)}, u32[]{:S(2)}) collective-permute-start(bf16[272,768]{1,0:T(8,128)(2,1)} %get-tuple-element.139), channel_id=1, source_target_pairs={{0,8},{8,9},{16,24},{24,25},{1,0},{9,1},{17,16},{25,17},{2,10},{10... | collective-permute-start | bytes 1253384 | tf_op jit(solution)/shard_map/out_b/ppermute | solution.py:985
  189.5 27.2 %collective-permute-start.23 = (bf16[768,768]{1,0:T(8,128)(2,1)}, bf16[768,768]{1,0:T(8,128)(2,1)S(1)}, u32[]{:S(2)}, u32[]{:S(2)}) collective-permute-start(bf16[768,768]{1,0:T(8,128)(2,1)} %get-tuple-element.151.refs_22_), channel_id=1, source_target_pairs={{0,8},{8,0},{16,24},{24,16},{1,9},{9,1},{17,25},{25,17},{2,10},{10... | collective-permute-start | bytes 3538952 | tf_op jit(solution)/shard_map/ff_heads/ppermute | solution.py:985
  190.0 27.3 %collective-permute-start.24 = (bf16[768,768]{1,0:T(8,128)(2,1)}, bf16[768,768]{1,0:T(8,128)(2,1)S(1)}, u32[]{:S(2)}, u32[]{:S(2)}) collective-permute-start(bf16[768,768]{1,0:T(8,128)(2,1)} %get-tuple-element.152.refs_23_), channel_id=1, source_target_pairs={{0,16},{8,24},{16,0},{24,8},{1,17},{9,25},{17,1},{25,9},{2,18},{10... | collective-permute-start | bytes 3538952 | tf_op jit(solution)/shard_map/ff_heads/ppermute | solution.py:985
  228.9 30.0 %collective-permute-start.28 = (bf16[448,768]{1,0:T(8,128)(2,1)}, bf16[448,768]{1,0:T(8,128)(2,1)S(1)}, u32[]{:S(2)}, u32[]{:S(2)}) collective-permute-start(bf16[448,768]{1,0:T(8,128)(2,1)} %get-tuple-element.164.refs_28_), channel_id=1, source_target_pairs={{0,8},{8,0},{16,24},{24,16},{1,9},{9,1},{17,25},{25,17},{2,10},{10... | collective-permute-start | bytes 2064392 | tf_op jit(solution)/shard_map/c_heads/ppermute | solution.py:985
  230.0 28.1 %collective-permute-start.26 = (bf16[384,768]{1,0:T(8,128)(2,1)S(1)}, bf16[384,768]{1,0:T(8,128)(2,1)S(1)}, u32[]{:S(2)}, u32[]{:S(2)}) collective-permute-start(bf16[384,768]{1,0:T(8,128)(2,1)S(1)} %copy-done.35), channel_id=1, source_target_pairs={{0,16},{8,24},{16,0},{24,8},{1,17},{9,25},{17,1},{25,9},{2,18},{10... | collective-permute-start | bytes 1769480 | tf_op jit(solution)/shard_map/ff_heads_2/ppermute | solution.py:985
  231.2 27.7 %collective-permute-start.27 = (bf16[384,768]{1,0:T(8,128)(2,1)S(1)}, bf16[384,768]{1,0:T(8,128)(2,1)S(1)}, u32[]{:S(2)}, u32[]{:S(2)}) collective-permute-start(bf16[384,768]{1,0:T(8,128)(2,1)S(1)} %copy-done.65), channel_id=1, source_target_pairs={{0,8},{8,0},{16,24},{24,16},{1,9},{9,1},{17,25},{25,17},{2,10},{10... | collective-permute-start | bytes 1769480 | tf_op jit(solution)/shard_map/ff_heads_2/ppermute | solution.py:985
  270.8 31.8 %collective-permute-start.30 = (bf16[448,768]{1,0:T(8,128)(2,1)}, bf16[448,768]{1,0:T(8,128)(2,1)S(1)}, u32[]{:S(2)}, u32[]{:S(2)}) collective-permute-start(bf16[448,768]{1,0:T(8,128)(2,1)} %get-tuple-element.176.refs_30_), channel_id=1, source_target_pairs={{0,16},{8,24},{16,0},{24,8},{1,17},{9,25},{17,1},{25,9},{2,18},{10... | collective-permute-start | bytes 2064392 | tf_op jit(solution)/shard_map/c_heads_2/ppermute | solution.py:985
  272.1 30.5 %collective-permute-start.31 = (bf16[448,768]{1,0:T(8,128)(2,1)}, bf16[448,768]{1,0:T(8,128)(2,1)S(1)}, u32[]{:S(2)}, u32[]{:S(2)}) collective-permute-start(bf16[448,768]{1,0:T(8,128)(2,1)} %get-tuple-element.177.refs_31_), channel_id=1, source_target_pairs={{0,8},{8,0},{16,24},{24,16},{1,9},{9,1},{17,25},{25,17},{2,10},{10... | collective-permute-start | bytes 2064392 | tf_op jit(solution)/shard_map/c_heads_2/ppermute | solution.py:985
  273.1 29.5 %collective-permute-start.32 = (bf16[192,768]{1,0:T(8,128)(2,1)S(1)}, bf16[192,768]{1,0:T(8,128)(2,1)S(1)}, u32[]{:S(2)}, u32[]{:S(2)}) collective-permute-start(bf16[192,768]{1,0:T(8,128)(2,1)S(1)} %copy-done.54), channel_id=1, source_target_pairs={{0,2},{8,10},{16,18},{24,26},{1,3},{9,11},{17,19},{25,27},{2,0},{1... | collective-permute-start | bytes 884744 | tf_op jit(solution)/shard_map/ff_depth/ppermute | solution.py:985
  273.2 29.3 %collective-permute-start.33 = (bf16[192,768]{1,0:T(8,128)(2,1)S(1)}, bf16[192,768]{1,0:T(8,128)(2,1)S(1)}, u32[]{:S(2)}, u32[]{:S(2)}) collective-permute-start(bf16[192,768]{1,0:T(8,128)(2,1)S(1)} %copy-done.70), channel_id=1, source_target_pairs={{0,4},{8,12},{16,20},{24,28},{1,5},{9,13},{17,21},{25,29},{2,6},{1... | collective-permute-start | bytes 884744 | tf_op jit(solution)/shard_map/ff_depth/ppermute | solution.py:985
  275.6 27.0 %collective-permute-start.34 = (bf16[192,768]{1,0:T(8,128)(2,1)S(1)}, bf16[192,768]{1,0:T(8,128)(2,1)S(1)}, u32[]{:S(2)}, u32[]{:S(2)}) collective-permute-start(bf16[192,768]{1,0:T(8,128)(2,1)S(1)} %copy-done.69), channel_id=1, source_target_pairs={{0,6},{8,14},{16,22},{24,30},{1,7},{9,15},{17,23},{25,31},{2,4},{1... | collective-permute-start | bytes 884744 | tf_op jit(solution)/shard_map/ff_depth/ppermute | solution.py:985
  313.5 38.0 %collective-permute-start.39 = (bf16[896,768]{1,0:T(8,128)(2,1)}, bf16[896,768]{1,0:T(8,128)(2,1)S(1)}, u32[]{:S(2)}, u32[]{:S(2)}) collective-permute-start(bf16[896,768]{1,0:T(8,128)(2,1)} %get-tuple-element.187.refs_25_), channel_id=1, source_target_pairs={{0,16},{8,24},{16,0},{24,8},{1,17},{9,25},{17,1},{25,9},{2,18},{10... | collective-permute-start | bytes 4128776 | tf_op jit(solution)/shard_map/s_heads/ppermute | solution.py:985
  316.3 35.1 %collective-permute-start.40 = (bf16[512,768]{1,0:T(8,128)(2,1)S(1)}, bf16[512,768]{1,0:T(8,128)(2,1)S(1)}, u32[]{:S(2)}, u32[]{:S(2)}) collective-permute-start(bf16[512,768]{1,0:T(8,128)(2,1)S(1)} %fusion.1.refs_26_), channel_id=1, source_target_pairs={{0,0},{8,1},{16,16},{24,17},{1,8},{9,9},{17,24},{25,25},{2,2},{10,... | collective-permute-start | bytes 2359304 | tf_op jit(solution)/shard_map/enc_grad/ppermute | solution.py:985
  319.1 32.4 %collective-permute-start.36 = (bf16[112,768]{1,0:T(8,128)(2,1)S(1)}, bf16[112,768]{1,0:T(8,128)(2,1)S(1)}, u32[]{:S(2)}, u32[]{:S(2)}) collective-permute-start(bf16[112,768]{1,0:T(8,128)(2,1)S(1)} %copy-done.64), channel_id=1, source_target_pairs={{0,2},{8,10},{16,18},{24,26},{1,3},{9,11},{17,19},{25,27},{2,0},{1... | collective-permute-start | bytes 516104 | tf_op jit(solution)/shard_map/c_depth/ppermute | solution.py:985
  320.2 31.2 %collective-permute-start.37 = (bf16[112,768]{1,0:T(8,128)(2,1)S(1)}, bf16[112,768]{1,0:T(8,128)(2,1)S(1)}, u32[]{:S(2)}, u32[]{:S(2)}) collective-permute-start(bf16[112,768]{1,0:T(8,128)(2,1)S(1)} %copy-done.72), channel_id=1, source_target_pairs={{0,4},{8,12},{16,20},{24,28},{1,5},{9,13},{17,21},{25,29},{2,6},{1... | collective-permute-start | bytes 516104 | tf_op jit(solution)/shard_map/c_depth/ppermute | solution.py:985
  322.4 29.1 %collective-permute-start.38 = (bf16[112,768]{1,0:T(8,128)(2,1)S(1)}, bf16[112,768]{1,0:T(8,128)(2,1)S(1)}, u32[]{:S(2)}, u32[]{:S(2)}) collective-permute-start(bf16[112,768]{1,0:T(8,128)(2,1)S(1)} %copy-done.71), channel_id=1, source_target_pairs={{0,6},{8,14},{16,22},{24,30},{1,7},{9,15},{17,23},{25,31},{2,4},{1... | collective-permute-start | bytes 516104 | tf_op jit(solution)/shard_map/c_depth/ppermute | solution.py:985
  356.1 8.7 %collective-permute-start.45 = (bf16[112,768]{1,0:T(8,128)(2,1)S(1)}, bf16[112,768]{1,0:T(8,128)(2,1)S(1)}, u32[]{:S(2)}, u32[]{:S(2)}) collective-permute-start(bf16[112,768]{1,0:T(8,128)(2,1)S(1)} %add_convert_fusion.2.refs_6_), channel_id=1, source_target_pairs={{0,2},{8,10},{16,18},{24,26},{1,3},{9,11},{17,19},{25,27},{2,0},{1... | collective-permute-start | bytes 516104 | tf_op jit(solution)/shard_map/c_back/ppermute | solution.py:985
  357.3 13.4 %collective-permute-start.46 = (bf16[112,768]{1,0:T(8,128)(2,1)S(1)}, bf16[112,768]{1,0:T(8,128)(2,1)S(1)}, u32[]{:S(2)}, u32[]{:S(2)}) collective-permute-start(bf16[112,768]{1,0:T(8,128)(2,1)S(1)} %add_convert_fusion.2.refs_6_), channel_id=1, source_target_pairs={{0,4},{8,12},{16,20},{24,28},{1,5},{9,13},{17,21},{25,29},{2,6},{1... | collective-permute-start | bytes 516104 | tf_op jit(solution)/shard_map/c_back/ppermute | solution.py:985
  359.4 16.2 %collective-permute-start.47 = (bf16[112,768]{1,0:T(8,128)(2,1)S(1)}, bf16[112,768]{1,0:T(8,128)(2,1)S(1)}, u32[]{:S(2)}, u32[]{:S(2)}) collective-permute-start(bf16[112,768]{1,0:T(8,128)(2,1)S(1)} %add_convert_fusion.2.refs_6_), channel_id=1, source_target_pairs={{0,6},{8,14},{16,22},{24,30},{1,7},{9,15},{17,23},{25,31},{2,4},{1... | collective-permute-start | bytes 516104 | tf_op jit(solution)/shard_map/c_back/ppermute | solution.py:985
  364.7 16.2 %collective-permute-start.44 = (bf16[448,768]{1,0:T(8,128)(2,1)}, bf16[448,768]{1,0:T(8,128)(2,1)S(1)}, u32[]{:S(2)}, u32[]{:S(2)}) collective-permute-start(bf16[448,768]{1,0:T(8,128)(2,1)} %get-tuple-element.194), channel_id=1, source_target_pairs={{0,8},{8,0},{16,24},{24,16},{1,9},{9,1},{17,25},{25,17},{2,10},{10... | collective-permute-start | bytes 2064392 | tf_op jit(solution)/shard_map/s_heads_2/ppermute | solution.py:985
  376.7 16.6 %collective-permute-start.51 = (bf16[448,768]{1,0:T(8,128)(2,1)S(1)}, bf16[448,768]{1,0:T(8,128)(2,1)S(1)}, u32[]{:S(2)}, u32[]{:S(2)}) collective-permute-start(bf16[448,768]{1,0:T(8,128)(2,1)S(1)} %pad_maximum_fusion.2.refs_1_), channel_id=1, source_target_pairs={{0,1},{8,9},{16,17},{24,25},{1,0},{9,8},{17,16},{25,24},{2,3},{10,... | collective-permute-start | bytes 2064392 | tf_op jit(solution)/shard_map/c_far/ppermute | solution.py:985
  385.2 11.9 %collective-permute-start.48 = (bf16[112,768]{1,0:T(8,128)(2,1)}, bf16[112,768]{1,0:T(8,128)(2,1)}, u32[]{:S(2)}, u32[]{:S(2)}) collective-permute-start(bf16[112,768]{1,0:T(8,128)(2,1)} %get-tuple-element.196), channel_id=1, source_target_pairs={{0,2},{8,10},{16,18},{24,26},{1,3},{9,11},{17,19},{25,27},{2,0},{1... | collective-permute-start | bytes 516104 | tf_op jit(solution)/shard_map/s_depth/ppermute | solution.py:985
  386.2 10.9 %collective-permute-start.49 = (bf16[112,768]{1,0:T(8,128)(2,1)}, bf16[112,768]{1,0:T(8,128)(2,1)}, u32[]{:S(2)}, u32[]{:S(2)}) collective-permute-start(bf16[112,768]{1,0:T(8,128)(2,1)} %get-tuple-element.197), channel_id=1, source_target_pairs={{0,4},{8,12},{16,20},{24,28},{1,5},{9,13},{17,21},{25,29},{2,6},{1... | collective-permute-start | bytes 516104 | tf_op jit(solution)/shard_map/s_depth/ppermute | solution.py:985
  388.3 15.6 %collective-permute-start.50 = (bf16[112,768]{1,0:T(8,128)(2,1)}, bf16[112,768]{1,0:T(8,128)(2,1)}, u32[]{:S(2)}, u32[]{:S(2)}) collective-permute-start(bf16[112,768]{1,0:T(8,128)(2,1)} %get-tuple-element.198), channel_id=1, source_target_pairs={{0,6},{8,14},{16,22},{24,30},{1,7},{9,15},{17,23},{25,31},{2,4},{1... | collective-permute-start | bytes 516104 | tf_op jit(solution)/shard_map/s_depth/ppermute | solution.py:985
  388.6 17.3 %collective-permute-start.42 = (bf16[272,768]{1,0:T(8,128)(2,1)S(1)}, bf16[272,768]{1,0:T(8,128)(2,1)S(1)}, u32[]{:S(2)}, u32[]{:S(2)}) collective-permute-start(bf16[272,768]{1,0:T(8,128)(2,1)S(1)} %get-tuple-element.226), channel_id=1, source_target_pairs={{0,0},{8,1},{16,16},{24,17},{1,8},{9,9},{17,24},{25,25},{2,2},{10,... | collective-permute-start | bytes 1253384 | tf_op jit(solution)/shard_map/in_a/ppermute | solution.py:985
  393.3 12.6 %collective-permute-start.43 = (bf16[272,768]{1,0:T(8,128)(2,1)S(1)}, bf16[272,768]{1,0:T(8,128)(2,1)S(1)}, u32[]{:S(2)}, u32[]{:S(2)}) collective-permute-start(bf16[272,768]{1,0:T(8,128)(2,1)S(1)} %get-tuple-element.227), channel_id=1, source_target_pairs={{0,8},{8,9},{16,24},{24,25},{1,0},{9,1},{17,16},{25,17},{2,10},{10... | collective-permute-start | bytes 1253384 | tf_op jit(solution)/shard_map/in_b/ppermute | solution.py:985
  406.7 17.1 %collective-permute-start.53 = (bf16[112,768]{1,0:T(8,128)(2,1)}, bf16[112,768]{1,0:T(8,128)(2,1)S(1)}, u32[]{:S(2)}, u32[]{:S(2)}) collective-permute-start(bf16[112,768]{1,0:T(8,128)(2,1)} %gate_back.1), channel_id=1, source_target_pairs={{0,4},{8,12},{16,20},{24,28},{1,5},{9,13},{17,21},{25,29},{2,6},{1... | collective-permute-start | bytes 516104 | tf_op jit(solution)/shard_map/s_back/ppermute | solution.py:985
  409.7 17.9 %collective-permute-start.54 = (bf16[112,768]{1,0:T(8,128)(2,1)}, bf16[112,768]{1,0:T(8,128)(2,1)S(1)}, u32[]{:S(2)}, u32[]{:S(2)}) collective-permute-start(bf16[112,768]{1,0:T(8,128)(2,1)} %gate_back.1), channel_id=1, source_target_pairs={{0,6},{8,14},{16,22},{24,30},{1,7},{9,15},{17,23},{25,31},{2,4},{1... | collective-permute-start | bytes 516104 | tf_op jit(solution)/shard_map/s_back/ppermute | solution.py:985
  411.0 18.9 %collective-permute-start.56 = (f32[96,768]{1,0:T(8,128)S(1)}, f32[96,768]{1,0:T(8,128)}, u32[]{:S(2)}, u32[]{:S(2)}) collective-permute-start(f32[96,768]{1,0:T(8,128)S(1)} %dynamic-slice_bitcast_fusion), channel_id=1, source_target_pairs={{0,1},{8,9},{16,17},{24,25},{1,0},{9,8},{17,16},{25,24},{2,3},{10,... | collective-permute-start | bytes 884744 | tf_op jit(solution)/shard_map/ff_last/ppermute | solution.py:985
  (94 other events, 493.1 us)
Sparse Core Ops, SparseCore 0:
  353.1 67.9 all-gather.2

commit v3 on v2

v3 whole, which is shorter than its diff:
```python
import jax
import jax.numpy as jnp
from jax import lax
from jax.experimental import pallas as pl
from jax.experimental.pallas import tpu as pltpu
from jax.sharding import PartitionSpec as P

BF = jnp.bfloat16
F32 = jnp.float32
HEAD = 64
PAIR = 128
EPS = 1e-05
ROW = 1088
CHUNK = 272
OWN = 544
ENC = 1024
HALF_ENC = 512
D = 768
GROUP = 192
PIECE = 96
BIAS_ROWS = 16
FF = 3072
MIB = 1 << 20


def nn(a, b):
    return jnp.dot(a, b, preferred_element_type=F32)


def nt(a, b):
    return lax.dot_general(a, b, (((1,), (1,)), ((), ())), preferred_element_type=F32)


def tn(a, b):
    return lax.dot_general(a, b, (((0,), (0,)), ((), ())), preferred_element_type=F32)


def lane_ids(shape):
    return lax.broadcasted_iota(jnp.int32, shape, len(shape) - 1)


def pair_lanes(p):
    return pl.ds(pl.multiple_of(p * PAIR, PAIR), PAIR)


def normalize(total):
    center = total - jnp.mean(total, axis=-1, keepdims=True)
    scale = lax.rsqrt(jnp.mean(center * center, axis=-1, keepdims=True) + EPS)
    return center * scale, scale


def norm_back(grad, hat, scale, gain):
    scaled = grad * gain
    inner = scaled - jnp.mean(scaled, axis=-1, keepdims=True)
    return scale * (inner - hat * jnp.mean(scaled * hat, axis=-1, keepdims=True))


def column(values):
    return jnp.sum(values.astype(F32), axis=0, keepdims=True)


def pick_lane(ref, rows, lane):
    block = ref[rows, :]
    return jnp.sum(jnp.where(lane_ids(block.shape) == lane, block, 0.0), axis=-1, keepdims=True)


def start(copies):
    for one in copies:
        one.start()


def finish(copies):
    for one in copies:
        one.wait()


def by_core(core, body):
    for value in (0, 1):

        @pl.when(core == value)
        def _():
            body(value)


class Row:
    def __init__(self, ref, row):
        self.ref, self.row = ref, row

    def __getitem__(self, _):
        return self.ref[self.row : self.row + 1, :]


class Late:
    def __init__(self, source, held, sem, now):
        self.copy = pltpu.make_async_copy(source, held, sem)
        self.held = held
        self.started = self.waited = False
        if now:
            self.begin()

    def begin(self):
        if not self.started:
            self.copy.start()
            self.started = True

    def get(self):
        self.begin()
        if not self.waited:
            self.copy.wait()
            self.waited = True
        return self.held


class Early:
    def __init__(self, held, target, sem):
        self.copy = pltpu.make_async_copy(held, target, sem)
        self.held = held
        self.sent = False

    def send(self):
        self.copy.start()
        self.sent = True


class Pieces:
    def __init__(self, both, rows, own, snd, sems):
        self.both, self.rows, self.targets, self.sems = both, rows, (own, snd), sems
        self.copies = []

    def send(self, at, count):
        for n in (1, 0):
            self.copies.append(
                pltpu.make_async_copy(
                    self.both.at[pl.ds(n * self.rows + at, count)],
                    self.targets[n].at[pl.ds(at, count)],
                    self.sems.at[len(self.copies)],
                )
            )
            self.copies[-1].start()

    def put(self, core, half, at, block):
        to = jnp.where(core == half, 0, self.rows) + at
        self.both[pl.ds(pl.multiple_of(to, 16), block.shape[0]), :] = block

    def put_both(self, at, block):
        put_rows(self.both, at, block)
        put_rows(self.both, self.rows + at, block)

    def put_own(self, at, block):
        put_rows(self.both, at, block)

    def put_snd(self, at, block):
        put_rows(self.both, self.rows + at, block)


def call(kernel, ins, outs, scratch, name, pins=()):
    vmem, anywhere = pl.BlockSpec(memory_space=pltpu.VMEM), pl.BlockSpec(memory_space=pl.ANY)
    smem = pl.BlockSpec(memory_space=pltpu.SMEM)
    specs = {"v": vmem, "a": anywhere, "l": anywhere, "d": anywhere, "e": anywhere, "p": anywhere}
    specs["s"] = smem
    late = [(n, x) for n, (x, kind) in enumerate(ins) if kind in "ld"]
    early = [(n, out) for n, out in enumerate(outs) if out[2] == "e"]
    pair = [n for n, out in enumerate(outs) if out[2] == "p"]
    first = len(ins)
    last = first + len(pins)
    end = last + len(outs)

    def body(*refs):
        took, gave, rest = list(refs[:first]), list(refs[last:end]), list(refs[end + 1 :])
        own, rest = rest[: len(scratch)], rest[len(scratch) :]
        for n, (at, _) in enumerate(late):
            took[at] = Late(took[at], rest[n], rest[-1].at[n], ins[at][1] == "l")
        rest = rest[len(late) :]
        for n, (at, _) in enumerate(early):
            gave[at] = Early(rest[n], gave[at], rest[-1].at[len(late) + n])
        results, pieces = list(gave), []
        if pair:
            rows = outs[pair[0]][0][0]
            pieces = [Pieces(rest[-3], rows, gave[pair[0]], gave[pair[1]], rest[-2])]
            results[pair[0] : pair[1] + 1] = pieces
        kernel(*took, *results, *own)
        refs[end][...] = jnp.zeros((8, 128), F32)
        for at, _ in late:
            took[at].get()
        for at, _ in early:
            if not gave[at].sent:
                gave[at].send()
        for at, _ in early:
            gave[at].copy.wait()
        for one in pieces:
            finish(one.copies)

    extra = [pltpu.VMEM(x.shape, x.dtype) for _, x in late]
    extra += [pltpu.VMEM(out[0], out[1]) for _, out in early]
    if pair:
        extra += [pltpu.VMEM((2 * outs[pair[0]][0][0], D), BF), pltpu.SemaphoreType.DMA((8,))]
    extra += [pltpu.SemaphoreType.DMA((max(len(late) + len(early), 1),))]
    return pl.pallas_call(
        body,
        in_specs=[specs[kind] for _, kind in ins] + [anywhere] * len(pins),
        out_specs=[specs[out[2]] for out in outs] + [vmem],
        out_shape=[jax.ShapeDtypeStruct(out[0], out[1]) for out in outs]
        + [jax.ShapeDtypeStruct((8, 128), F32)],
        scratch_shapes=list(scratch) + extra,
        compiler_params=pltpu.CompilerParams(vmem_limit_bytes=64 * MIB - 65536),
        cost_estimate=pl.CostEstimate(flops=1000, bytes_accessed=1000, transcendentals=0),
        name=name,
    )(*[x for x, _ in ins], *pins)


def after(value, zero):
    return value + zero[0, 0].astype(value.dtype)


def weight_copies(w, slot, core, own, near, far, dst, sems):
    copies = [pltpu.make_async_copy(own[w], dst.at[pl.ds(0, GROUP)], sems.at[slot, 0])]
    rows = pl.ds(w * PIECE, PIECE)
    for i in (1, 2, 3):
        for at, which, refs in ((i, core, near), (3 + i, 1 - core, far)):
            to = pl.multiple_of(GROUP * i + PIECE * which, PIECE)
            copies.append(
                pltpu.make_async_copy(
                    refs[i - 1].at[rows], dst.at[pl.ds(to, PIECE)], sems.at[slot, at]
                )
            )
    return copies


def bias_copies(near, lines, sems):
    return [
        pltpu.make_async_copy(ref.at[pl.ds(ref.shape[0] - 16, 16)], lines.at[i], sems.at[i])
        for i, ref in enumerate(near)
    ]


def gathered_bias(own_line, lines, which):
    parts = [own_line]
    for i in range(3):
        split = lines[i, 3 * which : 3 * which + 3, :GROUP].astype(F32)
        parts.append(split[0:1] + split[1:2] + split[2:3])
    return jnp.concatenate(parts, axis=1)


def put_rows(target, at, block):
    target[at : at + block.shape[0], :] = block


def store_pieces(core, block, places, pieces):
    for g, at in enumerate(places):
        for half in (0, 1):
            row = g * GROUP + half * PIECE
            pieces.put(core, half, at, block[row : row + PIECE])


def store_bias(row, places, pieces):
    for i, at in enumerate(places):
        one = jnp.concatenate(
            [row[:, i * GROUP : (i + 1) * GROUP], jnp.zeros((1, D - GROUP), F32)], axis=1
        )
        block = jnp.concatenate([one, jnp.zeros((BIAS_ROWS - 1, D), F32)], axis=0).astype(BF)
        pieces.put_both(at + PIECE, block)


def forward_heads(q2, keys, values, bias, row_stats, p):
    lane = lane_ids(q2.shape)
    outs = []
    for t in (0, 1):
        query = jnp.where((lane // HEAD) == t, q2, jnp.zeros_like(q2))
        scores = nt(query, keys)
        if bias is not None:
            scores = scores + bias
        highest = jnp.max(scores, axis=-1, keepdims=True)
        raised = jnp.exp(scores - highest)
        total = jnp.sum(raised, axis=-1, keepdims=True)
        outs.append(nn(raised.astype(BF), values) / total)
        row_stats = jnp.where(
            lane_ids(row_stats.shape) == 2 * p + t, highest + jnp.log(total), row_stats
        )
    return jnp.where((lane // HEAD) == 0, outs[0], outs[1]).astype(BF), row_stats


def backward_heads(q2, g2, o2, keys, values, bias, stats, p):
    count = q2.shape[0]
    first = (lane_ids(q2.shape) // HEAD) == 0
    zero = jnp.zeros_like(q2)

    def stacked(a):
        return jnp.concatenate([jnp.where(first, a, zero), jnp.where(first, zero, a)], axis=0)

    query, grad = stacked(q2), stacked(g2)
    product = g2.astype(F32) * o2.astype(F32)
    inner = jnp.concatenate(
        [
            jnp.sum(jnp.where(first, product, 0.0), axis=-1, keepdims=True),
            jnp.sum(jnp.where(first, 0.0, product), axis=-1, keepdims=True),
        ],
        axis=0,
    )
    lanes = lane_ids(stats.shape)
    lse = jnp.concatenate(
        [
            jnp.sum(jnp.where(lanes == 2 * p + t, stats, 0.0), axis=-1, keepdims=True)
            for t in (0, 1)
        ],
        axis=0,
    )
    scores = nt(query, keys)
    if bias is not None:
        scores = scores + jnp.concatenate([bias, bias], axis=0)
    shares = jnp.exp(scores - lse)
    grad_scores = (shares * (nt(grad, values) - inner)).astype(BF)
    grad_q = nn(grad_scores, keys)
    return (
        jnp.where(first, grad_q[:count], grad_q[count:]),
        tn(grad_scores, query),
        tn(shares.astype(BF), grad),
    )


def document_ends(xa, place):
    pair_at = place[1] // 2
    lengths = jnp.where(
        pair_at == 0,
        xa[0:1, :8] * 16.0 + xa[2:3, :8],
        xa[1:2, :8] * 16.0
        + xa[3:4, :8],
    )
    ends, total = [], 0.0
    for d in range(8):
        total = total + lengths[:, d : d + 1]
        ends.append(total)
    return ends


def mask_bias(ends, chunk, width):
    qpos = chunk * CHUNK + lax.broadcasted_iota(jnp.int32, (CHUNK, 1), 0)
    kpos = lax.broadcasted_iota(jnp.int32, (1, width), 1)
    qat, kat = qpos.astype(F32), kpos.astype(F32)
    qseg = jnp.zeros((CHUNK, 1), F32)
    kseg = jnp.zeros((1, width), F32)
    for end in ends:
        qseg = qseg + jnp.where(qat >= end, 1.0, 0.0)
        kseg = kseg + jnp.where(kat >= end, 1.0, 0.0)
    return jnp.where((qseg == kseg) & (kpos <= qpos), 0.0, -1000000000.0)


def chunk_of(core, which):
    return (2 * core, 3 - 2 * core, 2 - 2 * core, 1 + 2 * core)[which]


def chunk_rows(core, which):
    return pl.ds(pl.multiple_of(chunk_of(core, which) * CHUNK, 16), CHUNK)


def key_counts(core):
    return ((0, 1), (1, 4)) if core == 0 else ((0, 3), (1, 2))


def prepare(
    place, x, lengths, wq, wk, wv, qbias, vbias, so, cwq, cwk, cwv, cwo, cqbias, cvbias, out_grad, enc,
    xa, xb, mine, mine_cross, mine_again, ga, gb, enc_out,
):
    core = place[0]
    enc_out[...] = enc[...]
    ga[...] = out_grad[0:CHUNK, :]
    gb[...] = out_grad[CHUNK:OWN, :]
    xa[0:CHUNK, :] = x[0:CHUNK, :]
    xa[CHUNK : CHUNK + 16, :] = jnp.zeros((16, D), BF)
    xa[CHUNK : CHUNK + 16, 0:128] = lengths[...]
    xb[...] = x[CHUNK:OWN, :]
    prepare_weights(core, (wq, wk, wv), qbias, vbias, mine)
    prepare_weights(core, (cwq, cwk, cwv, cwo, so), cqbias, cvbias, mine_cross)
    mine_again[...] = mine_cross[...]


def prepare_weights(core, weights, qbias, vbias, mine):
    half = pl.ds(pl.multiple_of(core * PIECE, PIECE), PIECE)
    for w, one in enumerate(weights):
        mine[w * PIECE : (w + 1) * PIECE, :] = one[half, :]
    rows = []
    for one in (qbias[...], vbias[...]):
        for _ in range(3):
            top = one.astype(BF).astype(F32)
            rows.append(top)
            one = one - top
    rows = jnp.concatenate(rows + [jnp.zeros((10, GROUP), F32)], axis=0)
    at = len(weights) * PIECE
    mine[at : at + 16, :] = jnp.concatenate(
        [rows, jnp.zeros((16, D - GROUP), F32)], axis=1
    ).astype(BF)


def gate(*refs):
    pass


def row_copies(core, xs, full, sems):
    return [
        pltpu.make_async_copy(
            x.at[pl.ds(0, CHUNK)], full.at[chunk_rows(core, which)], sems.at[which]
        )
        for which, x in enumerate(xs)
    ]


def self_forward(
    place, xa, xb, ya, yb, w0, w1, w2, n1, n2, n3, f1, f2, f3, qbias, vbias,
    q_out, k_out, v_out, att, stats,
    wq, wk, wv, full, bias, lines, sems, line_sems, row_sems,
):
    core = place[0]
    near, far = (n1, n2, n3), (f1, f2, f3)
    sets = [
        weight_copies(w, w, core, (w0, w1, w2), near, far, dst, sems)
        for w, dst in enumerate((wq, wk, wv))
    ]
    held = bias_copies(near, lines, line_sems)
    rows = row_copies(core, (xa, xb, ya, yb), full, row_sems)
    start(rows)
    start(held)
    for one in sets:
        start(one)
    finish(rows[:1])
    tail = pltpu.make_async_copy(xa.at[pl.ds(CHUNK, 16)], lines.at[3], line_sems.at[3])
    tail.start()
    tail.wait()
    ends = document_ends(lines[3].astype(F32), place)
    for slot in (0, 1):
        bias[slot] = mask_bias(ends, chunk_of(core, slot), ROW)
    finish(rows[1:])
    finish(held)
    for one in sets:
        finish(one)
    line = gathered_bias(qbias[...], lines, 0)
    k_out.held[...] = nt(full[...], wk[...]).astype(BF)
    k_out.send()
    for which in (0, 1):
        q_out.held[which * CHUNK : (which + 1) * CHUNK, :] = (
            (nt(full[chunk_rows(core, which), :], wq[...]) + line) * 0.125
        ).astype(BF)
    q_out.send()
    line = gathered_bias(vbias[...], lines, 1)
    v_out.held[...] = (nt(full[...], wv[...]) + line).astype(BF)
    v_out.send()
    q, k, v = q_out.held, k_out.held, v_out.held
    stats[...] = jnp.zeros_like(stats)

    def attend(value):
        def pair(p, carry):
            lanes = pair_lanes(p)
            for slot, count in key_counts(value):
                rows = pl.ds(slot * CHUNK, CHUNK)
                width = count * CHUNK
                out, now = forward_heads(
                    q[rows, lanes], k[0:width, lanes], v[0:width, lanes],
                    bias[slot, :, 0:width], stats[rows, :], p,
                )
                att[rows, lanes] = out
                stats[rows, :] = now
            return carry

        lax.fori_loop(0, 6, pair, 0)

    by_core(core, attend)


def cross_forward(
    place, xa, xb, self_att, params, ea, eb, w0, w1, w2, w3, w4, n1, n2, n3,
    f1, f2, f3, qbias, vbias,
    hat1, scale1, q_out, k_out, v_out, att, stats, hat_out,
    wq, wk, wv, wo, full, lines, sems, line_sems, row_sems, self_wo, self_sems,
):
    core = place[0]
    self_bias, gain1, shift1, obias = (Row(params, n) for n in range(4))
    near, far = (n1, n2, n3), (f1, f2, f3)
    rows = [
        pltpu.make_async_copy(e, full.at[pl.ds(i * HALF_ENC, HALF_ENC)], row_sems.at[i])
        for i, e in enumerate((ea, eb))
    ]
    held = bias_copies(near, lines, line_sems)
    sets = [
        weight_copies(w, w, core, (w0, w1, w2, w3), near, far, dst, sems)
        for w, dst in enumerate((wq, wk, wv, wo))
    ]
    self_set = weight_copies(
        4, 0, core, (None, None, None, None, w4), near, far, self_wo, self_sems
    )
    start(self_set)
    start(held)
    start(sets[0])
    start(rows)
    for one in sets[1:]:
        start(one)
    finish(self_set)
    product = nn(self_att[...], self_wo[...]) + self_bias[...]
    for which, x in enumerate((xa, xb)):
        part = slice(which * CHUNK, (which + 1) * CHUNK)
        hat, scale = normalize(x[0:CHUNK, :].astype(F32) + product[part])
        hat1.held[part, :] = hat
        scale1[part, :] = jnp.broadcast_to(scale, (CHUNK, 128))
    hat1.send()
    hidden = (hat1.held[...] * gain1[...] + shift1[...]).astype(BF)
    finish(held)
    finish(sets[0])
    line = gathered_bias(qbias[...], lines, 0)
    q_out.held[...] = ((nt(hidden, wq[...]) + line) * 0.125).astype(BF)
    q_out.send()
    finish(rows)
    finish(sets[1])
    k_out.held[...] = nt(full[...], wk[...]).astype(BF)
    k_out.send()
    finish(sets[2])
    line = gathered_bias(vbias[...], lines, 1)
    v_out.held[...] = (nt(full[...], wv[...]) + line).astype(BF)
    v_out.send()
    finish(sets[3])
    q, k, v = q_out.held, k_out.held, v_out.held
    stats[...] = jnp.zeros_like(stats)

    def pair(p, carry):
        lanes = pair_lanes(p)
        for slot in (0, 1):
            rows = pl.ds(slot * CHUNK, CHUNK)
            out, now = forward_heads(
                q[rows, lanes], k[:, lanes], v[:, lanes], None, stats[rows, :], p
            )
            att[rows, lanes] = out
            stats[rows, :] = now
        return carry

    lax.fori_loop(0, 6, pair, 0, unroll=True)
    hidden = hat1.held[...] * gain1[...] + shift1[...]
    hat, scale = normalize(hidden + (nn(att[...], wo[...]) + obias[...]))
    hat_out[...] = hat
    stats[...] = jnp.where(lane_ids(stats.shape) == 12, scale, stats[...])


FF_STEP = 512
FF_BLOCK = 768


def gelu_parts(u):
    size = jnp.abs(u)
    t = 1.0 / (1.0 + (0.3275911 * 0.7071067811865476) * size)
    poly = t * (
        0.254829592
        + t * (-0.284496736 + t * (1.421413741 + t * (-1.453152027 + t * 1.061405429)))
    )
    bell = jnp.exp(-0.5 * u * u)
    tail = 0.5 * poly * bell
    phi = jnp.where(u >= 0.0, 1.0 - tail, tail)
    return u * phi, phi + u * bell * 0.3989422804014327


def feed_forward(
    place, hat2, stats, params, up_hbm, up_bias, down_hbm, ga_here, ga, gb,
    out_a, out_b, dsecond, left, right, snd, vec, upb,
    up, down, active, slope, hid, total, third, grads, held, sems, out_sems,
):
    core, group = place[0], place[1]
    gain2, shift2, down_bias, gain3, shift3 = (Row(params, 4 + n) for n in range(5))
    steps = FF // FF_STEP
    ups = [
        pltpu.make_async_copy(
            up_hbm.at[:, pl.ds(i * FF_STEP, FF_STEP)],
            up.at[:, pl.ds(i * FF_STEP, FF_STEP)],
            sems.at[0, i],
        )
        for i in range(steps)
    ]
    downs = [
        pltpu.make_async_copy(
            down_hbm.at[pl.ds(i * FF_STEP, FF_STEP)],
            down.at[pl.ds(i * FF_STEP, FF_STEP)],
            sems.at[1, i],
        )
        for i in range(steps)
    ]
    for i in range(steps):
        ups[i].start()
        downs[i].start()
    second = hat2[...] * gain2[...] + shift2[...]
    hid[...] = second.astype(BF)
    total[...] = second + down_bias[...]
    for i in range(steps):
        cols = pl.ds(i * FF_STEP, FF_STEP)
        ups[i].wait()
        u = nn(hid[...], up[:, cols]) + up_bias[:, cols]
        act, slo = gelu_parts(u)
        active[:, cols] = act.astype(BF)
        slope[:, cols] = slo
        downs[i].wait()
        total[...] += nn(active[:, cols], down[cols, :])
    hat3, scale3 = normalize(total[...])
    out = (hat3 * gain3[...] + shift3[...]).astype(BF)
    out_a[...] = out[0:CHUNK]
    out_b[...] = out[CHUNK:OWN]
    first = jnp.where(core == group % 2, ga_here.get()[...], ga.get()[...])
    grad = jnp.concatenate([first, gb.get()[...]], axis=0).astype(F32)
    vec[0:1, :] = column(grad * hat3)
    vec[1:2, :] = column(grad)
    dthird = norm_back(grad, hat3, scale3, gain3[...])
    total[...] = dthird
    third[...] = dthird.astype(BF)
    vec[2:3, :] = column(third[...])
    for i in range(FF // FF_BLOCK):
        cols = pl.ds(i * FF_BLOCK, FF_BLOCK)
        du = (nt(third[...], down[cols, :]) * slope[:, cols]).astype(BF)
        grads[:, cols] = du
        upb[:, cols] = column(du)
        total[...] += nt(du, up[:, cols])
    grad = total[...]
    hat = hat2[...]
    scale = pick_lane(stats, slice(None), 12)
    vec[3:4, :] = column(grad * hat)
    vec[4:5, :] = column(grad)
    dsec = norm_back(grad, hat, scale, gain2[...])
    dsecond.held[...] = dsec
    dsecond.send()
    vec[5:6, :] = column(dsec.astype(BF))
    vec[6:8, :] = jnp.zeros((2, D), F32)

    def hand_over(value):
        pairs = ((grads, hid), (active, third))
        mine, other = pairs[value], pairs[1 - value]
        copies = [
            pltpu.make_async_copy(mine[0], left, out_sems.at[4]),
            pltpu.make_async_copy(mine[1], right, out_sems.at[5]),
        ]
        start(copies)
        for i in range(4):
            cols = pl.ds(pl.multiple_of((group ^ i) * D, D), D)
            rows = pl.ds(i * D, D)
            held[rows, :] = tn(other[0][:, cols], other[1][...]).astype(BF)
            copies.append(pltpu.make_async_copy(held.at[rows], snd.at[rows], out_sems.at[i]))
            copies[-1].start()
        finish(copies)

    by_core(core, hand_over)


def ff_weight_grads(place, left, right, out, held, left_held, right_held, sems):
    copies = [pltpu.make_async_copy(right, right_held, sems.at[0])]
    for i in range(4):
        cols = pl.ds(pl.multiple_of((place[1] ^ i) * D, D), D)
        copies.append(pltpu.make_async_copy(left.at[:, cols], left_held.at[i], sems.at[1 + i]))
    start(copies[:2])
    finish(copies[:2])
    start(copies[2:])
    outs = []
    for i in range(4):
        if i:
            copies[1 + i].wait()
        rows = pl.ds(i * D, D)
        held[rows, :] = tn(left_held[i], right_held[...]).astype(BF)
        outs.append(pltpu.make_async_copy(held.at[rows], out.at[rows], sems.at[5 + i]))
        outs[i].start()
    finish(outs)


def out_grads(core, att, low, wo, grad, places, pieces):
    store_pieces(core, tn(att[...], low[...]).astype(BF), places, pieces)
    store_bias(jnp.zeros((1, D), F32), places, pieces)
    grad[...] = nt(low[...], wo[...]).astype(BF)


def weight_grads(core, dq, dk, dv, queries, keys, places, pieces):
    store_pieces(core, tn(dq[...], queries).astype(BF), places[0], pieces)
    store_pieces(core, tn(dk[...], keys).astype(BF), places[1], pieces)
    store_pieces(core, tn(dv[...], keys).astype(BF), places[2], pieces)
    store_bias(column(dq[...]), places[0], pieces)
    store_bias(jnp.zeros((1, dk.shape[1]), F32), places[1], pieces)
    store_bias(column(dv[...]), places[2], pieces)


def cross_part(core, first, grad, att, q, k, v, stats, queries, full, places, pieces, dq, dk, dv):

    def pair(p, carry):
        lanes = pair_lanes(first + p)
        out = pair_lanes(p)
        gq, gk, gv = backward_heads(
            q[:, lanes], grad[:, lanes], att[:, lanes], k[:, lanes], v[:, lanes],
            None, stats[...], first + p,
        )
        dq[:, out] = (gq * 0.125).astype(BF)
        dk[:, out] = gk.astype(BF)
        dv[:, out] = gv.astype(BF)
        return carry

    lax.fori_loop(0, 3, pair, 0, unroll=True)
    half = pl.ds(0, D // 2)
    weight_grads(
        core, dq.at[:, half], dk.at[:, half], dv.at[:, half], queries(), full[...], places, pieces
    )


def cross_backward_a(
    place, dsecond, att, q, k, v, stats, hat1, params, ea, eb, w3, n1, n2, n3, f1, f2, f3,
    dq, dk, dv, grad, pieces,
    wo, low, full, sems, row_sems,
):
    core = place[0]
    gain1, shift1 = Row(params, 1), Row(params, 2)
    copies = weight_copies(
        3, 0, core, (None, None, None, w3), (n1, n2, n3), (f1, f2, f3), wo, sems
    )
    rows = [
        pltpu.make_async_copy(e, full.at[pl.ds(i * HALF_ENC, HALF_ENC)], row_sems.at[i])
        for i, e in enumerate((ea, eb))
    ]
    start(copies)
    low[...] = dsecond.get()[...].astype(BF)
    size = pieces.rows // 10
    places = [[(4 * g + w) * size for g in (0, 1)] for w in range(3)]
    places_o = [8 * size, 9 * size, 3 * size, 7 * size]
    att = att.get()
    finish(copies)
    out_grads(core, att, low, wo, grad.held, places_o, pieces)
    grad.send()
    q, k, v, stats = q.get(), k.get(), v.get(), stats.get()
    start(rows)
    hat1.begin()

    def queries():
        for one in (dq, dk, dv):
            one.send()
        finish(rows)
        return (hat1.get()[...] * gain1[...] + shift1[...]).astype(BF)

    cross_part(
        core, 3, grad.held, att, q, k, v, stats, queries, full, places, pieces,
        dq.held, dk.held, dv.held,
    )
    pieces.send(0, 10 * size)


def cross_backward_b(
    place, dq_a, dk_a, dv_a, dsecond, grad, att, q, k, v, stats, hat1, scale1, params, ea, eb,
    vec_a, upb, w0, w1, w2, n1, n2, n3, f1, f2, f3,
    dfirst, pieces, vec,
    wq, wk, wv, dq, dk, dv, full, sems, row_sems,
):
    core = place[0]
    gain1, shift1 = Row(params, 1), Row(params, 2)
    near, far, ws = (n1, n2, n3), (f1, f2, f3), (w0, w1, w2)
    sets = [
        weight_copies(w, w, core, ws, near, far, dst, sems)
        for w, dst in enumerate((wq, wk, wv))
    ]
    rows = [
        pltpu.make_async_copy(e, full.at[pl.ds(i * HALF_ENC, HALF_ENC)], row_sems.at[i])
        for i, e in enumerate((ea, eb))
    ]
    second = pl.ds(D // 2, D // 2)
    parts = [
        pltpu.make_async_copy(one, dst.at[:, second], row_sems.at[2 + n])
        for n, (one, dst) in enumerate(((dq_a, dq), (dk_a, dk), (dv_a, dv)))
    ]
    grad, att, stats = grad.get(), att.get(), stats.get()
    q, k, v = q.get(), k.get(), v.get()
    start(rows)
    hat1.begin()
    for one in sets:
        start(one)
    start(parts)
    dsecond.begin()
    scale1.begin()
    size = (pieces.rows - HALF_ENC) // 6
    places = [[(3 * g + w) * size for g in (0, 1)] for w in range(3)]

    def queries():
        finish(rows)
        return (hat1.get()[...] * gain1[...] + shift1[...]).astype(BF)

    cross_part(
        core, 0, grad, att, q, k, v, stats, queries, full, places, pieces, dq, dk, dv
    )
    pieces.send(0, 6 * size)
    finish(parts)
    for one in sets:
        finish(one)
    enc = nn(dk[...], wk[...]) + nn(dv[...], wv[...])
    pieces.put_own(6 * size, enc[0:HALF_ENC].astype(BF))
    pieces.put_snd(6 * size, enc[HALF_ENC:ENC].astype(BF))
    pieces.send(6 * size, HALF_ENC)
    total = dsecond.get()[...] + nn(dq[...], wq[...])
    hat = hat1.get()[...]
    vec[0:6, :] = vec_a[0:6, :]
    vec[6:7, :] = column(total * hat)
    vec[7:8, :] = column(total)
    dfi = norm_back(total, hat, scale1.get()[:, 0:1], gain1[...])
    dfirst.held[...] = dfi
    dfirst.send()
    vec[8:9, :] = column(dfi.astype(BF))
    for n in range(4):
        vec[9 + n : 10 + n, :] = upb[:, n * D : (n + 1) * D]
    vec[13:16, :] = jnp.zeros((3, D), F32)


def self_part(
    core, first, ends, grad, att, q, k, v, stats, full, places, pieces, dq, dk, dv, bias, rows
):
    for slot in (0, 1):
        bias[slot] = mask_bias(ends, chunk_of(core, slot), ROW)

    def attend(value):
        def pair(p, carry):
            lanes = pair_lanes(first + p)
            out = pair_lanes(p)
            (low_slot, low), (high_slot, high) = sorted(key_counts(value), key=lambda x: x[1])
            parts = {}
            for slot, count in ((low_slot, low), (high_slot, high)):
                rows = pl.ds(slot * CHUNK, CHUNK)
                width = count * CHUNK
                gq, gk, gv = backward_heads(
                    q[rows, lanes], grad[rows, lanes], att[rows, lanes],
                    k[0:width, lanes], v[0:width, lanes],
                    bias[slot, :, 0:width], stats[rows, :], first + p,
                )
                dq[rows, out] = (gq * 0.125).astype(BF)
                parts[slot] = (gk, gv)
            for n, dst in ((0, dk), (1, dv)):
                wide, narrow = parts[high_slot][n], parts[low_slot][n]
                shared, reach = low * CHUNK, high * CHUNK
                dst[0:shared, out] = (wide[0:shared] + narrow).astype(BF)
                dst[shared:reach, out] = wide[shared:reach].astype(BF)
                if reach < ROW:
                    dst[reach:ROW, out] = jnp.zeros((ROW - reach, PAIR), BF)
            return carry

        lax.fori_loop(0, 3, pair, 0)

    by_core(core, attend)
    finish(rows)
    half = pl.ds(0, D // 2)
    queries = jnp.concatenate([full[chunk_rows(core, n), :] for n in (0, 1)], axis=0)
    weight_grads(
        core, dq.at[:, half], dk.at[:, half], dv.at[:, half], queries, full[...], places, pieces
    )


def self_backward_a(
    place, dfirst, att, q, k, v, stats, xa, xb, ya, yb, w3, m1, m2, m3, g1, g2, g3,
    dq, dk, dv, grad, pieces,
    wo, low, bias, full, lines, sems, row_sems,
):
    core = place[0]
    copies = weight_copies(
        4, 0, core, (None, None, None, None, w3), (m1, m2, m3), (g1, g2, g3), wo, sems
    )
    tail = pltpu.make_async_copy(xa.at[pl.ds(CHUNK, 16)], lines, row_sems.at[4])
    rows = row_copies(core, (xa, xb, ya, yb), full, row_sems)
    start(copies)
    tail.start()
    low[...] = dfirst.get()[...].astype(BF)
    size = pieces.rows // 10
    places = [[(4 * g + w) * size for g in (0, 1)] for w in range(3)]
    places_o = [8 * size, 9 * size, 3 * size, 7 * size]
    att = att.get()
    finish(copies)
    out_grads(core, att, low, wo, grad.held, places_o, pieces)
    grad.send()
    tail.wait()
    q, k, v, stats = q.get(), k.get(), v.get(), stats.get()
    start(rows)
    self_part(
        core, 3, document_ends(lines[...].astype(F32), place), grad.held, att, q, k, v, stats, full,
        places, pieces, dq.held, dk.held, dv.held, bias, rows,
    )
    pieces.send(0, 10 * size)
    for one in (dq, dk, dv):
        one.send()


def self_backward_b(
    place, dq_a, dk_a, dv_a, dfirst, grad, att, q, k, v, stats, xa, xb, ya, yb,
    w0, w1, w2, n1, n2, n3, f1, f2, f3,
    pieces,
    wq, wk, wv, dq, dk, dv, bias, full, total, lines, sems, row_sems,
):
    core = place[0]
    size = (pieces.rows - 2 * CHUNK) // 6
    places = [[(3 * g + w) * size for g in (0, 1)] for w in range(3)]
    near, far, ws = (n1, n2, n3), (f1, f2, f3), (w0, w1, w2)
    sets = [
        weight_copies(w, w, core, ws, near, far, dst, sems)
        for w, dst in enumerate((wq, wk, wv))
    ]
    tail = pltpu.make_async_copy(xa.at[pl.ds(CHUNK, 16)], lines, row_sems.at[4])
    rows = row_copies(core, (xa, xb, ya, yb), full, row_sems)
    second = pl.ds(D // 2, D // 2)
    parts = [
        pltpu.make_async_copy(one, dst.at[:, second], row_sems.at[5 + n])
        for n, (one, dst) in enumerate(((dq_a, dq), (dk_a, dk), (dv_a, dv)))
    ]
    tail.start()
    tail.wait()
    grad, att, stats = grad.get(), att.get(), stats.get()
    q, k, v = q.get(), k.get(), v.get()
    start(rows)
    for one in sets:
        start(one)
    start(parts)
    dfirst.begin()
    self_part(
        core, 0, document_ends(lines[...].astype(F32), place), grad, att, q, k, v, stats, full,
        places, pieces, dq, dk, dv, bias, rows,
    )
    pieces.send(0, 6 * size)
    finish(parts)
    for one in sets:
        finish(one)
    total[...] = nn(dk[...], wk[...]) + nn(dv[...], wv[...])
    mine = nn(dq[...], wq[...]) + dfirst.get()[...]
    for n in (0, 1):
        at = 6 * size + n * CHUNK
        pieces.put_snd(at, total[chunk_rows(core, 2 + n), :].astype(BF))
        pieces.put_own(
            at, (mine[n * CHUNK : (n + 1) * CHUNK] + total[chunk_rows(core, n), :]).astype(BF)
        )
    pieces.send(6 * size, 2 * CHUNK)


def add_jobs(jobs, ins, store, held, sems):
    copies, at, most = [], 0, job_most(jobs)
    for _, rows, sources in jobs:
        mine = []
        for operand, row in sources:
            mine.append(
                (
                    pltpu.make_async_copy(
                        ins[operand].at[pl.ds(row, rows)], held.at[pl.ds(at, rows)],
                        sems.at[len(copies) * most + len(mine)],
                    ),
                    at,
                )
            )
            at += rows
        copies.append(mine)
    for mine in copies:
        for copy, _ in mine:
            copy.start()
    for (place, rows, _), mine in zip(jobs, copies):
        total = 0.0
        for copy, row in mine:
            copy.wait()
            total = total + held[row : row + rows, :].astype(F32)
        store(place, total)


def job_most(jobs):
    return max(len(sources) for _, _, sources in jobs)


def job_rows(jobs):
    return sum(rows * len(sources) for _, rows, sources in jobs)


def add_call(name, place, arrays, outs, jobs, pins=()):
    count = len(arrays)

    def kernel(place, *refs):
        ins, targets = refs[:count], refs[count : count + len(outs)]
        held, out_held, sems, out_sems = refs[count + len(outs) :]
        copies = []

        def store(where, total):
            at = sum(outs[: where[0]]) + where[1]
            put_rows(out_held, at, total.astype(BF))
            rows = pl.ds(at, total.shape[0])
            copies.append(
                pltpu.make_async_copy(
                    out_held.at[rows],
                    targets[where[0]].at[pl.ds(where[1], total.shape[0])],
                    out_sems.at[len(copies)],
                )
            )
            copies[-1].start()

        add_jobs(jobs, ins, store, held, sems)
        finish(copies)

    dma = pltpu.SemaphoreType.DMA
    return call(
        kernel, [(place, "s")] + [(one, "a") for one in arrays],
        [((rows, D), BF, "a") for rows in outs],
        [
            pltpu.VMEM((job_rows(jobs), D), BF), pltpu.VMEM((sum(outs), D), BF),
            dma((job_most(jobs) * len(jobs),)), dma((len(jobs),)),
        ],
        name, pins=pins,
    )


def total_call(name, place, arrays, total_rows, jobs, groups, depth, pins=(), mine_type=F32):
    count = len(arrays)
    size = total_rows // groups // depth

    def kernel(place, *refs):
        mine, parts = refs[count], refs[count + 1 : count + depth]
        held, total, sems = refs[count + depth :]

        def store(row, value):
            put_rows(total, row, value)

        add_jobs(jobs, refs[:count], store, held, sems)
        for d in range(depth):
            for g in range(groups):
                at = pl.multiple_of(
                    g * (total_rows // groups) + (place[2] ^ d) * size, 8
                )
                block = total[pl.ds(at, size), :]
                if d == 0:
                    put_rows(mine, g * size, block.astype(mine_type))
                else:
                    put_rows(parts[d - 1], g * size, block.astype(BF))

    return call(
        kernel, [(place, "s")] + [(one, "a") for one in arrays],
        [((groups * size, D), mine_type, "v")] + [((groups * size, D), BF, "v")] * (depth - 1),
        [
            pltpu.VMEM((job_rows(jobs), D), BF), pltpu.VMEM((total_rows, D), F32),
            pltpu.SemaphoreType.DMA((job_most(jobs) * len(jobs),)),
        ],
        name, pins=pins,
    )


def spread(depth, count):
    def kernel(place, *refs):
        own, other, refs = refs[:count], refs[count : 2 * count], refs[2 * count :]
        outs, biases, total = refs[:4], refs[4:-1], refs[-1]
        core, k = place[0], place[2]
        size = total.shape[1] // depth
        for which, parts in enumerate((own, other)):
            for d in range(depth):
                at = pl.multiple_of((k ^ d) * size, 8)
                ref, row = (parts[d], 0) if count == depth else (parts[0], d * size)
                total[which, pl.ds(at, size), :] = ref[row : row + size, :].astype(F32)
        rows = total.shape[1] // 4
        for n, out in enumerate(outs):
            for which, half in ((0, core), (1, 1 - core)):
                to = pl.ds(pl.multiple_of(half * PIECE, PIECE), PIECE)
                out[to, :] = total[which, n * rows : n * rows + PIECE, :]
        for n, bias in zip((0, 2), biases):
            at = n * rows + PIECE
            bias[...] = total[0, at : at + 1, :GROUP]

    return kernel


def solution(mesh):
    names = tuple(mesh.axis_names)
    heads, rows = mesh.shape["heads"], mesh.shape["rows"]
    depth = rows // 2
    piece = FF // (heads * rows)
    weight_rows = PIECE + BIAS_ROWS
    while (4 * weight_rows) % (8 * depth):
        weight_rows += BIAS_ROWS
    def send(value, where, label="moved"):
        pairs = []
        for r in range(rows):
            for h in range(heads):
                to_r, to_h = where(r, h)
                if (to_r, to_h) == (r, h):
                    continue
                index = {"rows": (r, to_r), "heads": (h, to_h)}
                a = b = 0
                for name in names:
                    a = a * mesh.shape[name] + index[name][0]
                    b = b * mesh.shape[name] + index[name][1]
                pairs.append((a, b))
        with jax.named_scope(label):
            return lax.ppermute(value, names, pairs)

    def swap(r, h):
        return (r & ~1) | (h & 1), (h & ~1) | (r & 1)

    def swap_b(r, h):
        return (r & ~1) | (1 - (h & 1)), (h & ~1) | (r & 1)

    def swap_b_back(r, h):
        return (r & ~1) | (h & 1), (h & ~1) | (1 - (r & 1))

    def core_to(r, h):
        return r ^ 1, h

    def head_to(d):
        return lambda r, h: (r, h ^ d)

    def depth_to(d):
        return lambda r, h: (r ^ (2 * d), h)

    def shards(
        layer_input, encoder_out, doc_lengths,
        self_query, self_qbias, self_key_weight, self_value, self_vbias, self_out, self_obias,
        first_gain, first_shift,
        cross_query, cross_qbias, cross_key, cross_value, cross_vbias, cross_out, cross_obias,
        second_gain, second_shift, up_weight, up_bias, down_weight, down_bias,
        third_gain, third_shift, out_grad,
    ):
        h = lax.axis_index("heads")
        r = lax.axis_index("rows")
        core, k = r % 2, r // 2
        place = jnp.stack([core, h, k]).astype(jnp.int32)
        stays = core == h % 2

        def line(vector):
            return vector.reshape(1, -1)

        params = jnp.stack(
            [
                self_obias, first_gain, first_shift, cross_obias, second_gain, second_shift,
                down_bias, third_gain, third_shift,
            ]
        )

        def v(*arrays):
            return [(one, "v") for one in arrays]

        def a(*arrays):
            return [(one, "a") for one in arrays]

        def l(*arrays):
            return [(one, "l") for one in arrays]

        def d(*arrays):
            return [(one, "d") for one in arrays]

        here = [(place, "s")]

        lengths = jnp.concatenate([doc_lengths // 16, doc_lengths % 16], axis=0).astype(BF)
        lengths = jnp.pad(lengths, ((0, 12), (0, 120)))
        self_own = [self_query.T, self_key_weight.T, self_value.T]
        cross_own = [cross_query.T, cross_key.T, cross_value.T, cross_out, self_out]
        xa, xb, mine, mine_cross, mine_again, ga, gb, enc, _ = call(
            prepare,
            here + v(layer_input, lengths, *self_own, line(self_qbias), line(self_vbias), self_out)
            + v(*cross_own[:4], line(cross_qbias), line(cross_vbias), out_grad, encoder_out),
            [
                ((CHUNK + 16, D), BF, "v"), ((CHUNK, D), BF, "v"),
                ((3 * PIECE + 16, D), BF, "v"), ((5 * PIECE + 16, D), BF, "v"),
                ((5 * PIECE + 16, D), BF, "v"),
                ((CHUNK, D), BF, "v"), ((CHUNK, D), BF, "v"), ((HALF_ENC, D), BF, "v"),
            ],
            [], "prepare",
        )

        def gather_groups(mine, label):
            x, y = send(mine, head_to(1), label), send(mine, head_to(2), label)
            return [x, y, send(x, head_to(2), label + "_2")]

        self_near = gather_groups(mine, "w_self_near")
        xb = send(xb, swap_b, "x_b")
        xa = jnp.where(stays, xa, send(xa, swap, "x_a"))
        ya = send(xa, core_to, "y_a")
        yb = send(xb, core_to, "y_b")
        self_far = [send(one, core_to, "w_self_far") for one in self_near]
        self_w = self_near + self_far

        def gated(values, pins, name):
            count = len(values)
            anywhere = pl.BlockSpec(memory_space=pl.ANY)
            return pl.pallas_call(
                gate,
                in_specs=[anywhere] * (count + len(pins)),
                out_specs=[anywhere] * count,
                out_shape=[jax.ShapeDtypeStruct(one.shape, one.dtype) for one in values],
                input_output_aliases={n: n for n in range(count)},
                name=name,
            )(*values, *pins)

        mine_cross, enc = gated([mine_cross, enc], [self_near[0], xa, xb], "gate_x")
        (mine_again,) = gated([mine_again], [self_near[2]], "gate_y")
        cross_near = [send(mine_cross, head_to(1), "w_cross_near")] + [
            send(mine_again, head_to(d), "w_cross_near") for d in (2, 3)
        ]
        ea = send(enc, swap_b, "e_a")

        dma = pltpu.SemaphoreType.DMA
        weight = pltpu.VMEM((D, D), BF)
        half_weight = pltpu.VMEM((D // 2, D), BF)
        masks = pltpu.VMEM((2, CHUNK, ROW), F32)
        lines_bf = pltpu.VMEM((4, 16, D), BF)
        row_full = pltpu.VMEM((ROW, D), BF)
        enc_full = pltpu.VMEM((ENC, D), BF)
        tokens = (OWN, D)
        q, kk, vv, att, stats1, zero = call(
            self_forward,
            here + a(xa, xb, ya, yb) + a(*self_own, *self_w) + v(line(self_qbias), line(self_vbias)),
            [
                (tokens, BF, "e"), ((ROW, D), BF, "e"), ((ROW, D), BF, "e"), (tokens, BF, "v"),
                ((OWN, 128), F32, "v"),
            ],
            [weight] * 3 + [row_full, masks, lines_bf, dma((3, 7)), dma((4,)), dma((4,))],
            "self_forward", pins=[mine_cross, mine_again, enc],
        )
        *cross_near, ea, ga_here, gb = gated(cross_near + [ea, ga, gb], [zero], "gate_far")
        cross_far = [send(one, core_to, "w_cross_far") for one in cross_near]
        eb = send(ea, core_to, "e_b")
        ga = send(ga_here, swap, "g_a")
        gb = send(gb, swap_b, "g_b")
        cross_w = cross_near + cross_far
        hat1, scale1, cq, ck, cv, catt, stats2, hat2, zero = call(
            cross_forward,
            here + v(xa, xb, att, params) + a(ea, eb)
            + a(*cross_own, *cross_w) + v(line(cross_qbias), line(cross_vbias)),
            [
                (tokens, F32, "e"), ((OWN, 128), F32, "v"),
                (tokens, BF, "e"), ((ENC, D), BF, "e"), ((ENC, D), BF, "e"), (tokens, BF, "v"),
                ((OWN, 128), F32, "v"), (tokens, F32, "v"),
            ],
            [weight] * 4 + [
                enc_full, lines_bf, dma((4, 7)), dma((4,)), dma((2,)), weight, dma((1, 7)),
            ],
            "cross_forward",
        )
        chunk = ((CHUNK, D), BF, "v")
        out_a, out_b, dsecond, left, right, ff_snd, vec_a, upb, zero = call(
            feed_forward,
            here + v(hat2, stats2, params) + a(up_weight) + v(line(up_bias)) + a(down_weight)
            + l(ga_here, ga, gb),
            [
                chunk, chunk, (tokens, F32, "e"), ((OWN, FF), BF, "a"), (tokens, BF, "a"),
                ((FF, D), BF, "a"), ((8, D), F32, "v"), ((1, FF), F32, "v"),
            ],
            [
                pltpu.VMEM((D, FF), BF), pltpu.VMEM((FF, D), BF), pltpu.VMEM((OWN, FF), BF),
                pltpu.VMEM((OWN, FF), F32), pltpu.VMEM(tokens, BF), pltpu.VMEM(tokens, F32),
                pltpu.VMEM(tokens, BF), pltpu.VMEM((OWN, FF), BF), pltpu.VMEM((FF, D), BF),
                dma((2, FF // FF_STEP)), dma((6,)),
            ],
            "feed_forward",
        )
        ff_got = send(ff_snd, core_to, "ff_core")
        out_got = send(out_a, swap, "out_a")
        out_b = send(out_b, swap_b_back, "out_b")
        ff_own, _ = call(
            ff_weight_grads, here + a(left, right), [((FF, D), BF, "a")],
            [
                pltpu.VMEM((FF, D), BF), pltpu.VMEM((4, OWN, D), BF), pltpu.VMEM(tokens, BF),
                dma((9,)),
            ],
            "ff_weight_grads",
        )
        output = jnp.concatenate([jnp.where(stays, out_a, out_got), out_b], axis=0)

        half = D // 2

        def ff_row(g, which):
            return g * D + which * half

        def both(row):
            return [(0, row), (1, row)]

        ff_x, ff_y, _ = add_call(
            "ff_add_1", place, [ff_own, ff_got], [D, D],
            [
                ((0, 0), half, both(ff_row(1, 0))), ((0, half), half, both(ff_row(3, 0))),
                ((1, 0), half, both(ff_row(2, 1))), ((1, half), half, both(ff_row(3, 1))),
            ],
            pins=[out_got, out_b],
        )
        ff_gx = send(ff_x, head_to(1), "ff_heads")
        ff_gy = send(ff_y, head_to(2), "ff_heads")

        wr = weight_rows
        rows_a = [((10 * wr, D), BF, "p")] * 2
        half_e = ((OWN, D // 2), BF, "e")
        cross_w4, self_w4 = cross_own[3], self_out
        enc_half, enc_grads = ((ENC, D // 2), BF, "e"), [enc_full] * 2
        cdq, cdk, cdv, cgrad, ca_own, ca_snd, zero = call(
            cross_backward_a,
            here + l(dsecond, catt, cq, ck, cv, stats2) + d(hat1)
            + v(params) + a(ea, eb, cross_w4, *cross_w),
            [half_e, enc_half, enc_half, (tokens, BF, "e")] + rows_a,
            [weight, pltpu.VMEM(tokens, BF), enc_full, dma((1, 7)), dma((2,))],
            "cross_backward_a", pins=[ff_x, ff_y],
        )
        (ca_snd,) = gated([ca_snd], [ff_gx, ff_gy], "gate_ca")
        ca_got = send(ca_snd, core_to, "ca_core")
        ff_x2, ff_y2, _ = add_call(
            "ff_add_2", place, [ff_own, ff_got, ff_gx, ff_gy], [half, half],
            [
                ((0, 0), half, both(ff_row(2, 0)) + [(2, half)]),
                ((1, 0), half, both(ff_row(1, 1)) + [(3, half)]),
            ],
            pins=[zero],
        )
        ff_gx2 = send(ff_x2, head_to(2), "ff_heads_2")
        ff_gy2 = send(ff_y2, head_to(1), "ff_heads_2")
        c_x3, _ = add_call(
            "c_add_1", place, [ca_own, ca_got], [4 * wr], [((0, 0), 4 * wr, both(4 * wr))],
            pins=[ff_x2],
        )
        c_gx3 = send(c_x3, head_to(1), "c_heads")
        dfirst, cb_own, cb_snd, vectors, zero = call(
            cross_backward_b,
            here + a(cdq, cdk, cdv) + d(dsecond) + l(cgrad, catt, cq, ck, cv, stats2)
            + d(hat1, scale1) + v(params) + a(ea, eb) + v(vec_a, upb)
            + a(*cross_own[:3], *cross_w),
            [
                (tokens, F32, "e"), ((6 * wr + HALF_ENC, D), BF, "p"),
                ((6 * wr + HALF_ENC, D), BF, "p"), ((16, D), F32, "v"),
            ],
            [weight] * 3 + [pltpu.VMEM(tokens, BF)] + enc_grads + [enc_full, dma((3, 7)), dma((5,))],
            "cross_backward_b", pins=[ff_x2, ff_y2, c_x3],
        )
        vectors = lax.all_gather(vectors, names)
        (cb_snd,) = gated([cb_snd], [ff_gx2, ff_gy2, c_gx3], "gate_cb")
        cb_got = send(cb_snd, core_to, "cb_core")

        def depth_send(parts, label):
            return [send(one, depth_to(d + 1), label) for d, one in enumerate(parts)]

        ff_mine, *ff_parts, _ = total_call(
            "ff_add_3", place, [ff_own, ff_got, ff_gx, ff_gy, ff_gx2, ff_gy2], D,
            [
                (0, half, both(ff_row(0, 0)) + [(2, 0), (4, 0)]),
                (half, half, both(ff_row(0, 1)) + [(3, 0), (5, 0)]),
            ],
            1, depth, pins=[zero],
        )
        ff_back = depth_send(ff_parts, "ff_depth")
        c_y2, c_x1, _ = add_call(
            "c_add_2", place, [ca_own, ca_got, cb_own, cb_got, c_gx3], [4 * wr, 4 * wr],
            [
                ((0, 0), 4 * wr, both(0) + [(4, 0)]),
                ((1, 0), 3 * wr, [(2, 3 * wr), (3, 3 * wr)]), ((1, 3 * wr), wr, both(9 * wr)),
            ],
            pins=[ff_parts[0]],
        )
        c_gy2 = send(c_y2, head_to(2), "c_heads_2")
        c_gx1 = send(c_x1, head_to(1), "c_heads_2")

        row_half, row_grads = ((ROW, D // 2), BF, "e"), [row_full] * 2
        sdq, sdk, sdv, sgrad, sa_own, sa_snd, zero = call(
            self_backward_a,
            here + l(dfirst, att, q, kk, vv, stats1) + a(xa, xb, ya, yb)
            + a(self_w4, *cross_w),
            [half_e, row_half, row_half, (tokens, BF, "e")] + rows_a,
            [weight, pltpu.VMEM(tokens, BF), masks]
            + [row_full, pltpu.VMEM((16, D), BF), dma((1, 7)), dma((5,))],
            "self_backward_a", pins=[*ff_parts, c_y2, c_x1],
        )
        (sa_snd,) = gated([sa_snd], [*ff_back, c_gy2, c_gx1], "gate_sa")
        sa_got = send(sa_snd, core_to, "sa_core")
        c_mine, *c_parts, _ = total_call(
            "c_add_3", place, [ca_own, ca_got, cb_own, cb_got, c_gy2, c_gx1], 4 * wr,
            [
                (0, 3 * wr, [(2, 0), (3, 0), (4, 0), (5, 0)]),
                (3 * wr, wr, [(0, 8 * wr), (1, 8 * wr), (4, 3 * wr), (5, 3 * wr)]),
            ],
            1, depth, pins=[zero], mine_type=BF,
        )
        c_depth = depth_send(c_parts, "c_depth")
        s_y, enc_sum, _ = add_call(
            "s_add_1", place, [sa_own, sa_got, cb_own, cb_got], [8 * wr, HALF_ENC],
            [((0, 0), 8 * wr, both(0)), ((1, 0), HALF_ENC, [(2, 6 * wr), (3, 6 * wr)])],
            pins=[c_parts[0]],
        )
        encoder_g = send(enc_sum, swap_b_back, "enc_grad")
        s_gy = send(s_y, head_to(2), "s_heads")
        sb_own, sb_snd, zero = call(
            self_backward_b,
            here + a(sdq, sdk, sdv) + d(dfirst) + l(sgrad, att, q, kk, vv, stats1)
            + a(xa, xb, ya, yb) + a(*self_own, *self_w),
            [((6 * wr + 2 * CHUNK, D), BF, "p"), ((6 * wr + 2 * CHUNK, D), BF, "p")],
            [weight] * 3 + [pltpu.VMEM(tokens, BF)] + row_grads + [masks]
            + [row_full, pltpu.VMEM((ROW, D), F32), pltpu.VMEM((16, D), BF), dma((3, 7)), dma((8,))],
            "self_backward_b", pins=[*c_parts, s_y, enc_sum],
        )
        (sb_snd,) = gated([sb_snd], [*c_depth, s_gy, encoder_g], "gate_sb")
        sb_got = send(sb_snd, core_to, "sb_core")

        def depth_sum(mine, got):
            for one in got:
                mine = mine + one.astype(F32)
            return mine

        part_rows = 4 * wr // depth
        s_x, in_a, in_b, c_part, _ = add_call(
            "s_add_2", place, [sa_own, sa_got, sb_own, sb_got, s_gy, c_mine, *c_depth],
            [4 * wr, CHUNK, CHUNK, part_rows],
            [
                ((0, 0), 3 * wr, [(2, 3 * wr), (3, 3 * wr), (4, 4 * wr)]),
                ((0, 3 * wr), wr, both(9 * wr) + [(4, 7 * wr)]),
                ((1, 0), CHUNK, [(2, 6 * wr), (3, 6 * wr)]),
                ((2, 0), CHUNK, [(2, 6 * wr + CHUNK), (3, 6 * wr + CHUNK)]),
                ((3, 0), part_rows, [(5 + n, 0) for n in range(depth)]),
            ],
        )
        c_back = [send(c_part, depth_to(d), "c_back") for d in range(1, depth)]
        s_gx = send(s_x, head_to(1), "s_heads_2")
        in_got = send(in_a, swap, "in_a")
        in_b = send(in_b, swap_b_back, "in_b")
        s_mine, *s_parts, _ = total_call(
            "s_add_3", place, [sa_own, sa_got, sb_own, sb_got, s_gy, s_gx], 4 * wr,
            [
                (0, 3 * wr, [(2, 0), (3, 0), (4, 0), (5, 0)]),
                (3 * wr, wr, [(0, 8 * wr), (1, 8 * wr), (4, 3 * wr), (5, 3 * wr)]),
            ],
            1, depth, pins=c_back,
        )
        s_depth = depth_send(s_parts, "s_depth")

        def whole_grads(own, other, label):
            *grads, qbias, vbias, _ = call(
                spread(depth, len(own)), here + v(*own, *other),
                [((GROUP, D), F32, "v")] * 4 + [((1, GROUP), F32, "v")] * 2,
                [pltpu.VMEM((2, 4 * wr, D), F32)], label + "_spread",
            )
            return grads, qbias[0], vbias[0]

        input_g = jnp.concatenate([jnp.where(stays, in_a, in_got), in_b], axis=0)
        c_own = jnp.concatenate(gated([c_part, *c_back], s_parts, "gate_c_far"), axis=0)
        c_other = send(c_own, core_to, "c_far")
        (cq_g, ck_g, cv_g, co_g), cqb, cvb = whole_grads([c_own], [c_other], "c")
        s_part = depth_sum(s_mine, s_depth).astype(BF)
        s_back = [send(s_part, depth_to(d), "s_back") for d in range(1, depth)]
        s_own = gated([s_part, *s_back], [cq_g, input_g, output], "gate_s_far")
        s_other = [send(one, core_to, "s_far") for one in s_own]
        (sq_g, sk_g, sv_g, so_g), sqb, svb = whole_grads(s_own, s_other, "s")

        ff = depth_sum(ff_mine, ff_back).reshape(2, piece, D)
        ff_here = lax.dynamic_index_in_dim(ff, core, 0, keepdims=False)
        ff_there = send(lax.dynamic_index_in_dim(ff, 1 - core, 0, keepdims=False), core_to, "ff_last")
        upweight_g = jnp.where(core == 0, ff_here, ff_there).T
        downweight_g = jnp.where(core == 0, ff_there, ff_here)

        vectors = jnp.sum(vectors, axis=0)
        ff_at = (h * rows + r) * piece
        upbias_g = lax.dynamic_slice_in_dim(vectors[9:13].reshape(FF), ff_at, piece)
        return (
            output, input_g, encoder_g,
            sq_g.T, sqb, sk_g.T, sv_g.T, svb, so_g, vectors[8], vectors[6], vectors[7],
            cq_g.T, cqb, ck_g.T, cv_g.T, cvb, co_g, vectors[5],
            vectors[3], vectors[4], upweight_g, upbias_g, downweight_g, vectors[2],
            vectors[0], vectors[1],
        )

    rowed, headed = P(("rows", "heads"), None), P(None, "heads")
    by_head, by_head_rows, whole = P("heads"), P("heads", None), P()
    ffed = ("heads", "rows")
    return jax.shard_map(
        shards,
        mesh=mesh,
        in_specs=(
            rowed, rowed, P("rows", None),
            headed, by_head, headed, headed, by_head, by_head_rows, whole, whole, whole,
            headed, by_head, headed, headed, by_head, by_head_rows, whole, whole, whole,
            whole, whole, whole, whole, whole, whole, rowed,
        ),
        out_specs=(
            rowed, rowed, rowed,
            headed, by_head, headed, headed, by_head, by_head_rows, whole, whole, whole,
            headed, by_head, headed, headed, by_head, by_head_rows, whole, whole, whole,
            P(None, ffed), P(ffed), P(ffed, None), whole, whole, whole,
        ),
        check_vma=False,
    )
```

time: 456 us -> 411 us (0.901)
  Pallas kernels: 246 us -> 218 us
  local copies, waits for them, and re-layouts: 32.8 us -> 9.37 us
  waiting for transfers between devices: 71.5 us -> 79.2 us
    pallas_call x21 -> x20, Pallas kernels: 246 us -> 218 us  [call(): pl.pallas_call(body, in_specs=[specs[kind] for _, kind in ins] + [anywher...]
    unnamed x168 -> x48, local copies, waits for them, and re-layouts: 24.3 us -> 5.14 us
    ppermute x57 -> x60, waiting for transfers between devices: 71.5 us -> 79.2 us  [send(): return lax.ppermute(value, names, pairs)]
    reshape x9 -> x0, local copies, waits for them, and re-layouts: 5.32 us -> none  [line(): return vector.reshape(1, -1)]
    ppermute x57 -> x60, starting transfers between devices: 65 us -> 67.2 us  [send(): return lax.ppermute(value, names, pairs)]
  transfers between devices with their start and end apart: 58 -> 61, of which waited for: 17 -> 21; matrix products, arithmetic and copies ran while one was open for 5% -> 5% of each run, Pallas kernels for 42% -> 41%
where the time goes in v3:
time: 411 us; the launch traced here: 403 us
  Pallas kernels  218 us (53%)
  waiting for transfers between devices  79.2 us (19%)
  starting transfers between devices  67.2 us (16%)
  between operations  15 us (4%)
  other arithmetic  14.1 us (3%)
  local copies, waits for them, and re-layouts  9.37 us (2%)
    pallas_call x20, Pallas kernels, call(): pl.pallas_call(body, in_specs=[specs[kind] for _, kind in ins] + [anywher...  218 us
    ppermute x60, waiting for transfers between devices, send(): return lax.ppermute(value, names, pairs)  79.2 us
    ppermute x60, starting transfers between devices, send(): return lax.ppermute(value, names, pairs)  67.2 us
  transfers between devices with their start and end apart: 61, of which 21 were waited for; matrix products, arithmetic and copies ran while one was open for 5% of the time, Pallas kernels for 41%

profile of v3, /device:TPU:9, one launch (start us, length us, event | category | flops | bytes accessed | tf_op | source)
XLA Modules:
  0.0 403.2 jit_solution(13355430582311863869)
XLA Ops:
  9.2 4.6 %prepare.1 = (bf16[288,768]{1,0:T(8,128)(2,1)}, bf16[272,768]{1,0:T(8,128)(2,1)}, bf16[304,768]{1,0:T(8,128)(2,1)}, bf16[496,768]{1,0:T(8,128)(2,1)}, bf16[496,7...) custom-call(s32[3]{0:T(128)} %pad_add_fusion.refs_0_, ...), custom_call_target="tpu_custom_call" | custom-call | flops 1000 | bytes 1000 | tf_op jit(solution)/shard_map/prepare/pallas_call | solution.py:198
  15.1 3.0 collective-permute-start
  19.4 6.2 %collective-permute-done.4.refs_2_.refs_8_.refs_18_ = bf16[304,768]{1,0:T(8,128)(2,1)S(1)} collective-permute-done((bf16[304,768]{1,0:T(8,128)(2,1)}, bf16[304,768]{1,0:T(8,128)(2,1)S(1)}, u32[]{:S(2)}, u32[]{:S(2)}) %collective-permute-start.4) | collective-permute-done | bytes 466976 | tf_op jit(solution)/shard_map/w_self_near/ppermute | solution.py:1074
  26.9 2.1 collective-permute-start.7
  29.0 2.6 collective-permute-done
  31.7 3.4 collective-permute-done.1.refs_4_.refs_2_.refs_8_.refs_12_
  36.5 3.7 collective-permute-done.6.refs_1_.refs_10_.refs_20_
  47.9 20.4 %self_forward.1 = (bf16[544,768]{1,0:T(8,128)(2,1)}, bf16[1088,768]{1,0:T(8,128)(2,1)}, bf16[1088,768]{1,0:T(8,128)(2,1)}, bf16[544,768]{1,0:T(8,128)(2,1)}, f32[544,128]{1,0:T(8,128)}, /*index=5*/f32[8,128]{1,0:T(8,128)}) custom-call(s32[3]{0:T(128)} %pad_add_fusion.refs_0_, bf16[288,768]{1,0:T(8,128)(2,1)} %copy-done, bf16[272,768]{1,0:T(8,128)(2,1)} %copy-done.1, ...), custom_call_target="tpu_custom_call" | custom-call | flops 1000 | bytes 1000 | tf_op jit(solution)/shard_map/self_forward/pallas_call | solution.py:198
  68.3 3.4 collective-permute-done.10.refs_0_
  71.8 10.9 %collective-permute-done.12.refs_2_ = bf16[496,768]{1,0:T(8,128)(2,1)} collective-permute-done((bf16[496,768]{1,0:T(8,128)(2,1)}, bf16[496,768]{1,0:T(8,128)(2,1)}, u32[]{:S(2)}, u32[]{:S(2)}) %collective-permute-start.12) | collective-permute-done | bytes 761888 | tf_op jit(solution)/shard_map/w_cross_near/ppermute | solution.py:1074
  82.8 3.9 collective-permute-start.15
  87.3 2.1 collective-permute-start.18
  92.2 22.6 %cross_forward.1 = (f32[544,768]{1,0:T(8,128)}, f32[544,128]{1,0:T(8,128)}, bf16[544,768]{1,0:T(8,128)(2,1)}, bf16[1024,768]{1,0:T(8,128)(2,1)}, bf16[1024,768]{...) custom-call(s32[3]{0:T(128)} %pad_add_fusion.refs_0_, ...), custom_call_target="tpu_custom_call" | custom-call | flops 1000 | bytes 1000 | tf_op jit(solution)/shard_map/cross_forward/pallas_call | solution.py:198
  114.8 30.0 %feed_forward.1 = (bf16[272,768]{1,0:T(8,128)(2,1)}, bf16[272,768]{1,0:T(8,128)(2,1)}, f32[544,768]{1,0:T(8,128)}, bf16[544,3072]{1,0:T(8,128)(2,1)}, bf16[544,7...) custom-call(s32[3]{0:T(128)} %pad_add_fusion.refs_0_, ...), custom_call_target="tpu_custom_call" | custom-call | flops 1000 | bytes 1000 | tf_op jit(solution)/shard_map/feed_forward/pallas_call | solution.py:198
  145.4 2.7 collective-permute-start.20
  148.1 9.4 %ff_weight_grads.1 = (bf16[3072,768]{1,0:T(8,128)(2,1)}, f32[8,128]{1,0:T(8,128)}) custom-call(s32[3]{0:T(128)} %pad_add_fusion.refs_0_, bf16[544,3072]{1,0:T(8,128)(2,1)} %get-tuple-element.160.refs_1_, bf16[544,768]{1,0:T(8,128)(2,1)} %get-tuple-element.161.refs_2_), custom_call_target="tpu_custom_call" | custom-call | flops 1000 | bytes 1000 | tf_op jit(solution)/shard_map/ff_weight_grads/pallas_call | solution.py:198
  157.6 4.8 %ff_add_1.1 = (bf16[768,768]{1,0:T(8,128)(2,1)}, bf16[768,768]{1,0:T(8,128)(2,1)}, f32[8,128]{1,0:T(8,128)}) custom-call(s32[3]{0:T(128)} %pad_add_fusion.refs_0_, bf16[3072,768]{1,0:T(8,128)(2,1)} %get-tuple-element.162.refs_1_, bf16[3072,768]{1,0:T(8,128)(2,1)} %collective-permute-done.22.refs_2_, bf16[272,768]{1,0:T(8,128)(2,1)} %collective-permute-done.20.refs_3_, ...), custom_call_target="tpu_custom_call" | custom-call | flops 1000 | bytes 1000 | tf_op jit(solution)/shard_map/ff_add_1/pallas_call | solution.py:198
  163.1 20.8 %cross_backward_a.1 = (bf16[544,384]{1,0:T(8,128)(2,1)}, bf16[1024,384]{1,0:T(8,128)(2,1)}, bf16[1024,384]{1,0:T(8,128)(2,1)}, bf16[544,768]{1,0:T(8,128)(2,1)},...) custom-call(s32[3]{0:T(128)} %pad_add_fusion.refs_0_, ...), custom_call_target="tpu_custom_call" | custom-call | flops 1000 | bytes 1000 | tf_op jit(solution)/shard_map/cross_backward_a/pallas_call | solution.py:198
  183.9 6.6 %collective-permute-done.23.refs_3_.refs_1_ = bf16[768,768]{1,0:T(8,128)(2,1)} collective-permute-done((bf16[768,768]{1,0:T(8,128)(2,1)}, bf16[768,768]{1,0:T(8,128)(2,1)}, u32[]{:S(2)}, u32[]{:S(2)}) %collective-permute-start.23) | collective-permute-done | bytes 1179680 | tf_op jit(solution)/shard_map/ff_heads/ppermute | solution.py:1074
  191.5 4.2 %ff_add_2.1 = (bf16[384,768]{1,0:T(8,128)(2,1)}, bf16[384,768]{1,0:T(8,128)(2,1)}, f32[8,128]{1,0:T(8,128)}) custom-call(s32[3]{0:T(128)} %pad_add_fusion.refs_0_, bf16[3072,768]{1,0:T(8,128)(2,1)} %get-tuple-element.162.refs_1_, bf16[3072,768]{1,0:T(8,128)(2,1)} %collective-permute-done.22.refs_2_, ...), custom_call_target="tpu_custom_call" | custom-call | flops 1000 | bytes 1000 | tf_op jit(solution)/shard_map/ff_add_2/pallas_call | solution.py:198
  195.7 3.6 c_add_1.1
  201.1 23.8 %cross_backward_b.1 = (f32[544,768]{1,0:T(8,128)}, bf16[1184,768]{1,0:T(8,128)(2,1)}, bf16[1184,768]{1,0:T(8,128)(2,1)}, f32[16,768]{1,0:T(8,128)}, f32[8,128]{1,0:T(8,128)}) custom-call(s32[3]{0:T(128)} %pad_add_fusion.refs_0_, bf16[544,384]{1,0:T(8,128)(2,1)} %get-tuple-element.166.refs_1_, bf16[1024,384]{1,0:T(8,128)(2,1)} %get-tuple-element.167.refs_2_, ...), custom_call_target="tpu_custom_call" | custom-call | flops 1000 | bytes 1000 | tf_op jit(solution)/shard_map/cross_backward_b/pallas_call | solution.py:198
  224.8 4.5 %collective-permute-done.27.refs_6_.refs_2_ = bf16[384,768]{1,0:T(8,128)(2,1)} collective-permute-done((bf16[384,768]{1,0:T(8,128)(2,1)}, bf16[384,768]{1,0:T(8,128)(2,1)}, u32[]{:S(2)}, u32[]{:S(2)}) %collective-permute-start.27) | collective-permute-done | bytes 589856 | tf_op jit(solution)/shard_map/ff_heads_2/ppermute | solution.py:1074
  230.2 4.4 %ff_add_3.1 = (f32[192,768]{1,0:T(8,128)}, bf16[192,768]{1,0:T(8,128)(2,1)}, bf16[192,768]{1,0:T(8,128)(2,1)}, bf16[192,768]{1,0:T(8,128)(2,1)}, f32[8,128]{1,0:T(8,128)}) custom-call(s32[3]{0:T(128)} %pad_add_fusion.refs_0_, bf16[3072,768]{1,0:T(8,128)(2,1)} %get-tuple-element.162.refs_1_, bf16[3072,768]{1,0:T(8,128)(2,1)} %collective-permute-done.22.refs_2_, ...), custom_call_target="tpu_custom_call" | custom-call | flops 1000 | bytes 1000 | tf_op jit(solution)/shard_map/ff_add_3/pallas_call | solution.py:198
  234.6 4.3 %c_add_2.1 = (bf16[448,768]{1,0:T(8,128)(2,1)}, bf16[448,768]{1,0:T(8,128)(2,1)}, f32[8,128]{1,0:T(8,128)}) custom-call(s32[3]{0:T(128)} %pad_add_fusion.refs_0_, bf16[1120,768]{1,0:T(8,128)(2,1)} %get-tuple-element.176.refs_1_, bf16[1120,768]{1,0:T(8,128)(2,1)} %collective-permute-done.25.refs_2_, bf16[1184,768]{1,0:T(8,128)(2,1)} %get-tuple-element.188.refs_3_, ...), custom_call_target="tpu_custom_call" | custom-call | flops 1000 | bytes 1000 | tf_op jit(solution)/shard_map/c_add_2/pallas_call | solution.py:198
  240.6 2.2 collective-permute-start.31
  242.9 20.4 %self_backward_a.1 = (bf16[544,384]{1,0:T(8,128)(2,1)}, bf16[1088,384]{1,0:T(8,128)(2,1)}, bf16[1088,384]{1,0:T(8,128)(2,1)}, bf16[544,768]{1,0:T(8,128)(2,1)}, ...) custom-call(s32[3]{0:T(128)} %pad_add_fusion.refs_0_, ...), custom_call_target="tpu_custom_call" | custom-call | flops 1000 | bytes 1000 | tf_op jit(solution)/shard_map/self_backward_a/pallas_call | solution.py:198
  263.4 5.1 %collective-permute-done.32.refs_3_ = bf16[192,768]{1,0:T(8,128)(2,1)} collective-permute-done((bf16[192,768]{1,0:T(8,128)(2,1)}, bf16[192,768]{1,0:T(8,128)(2,1)}, u32[]{:S(2)}, u32[]{:S(2)}) %collective-permute-start.32) | collective-permute-done | bytes 294944 | tf_op jit(solution)/shard_map/ff_depth/ppermute | solution.py:1074
  270.3 3.3 c_add_3.1
  273.9 4.6 %s_add_1.1 = (bf16[896,768]{1,0:T(8,128)(2,1)}, bf16[512,768]{1,0:T(8,128)(2,1)}, f32[8,128]{1,0:T(8,128)}) custom-call(s32[3]{0:T(128)} %pad_add_fusion.refs_0_, bf16[1120,768]{1,0:T(8,128)(2,1)} %get-tuple-element.192.refs_1_, bf16[1120,768]{1,0:T(8,128)(2,1)} %collective-permute-done.35.refs_2_, bf16[1184,768]{1,0:T(8,128)(2,1)} %get-tuple-element.188.refs_3_, ...), custom_call_target="tpu_custom_call" | custom-call | flops 1000 | bytes 1000 | tf_op jit(solution)/shard_map/s_add_1/pallas_call | solution.py:198
  280.5 2.5 collective-permute-start.37
  283.1 23.2 %self_backward_b.1 = (bf16[1216,768]{1,0:T(8,128)(2,1)}, bf16[1216,768]{1,0:T(8,128)(2,1)}, f32[8,128]{1,0:T(8,128)}) custom-call(s32[3]{0:T(128)} %pad_add_fusion.refs_0_, bf16[544,384]{1,0:T(8,128)(2,1)} %get-tuple-element.194.refs_1_, bf16[1088,384]{1,0:T(8,128)(2,1)} %get-tuple-element.195.refs_2_, bf16[1088,384]{1,0:T(8,128)(2,1)} %get-tuple-element.196.refs_3_, ...), custom_call_target="tpu_custom_call" | custom-call | flops 1000 | bytes 1000 | tf_op jit(solution)/shard_map/self_backward_b/pallas_call | solution.py:198
  306.3 3.9 collective-permute-done.39.refs_4_.refs_5_
  311.5 3.8 collective-permute-done.41.refs_4_
  315.3 4.4 %s_add_2.1 = (bf16[448,768]{1,0:T(8,128)(2,1)}, bf16[272,768]{1,0:T(8,128)(2,1)}, bf16[272,768]{1,0:T(8,128)(2,1)}, bf16[112,768]{1,0:T(8,128)(2,1)}, f32[8,128]{1,0:T(8,128)}) custom-call(s32[3]{0:T(128)} %pad_add_fusion.refs_0_, bf16[1120,768]{1,0:T(8,128)(2,1)} %get-tuple-element.192.refs_1_, bf16[1120,768]{1,0:T(8,128)(2,1)} %collective-permute-done.35.refs_2_, ...), custom_call_target="tpu_custom_call" | custom-call | flops 1000 | bytes 1000 | tf_op jit(solution)/shard_map/s_add_2/pallas_call | solution.py:198
  321.2 2.0 pad_maximum_fusion.refs_6_
  323.2 2.5 collective-permute-start.46
  325.8 2.1 convert_add_fusion
  329.9 4.5 %collective-permute-start.42 = (bf16[272,768]{1,0:T(8,128)(2,1)}, bf16[272,768]{1,0:T(8,128)(2,1)}, u32[]{:S(2)}, u32[]{:S(2)}) collective-permute-start(bf16[272,768]{1,0:T(8,128)(2,1)} %get-tuple-element.207), channel_id=1, source_target_pairs={{8,1},{24,17},{1,8},{17,24},{10,3},{26,19},{3,10},{19,26},{12,5},{... | collective-permute-start | bytes 1253384 | tf_op jit(solution)/shard_map/in_a/ppermute | solution.py:1074
  334.4 7.4 %collective-permute-done.47.refs_9_.refs_3_ = bf16[112,768]{1,0:T(8,128)(2,1)} collective-permute-done((bf16[112,768]{1,0:T(8,128)(2,1)S(1)}, bf16[112,768]{1,0:T(8,128)(2,1)}, u32[]{:S(2)}, u32[]{:S(2)}) %collective-permute-start.47) | collective-permute-done | bytes 172064 | tf_op jit(solution)/shard_map/c_back/ppermute | solution.py:1074
  341.8 3.4 s_add_3.1
  351.7 3.6 collective-permute-done.50
  355.3 7.1 %collective-permute-start.54 = (bf16[448,768]{1,0:T(8,128)(2,1)S(1)}, bf16[448,768]{1,0:T(8,128)(2,1)}, u32[]{:S(2)}, u32[]{:S(2)}) collective-permute-start(bf16[448,768]{1,0:T(8,128)(2,1)S(1)} %constant_dynamic-update-slice_fusion.refs_1_), channel_id=1, source_target_pairs={{0,1},{8,9},{16,17},{24,25},{1,0},{9,8},{17,16},{25,24},{2,3},{10,... | collective-permute-start | bytes 2064392 | tf_op jit(solution)/shard_map/c_far/ppermute | solution.py:1074
  372.1 3.0 c_spread.1
  375.1 5.1 %collective-permute-done.52.refs_2_ = bf16[112,768]{1,0:T(8,128)(2,1)} collective-permute-done((bf16[112,768]{1,0:T(8,128)(2,1)}, bf16[112,768]{1,0:T(8,128)(2,1)}, u32[]{:S(2)}, u32[]{:S(2)}) %collective-permute-start.52) | collective-permute-done | bytes 172064 | tf_op jit(solution)/shard_map/s_back/ppermute | solution.py:1074
  380.3 4.7 %collective-permute-done.53.refs_3_ = bf16[112,768]{1,0:T(8,128)(2,1)} collective-permute-done((bf16[112,768]{1,0:T(8,128)(2,1)}, bf16[112,768]{1,0:T(8,128)(2,1)}, u32[]{:S(2)}, u32[]{:S(2)}) %collective-permute-start.53) | collective-permute-done | bytes 172064 | tf_op jit(solution)/shard_map/s_back/ppermute | solution.py:1074
  391.0 3.1 s_spread.1
  394.0 2.1 copy.101
  (180 shorter events, 56.2 us)
Async XLA Ops:
  7.2 381.0 %all-gather.3.cloned.1.call-start = ((), (), s32[]{:S(2)}) async-start(), calls=%async_computation | async-start | bytes 1622016 | tf_op jit(solution)/shard_map/all_gather | solution.py:1309
  13.8 11.8 %collective-permute-start.4 = (bf16[304,768]{1,0:T(8,128)(2,1)}, bf16[304,768]{1,0:T(8,128)(2,1)S(1)}, u32[]{:S(2)}, u32[]{:S(2)}) collective-permute-start(bf16[304,768]{1,0:T(8,128)(2,1)} %get-tuple-element.134), channel_id=1, source_target_pairs={{0,8},{8,0},{16,24},{24,16},{1,9},{9,1},{17,25},{25,17},{2,10},{10... | collective-permute-start | bytes 1400840 | tf_op jit(solution)/shard_map/w_self_near/ppermute | solution.py:1074
  15.1 16.5 %collective-permute-start = (bf16[288,768]{1,0:T(8,128)(2,1)}, bf16[288,768]{1,0:T(8,128)(2,1)S(1)}, u32[]{:S(2)}, u32[]{:S(2)}) collective-permute-start(bf16[288,768]{1,0:T(8,128)(2,1)} %get-tuple-element.132), channel_id=1, source_target_pairs={{8,1},{24,17},{1,8},{17,24},{10,3},{26,19},{3,10},{19,26},{12,5},{... | collective-permute-start | bytes 1327112 | tf_op jit(solution)/shard_map/x_a/ppermute | solution.py:1074
  18.1 17.0 %collective-permute-start.1 = (bf16[272,768]{1,0:T(8,128)(2,1)}, bf16[272,768]{1,0:T(8,128)(2,1)S(1)}, u32[]{:S(2)}, u32[]{:S(2)}) collective-permute-start(bf16[272,768]{1,0:T(8,128)(2,1)} %get-tuple-element.133), channel_id=1, source_target_pairs={{0,1},{8,0},{16,17},{24,16},{1,9},{9,8},{17,25},{25,24},{2,3},{10,... | collective-permute-start | bytes 1253384 | tf_op jit(solution)/shard_map/x_b/ppermute | solution.py:1074
  18.1 18.3 %collective-permute-start.5 = (bf16[304,768]{1,0:T(8,128)(2,1)}, bf16[304,768]{1,0:T(8,128)(2,1)S(1)}, u32[]{:S(2)}, u32[]{:S(2)}) collective-permute-start(bf16[304,768]{1,0:T(8,128)(2,1)} %get-tuple-element.134), channel_id=1, source_target_pairs={{0,16},{8,24},{16,0},{24,8},{1,17},{9,25},{17,1},{25,9},{2,18},{10... | collective-permute-start | bytes 1400840 | tf_op jit(solution)/shard_map/w_self_near/ppermute | solution.py:1074
  25.6 14.6 %collective-permute-start.6 = (bf16[304,768]{1,0:T(8,128)(2,1)S(1)}, bf16[304,768]{1,0:T(8,128)(2,1)S(1)}, u32[]{:S(2)}, u32[]{:S(2)}) collective-permute-start(bf16[304,768]{1,0:T(8,128)(2,1)S(1)} %collective-permute-done.4.refs_2_.refs_8_.refs_18_), channel_id=1, source_target_pairs={{0,16},{8,24},{16,0},{24,8},{1,17},{9,25},{17,1},{25,9},{2,18},{10... | collective-permute-start | bytes 1400840 | tf_op jit(solution)/shard_map/w_self_near_2/ppermute | solution.py:1074
  26.9 16.7 %collective-permute-start.7 = (bf16[304,768]{1,0:T(8,128)(2,1)S(1)}, bf16[304,768]{1,0:T(8,128)(2,1)}, u32[]{:S(2)}, u32[]{:S(2)}) collective-permute-start(bf16[304,768]{1,0:T(8,128)(2,1)S(1)} %collective-permute-done.4.refs_2_.refs_8_.refs_18_), channel_id=1, source_target_pairs={{0,1},{8,9},{16,17},{24,25},{1,0},{9,8},{17,16},{25,24},{2,3},{10,... | collective-permute-start | bytes 1400840 | tf_op jit(solution)/shard_map/w_self_far/ppermute | solution.py:1074
  31.6 10.7 %collective-permute-start.2 = (bf16[288,768]{1,0:T(8,128)(2,1)S(1)}, bf16[288,768]{1,0:T(8,128)(2,1)S(1)}, u32[]{:S(2)}, u32[]{:S(2)}) collective-permute-start(bf16[288,768]{1,0:T(8,128)(2,1)S(1)} %broadcast_select_fusion.refs_3_.refs_1_.refs_7_.refs_11_), channel_id=1, source_target_pairs={{0,1},{8,9},{16,17},{24,25},{1,0},{9,8},{17,16},{25,24},{2,3},{10,... | collective-permute-start | bytes 1327112 | tf_op jit(solution)/shard_map/y_a/ppermute | solution.py:1074
  36.4 7.9 %collective-permute-start.8 = (bf16[304,768]{1,0:T(8,128)(2,1)S(1)}, bf16[304,768]{1,0:T(8,128)(2,1)}, u32[]{:S(2)}, u32[]{:S(2)}) collective-permute-start(bf16[304,768]{1,0:T(8,128)(2,1)S(1)} %collective-permute-done.5.refs_9_.refs_19_), channel_id=1, source_target_pairs={{0,1},{8,9},{16,17},{24,25},{1,0},{9,8},{17,16},{25,24},{2,3},{10,... | collective-permute-start | bytes 1400840 | tf_op jit(solution)/shard_map/w_self_far/ppermute | solution.py:1074
  40.2 31.6 %collective-permute-start.13 = (bf16[512,768]{1,0:T(8,128)(2,1)}, bf16[512,768]{1,0:T(8,128)(2,1)}, u32[]{:S(2)}, u32[]{:S(2)}) collective-permute-start(bf16[512,768]{1,0:T(8,128)(2,1)} %get-tuple-element.139.refs_18_), channel_id=1, source_target_pairs={{0,1},{8,0},{16,17},{24,16},{1,9},{9,8},{17,25},{25,24},{2,3},{10,... | collective-permute-start | bytes 2359304 | tf_op jit(solution)/shard_map/e_a/ppermute | solution.py:1074
  41.0 30.8 %collective-permute-start.10 = (bf16[496,768]{1,0:T(8,128)(2,1)}, bf16[496,768]{1,0:T(8,128)(2,1)}, u32[]{:S(2)}, u32[]{:S(2)}) collective-permute-start(bf16[496,768]{1,0:T(8,128)(2,1)} %get-tuple-element.137.refs_16_), channel_id=1, source_target_pairs={{0,8},{8,0},{16,24},{24,16},{1,9},{9,1},{17,25},{25,17},{2,10},{10... | collective-permute-start | bytes 2285576 | tf_op jit(solution)/shard_map/w_cross_near/ppermute | solution.py:1074
  42.3 29.5 %collective-permute-start.11 = (bf16[496,768]{1,0:T(8,128)(2,1)}, bf16[496,768]{1,0:T(8,128)(2,1)}, u32[]{:S(2)}, u32[]{:S(2)}) collective-permute-start(bf16[496,768]{1,0:T(8,128)(2,1)} %gate_y.1.refs_17_), channel_id=1, source_target_pairs={{0,16},{8,24},{16,0},{24,8},{1,17},{9,25},{17,1},{25,9},{2,18},{10... | collective-permute-start | bytes 2285576 | tf_op jit(solution)/shard_map/w_cross_near/ppermute | solution.py:1074
  43.5 39.2 %collective-permute-start.12 = (bf16[496,768]{1,0:T(8,128)(2,1)}, bf16[496,768]{1,0:T(8,128)(2,1)}, u32[]{:S(2)}, u32[]{:S(2)}) collective-permute-start(bf16[496,768]{1,0:T(8,128)(2,1)} %gate_y.1.refs_17_), channel_id=1, source_target_pairs={{0,24},{8,16},{16,8},{24,0},{1,25},{9,17},{17,9},{25,1},{2,26},{10... | collective-permute-start | bytes 2285576 | tf_op jit(solution)/shard_map/w_cross_near/ppermute | solution.py:1074
  82.8 6.6 %collective-permute-start.15 = (bf16[496,768]{1,0:T(8,128)(2,1)}, bf16[496,768]{1,0:T(8,128)(2,1)}, u32[]{:S(2)}, u32[]{:S(2)}) collective-permute-start(bf16[496,768]{1,0:T(8,128)(2,1)} %get-tuple-element.145.refs_12_.refs_21_), channel_id=1, source_target_pairs={{0,1},{8,9},{16,17},{24,25},{1,0},{9,8},{17,16},{25,24},{2,3},{10,... | collective-permute-start | bytes 2285576 | tf_op jit(solution)/shard_map/w_cross_far/ppermute | solution.py:1074
  87.3 27.5 %collective-permute-start.18 = (bf16[272,768]{1,0:T(8,128)(2,1)}, bf16[272,768]{1,0:T(8,128)(2,1)}, u32[]{:S(2)}, u32[]{:S(2)}) collective-permute-start(bf16[272,768]{1,0:T(8,128)(2,1)} %get-tuple-element.150.refs_7_), channel_id=1, source_target_pairs={{8,1},{24,17},{1,8},{17,24},{10,3},{26,19},{3,10},{19,26},{12,5},{... | collective-permute-start | bytes 1253384 | tf_op jit(solution)/shard_map/g_a/ppermute | solution.py:1074
  89.4 25.5 %collective-permute-start.19 = (bf16[272,768]{1,0:T(8,128)(2,1)}, bf16[272,768]{1,0:T(8,128)(2,1)}, u32[]{:S(2)}, u32[]{:S(2)}) collective-permute-start(bf16[272,768]{1,0:T(8,128)(2,1)} %get-tuple-element.151), channel_id=1, source_target_pairs={{0,1},{8,0},{16,17},{24,16},{1,9},{9,8},{17,25},{25,24},{2,3},{10,... | collective-permute-start | bytes 1253384 | tf_op jit(solution)/shard_map/g_b/ppermute | solution.py:1074
  144.8 12.8 %collective-permute-start.22 = (bf16[3072,768]{1,0:T(8,128)(2,1)}, bf16[3072,768]{1,0:T(8,128)(2,1)}, u32[]{:S(2)}, u32[]{:S(2)}) collective-permute-start(bf16[3072,768]{1,0:T(8,128)(2,1)} %get-tuple-element.163), channel_id=1, source_target_pairs={{0,1},{8,9},{16,17},{24,25},{1,0},{9,8},{17,16},{25,24},{2,3},{10,... | collective-permute-start | bytes 14155784 | tf_op jit(solution)/shard_map/ff_core/ppermute | solution.py:1074
  145.2 12.3 %collective-permute-start.21 = (bf16[272,768]{1,0:T(8,128)(2,1)}, bf16[272,768]{1,0:T(8,128)(2,1)}, u32[]{:S(2)}, u32[]{:S(2)}) collective-permute-start(bf16[272,768]{1,0:T(8,128)(2,1)} %get-tuple-element.153), channel_id=1, source_target_pairs={{0,8},{8,9},{16,24},{24,25},{1,0},{9,1},{17,16},{25,17},{2,10},{10... | collective-permute-start | bytes 1253384 | tf_op jit(solution)/shard_map/out_b/ppermute | solution.py:1074
  145.4 12.2 %collective-permute-start.20 = (bf16[272,768]{1,0:T(8,128)(2,1)}, bf16[272,768]{1,0:T(8,128)(2,1)}, u32[]{:S(2)}, u32[]{:S(2)}) collective-permute-start(bf16[272,768]{1,0:T(8,128)(2,1)} %get-tuple-element.152), channel_id=1, source_target_pairs={{8,1},{24,17},{1,8},{17,24},{10,3},{26,19},{3,10},{19,26},{12,5},{... | collective-permute-start | bytes 1253384 | tf_op jit(solution)/shard_map/out_a/ppermute | solution.py:1074
  162.4 28.1 %collective-permute-start.23 = (bf16[768,768]{1,0:T(8,128)(2,1)}, bf16[768,768]{1,0:T(8,128)(2,1)}, u32[]{:S(2)}, u32[]{:S(2)}) collective-permute-start(bf16[768,768]{1,0:T(8,128)(2,1)} %get-tuple-element.164.refs_18_), channel_id=1, source_target_pairs={{0,8},{8,0},{16,24},{24,16},{1,9},{9,1},{17,25},{25,17},{2,10},{10... | collective-permute-start | bytes 3538952 | tf_op jit(solution)/shard_map/ff_heads/ppermute | solution.py:1074
  162.8 27.6 %collective-permute-start.24 = (bf16[768,768]{1,0:T(8,128)(2,1)}, bf16[768,768]{1,0:T(8,128)(2,1)}, u32[]{:S(2)}, u32[]{:S(2)}) collective-permute-start(bf16[768,768]{1,0:T(8,128)(2,1)} %get-tuple-element.165.refs_19_), channel_id=1, source_target_pairs={{0,16},{8,24},{16,0},{24,8},{1,17},{9,25},{17,1},{25,9},{2,18},{10... | collective-permute-start | bytes 3538952 | tf_op jit(solution)/shard_map/ff_heads/ppermute | solution.py:1074
  199.3 30.1 %collective-permute-start.28 = (bf16[448,768]{1,0:T(8,128)(2,1)}, bf16[448,768]{1,0:T(8,128)(2,1)}, u32[]{:S(2)}, u32[]{:S(2)}) collective-permute-start(bf16[448,768]{1,0:T(8,128)(2,1)} %get-tuple-element.178.refs_29_), channel_id=1, source_target_pairs={{0,8},{8,0},{16,24},{24,16},{1,9},{9,1},{17,25},{25,17},{2,10},{10... | collective-permute-start | bytes 2064392 | tf_op jit(solution)/shard_map/c_heads/ppermute | solution.py:1074
  200.5 24.4 %collective-permute-start.26 = (bf16[384,768]{1,0:T(8,128)(2,1)}, bf16[384,768]{1,0:T(8,128)(2,1)}, u32[]{:S(2)}, u32[]{:S(2)}) collective-permute-start(bf16[384,768]{1,0:T(8,128)(2,1)} %get-tuple-element.174.refs_3_.refs_27_), channel_id=1, source_target_pairs={{0,16},{8,24},{16,0},{24,8},{1,17},{9,25},{17,1},{25,9},{2,18},{10... | collective-permute-start | bytes 1769480 | tf_op jit(solution)/shard_map/ff_heads_2/ppermute | solution.py:1074
  200.7 28.7 %collective-permute-start.27 = (bf16[384,768]{1,0:T(8,128)(2,1)}, bf16[384,768]{1,0:T(8,128)(2,1)}, u32[]{:S(2)}, u32[]{:S(2)}) collective-permute-start(bf16[384,768]{1,0:T(8,128)(2,1)} %get-tuple-element.175.refs_28_), channel_id=1, source_target_pairs={{0,8},{8,0},{16,24},{24,16},{1,9},{9,1},{17,25},{25,17},{2,10},{10... | collective-permute-start | bytes 1769480 | tf_op jit(solution)/shard_map/ff_heads_2/ppermute | solution.py:1074
  238.9 29.6 %collective-permute-start.33 = (bf16[448,768]{1,0:T(8,128)(2,1)}, bf16[448,768]{1,0:T(8,128)(2,1)}, u32[]{:S(2)}, u32[]{:S(2)}) collective-permute-start(bf16[448,768]{1,0:T(8,128)(2,1)} %get-tuple-element.190.refs_21_), channel_id=1, source_target_pairs={{0,16},{8,24},{16,0},{24,8},{1,17},{9,25},{17,1},{25,9},{2,18},{10... | collective-permute-start | bytes 2064392 | tf_op jit(solution)/shard_map/c_heads_2/ppermute | solution.py:1074
  239.2 29.3 %collective-permute-start.34 = (bf16[448,768]{1,0:T(8,128)(2,1)}, bf16[448,768]{1,0:T(8,128)(2,1)}, u32[]{:S(2)}, u32[]{:S(2)}) collective-permute-start(bf16[448,768]{1,0:T(8,128)(2,1)} %get-tuple-element.191.refs_22_), channel_id=1, source_target_pairs={{0,8},{8,0},{16,24},{24,16},{1,9},{9,1},{17,25},{25,17},{2,10},{10... | collective-permute-start | bytes 2064392 | tf_op jit(solution)/shard_map/c_heads_2/ppermute | solution.py:1074
  240.3 23.1 %collective-permute-start.30 = (bf16[192,768]{1,0:T(8,128)(2,1)}, bf16[192,768]{1,0:T(8,128)(2,1)}, u32[]{:S(2)}, u32[]{:S(2)}) collective-permute-start(bf16[192,768]{1,0:T(8,128)(2,1)} %get-tuple-element.185.refs_6_.refs_18_), channel_id=1, source_target_pairs={{0,2},{8,10},{16,18},{24,26},{1,3},{9,11},{17,19},{25,27},{2,0},{1... | collective-permute-start | bytes 884744 | tf_op jit(solution)/shard_map/ff_depth/ppermute | solution.py:1074
  240.6 22.8 %collective-permute-start.31 = (bf16[192,768]{1,0:T(8,128)(2,1)}, bf16[192,768]{1,0:T(8,128)(2,1)}, u32[]{:S(2)}, u32[]{:S(2)}) collective-permute-start(bf16[192,768]{1,0:T(8,128)(2,1)} %get-tuple-element.186.refs_19_), channel_id=1, source_target_pairs={{0,4},{8,12},{16,20},{24,28},{1,5},{9,13},{17,21},{25,29},{2,6},{1... | collective-permute-start | bytes 884744 | tf_op jit(solution)/shard_map/ff_depth/ppermute | solution.py:1074
  242.7 25.8 %collective-permute-start.32 = (bf16[192,768]{1,0:T(8,128)(2,1)}, bf16[192,768]{1,0:T(8,128)(2,1)}, u32[]{:S(2)}, u32[]{:S(2)}) collective-permute-start(bf16[192,768]{1,0:T(8,128)(2,1)} %get-tuple-element.187.refs_20_), channel_id=1, source_target_pairs={{0,6},{8,14},{16,22},{24,30},{1,7},{9,15},{17,23},{25,31},{2,4},{1... | collective-permute-start | bytes 884744 | tf_op jit(solution)/shard_map/ff_depth/ppermute | solution.py:1074
  278.5 31.8 %collective-permute-start.39 = (bf16[896,768]{1,0:T(8,128)(2,1)}, bf16[896,768]{1,0:T(8,128)(2,1)}, u32[]{:S(2)}, u32[]{:S(2)}) collective-permute-start(bf16[896,768]{1,0:T(8,128)(2,1)} %get-tuple-element.202.refs_27_), channel_id=1, source_target_pairs={{0,16},{8,24},{16,0},{24,8},{1,17},{9,25},{17,1},{25,9},{2,18},{10... | collective-permute-start | bytes 4128776 | tf_op jit(solution)/shard_map/s_heads/ppermute | solution.py:1074
  279.8 26.5 %collective-permute-start.40 = (bf16[512,768]{1,0:T(8,128)(2,1)}, bf16[512,768]{1,0:T(8,128)(2,1)}, u32[]{:S(2)}, u32[]{:S(2)}) collective-permute-start(bf16[512,768]{1,0:T(8,128)(2,1)} %get-tuple-element.203.refs_28_), channel_id=1, source_target_pairs={{0,8},{8,9},{16,24},{24,25},{1,0},{9,1},{17,16},{25,17},{2,10},{10... | collective-permute-start | bytes 2359304 | tf_op jit(solution)/shard_map/enc_grad/ppermute | solution.py:1074
  280.5 25.8 %collective-permute-start.36 = (bf16[112,768]{1,0:T(8,128)(2,1)}, bf16[112,768]{1,0:T(8,128)(2,1)}, u32[]{:S(2)}, u32[]{:S(2)}) collective-permute-start(bf16[112,768]{1,0:T(8,128)(2,1)} %get-tuple-element.199.refs_5_.refs_24_), channel_id=1, source_target_pairs={{0,2},{8,10},{16,18},{24,26},{1,3},{9,11},{17,19},{25,27},{2,0},{1... | collective-permute-start | bytes 516104 | tf_op jit(solution)/shard_map/c_depth/ppermute | solution.py:1074
  280.5 25.8 %collective-permute-start.37 = (bf16[112,768]{1,0:T(8,128)(2,1)}, bf16[112,768]{1,0:T(8,128)(2,1)}, u32[]{:S(2)}, u32[]{:S(2)}) collective-permute-start(bf16[112,768]{1,0:T(8,128)(2,1)} %get-tuple-element.200.refs_25_), channel_id=1, source_target_pairs={{0,4},{8,12},{16,20},{24,28},{1,5},{9,13},{17,21},{25,29},{2,6},{1... | collective-permute-start | bytes 516104 | tf_op jit(solution)/shard_map/c_depth/ppermute | solution.py:1074
  282.9 23.4 %collective-permute-start.38 = (bf16[112,768]{1,0:T(8,128)(2,1)}, bf16[112,768]{1,0:T(8,128)(2,1)}, u32[]{:S(2)}, u32[]{:S(2)}) collective-permute-start(bf16[112,768]{1,0:T(8,128)(2,1)} %get-tuple-element.201.refs_26_), channel_id=1, source_target_pairs={{0,6},{8,14},{16,22},{24,30},{1,7},{9,15},{17,23},{25,31},{2,4},{1... | collective-permute-start | bytes 516104 | tf_op jit(solution)/shard_map/c_depth/ppermute | solution.py:1074
  319.7 22.1 %collective-permute-start.44 = (bf16[448,768]{1,0:T(8,128)(2,1)}, bf16[448,768]{1,0:T(8,128)(2,1)}, u32[]{:S(2)}, u32[]{:S(2)}) collective-permute-start(bf16[448,768]{1,0:T(8,128)(2,1)} %get-tuple-element.209), channel_id=1, source_target_pairs={{0,8},{8,0},{16,24},{24,16},{1,9},{9,1},{17,25},{25,17},{2,10},{10... | collective-permute-start | bytes 2064392 | tf_op jit(solution)/shard_map/s_heads_2/ppermute | solution.py:1074
  323.1 6.7 %collective-permute-start.45 = (bf16[112,768]{1,0:T(8,128)(2,1)S(1)}, bf16[112,768]{1,0:T(8,128)(2,1)}, u32[]{:S(2)}, u32[]{:S(2)}) collective-permute-start(bf16[112,768]{1,0:T(8,128)(2,1)S(1)} %copy-done.10), channel_id=1, source_target_pairs={{0,2},{8,10},{16,18},{24,26},{1,3},{9,11},{17,19},{25,27},{2,0},{1... | collective-permute-start | bytes 516104 | tf_op jit(solution)/shard_map/c_back/ppermute | solution.py:1074
  323.2 11.2 %collective-permute-start.46 = (bf16[112,768]{1,0:T(8,128)(2,1)S(1)}, bf16[112,768]{1,0:T(8,128)(2,1)}, u32[]{:S(2)}, u32[]{:S(2)}) collective-permute-start(bf16[112,768]{1,0:T(8,128)(2,1)S(1)} %copy-done.10), channel_id=1, source_target_pairs={{0,4},{8,12},{16,20},{24,28},{1,5},{9,13},{17,21},{25,29},{2,6},{1... | collective-permute-start | bytes 516104 | tf_op jit(solution)/shard_map/c_back/ppermute | solution.py:1074
  325.6 16.2 %collective-permute-start.47 = (bf16[112,768]{1,0:T(8,128)(2,1)S(1)}, bf16[112,768]{1,0:T(8,128)(2,1)}, u32[]{:S(2)}, u32[]{:S(2)}) collective-permute-start(bf16[112,768]{1,0:T(8,128)(2,1)S(1)} %copy-done.10), channel_id=1, source_target_pairs={{0,6},{8,14},{16,22},{24,30},{1,7},{9,15},{17,23},{25,31},{2,4},{1... | collective-permute-start | bytes 516104 | tf_op jit(solution)/shard_map/c_back/ppermute | solution.py:1074
  327.9 39.8 %collective-permute-start.43 = (bf16[272,768]{1,0:T(8,128)(2,1)}, bf16[272,768]{1,0:T(8,128)(2,1)}, u32[]{:S(2)}, u32[]{:S(2)}) collective-permute-start(bf16[272,768]{1,0:T(8,128)(2,1)} %get-tuple-element.208), channel_id=1, source_target_pairs={{0,8},{8,9},{16,24},{24,25},{1,0},{9,1},{17,16},{25,17},{2,10},{10... | collective-permute-start | bytes 1253384 | tf_op jit(solution)/shard_map/in_b/ppermute | solution.py:1074
  329.9 38.9 %collective-permute-start.42 = (bf16[272,768]{1,0:T(8,128)(2,1)}, bf16[272,768]{1,0:T(8,128)(2,1)}, u32[]{:S(2)}, u32[]{:S(2)}) collective-permute-start(bf16[272,768]{1,0:T(8,128)(2,1)} %get-tuple-element.207), channel_id=1, source_target_pairs={{8,1},{24,17},{1,8},{17,24},{10,3},{26,19},{3,10},{19,26},{12,5},{... | collective-permute-start | bytes 1253384 | tf_op jit(solution)/shard_map/in_a/ppermute | solution.py:1074
  345.3 10.1 %collective-permute-start.50 = (bf16[112,768]{1,0:T(8,128)(2,1)}, bf16[112,768]{1,0:T(8,128)(2,1)S(1)}, u32[]{:S(2)}, u32[]{:S(2)}) collective-permute-start(bf16[112,768]{1,0:T(8,128)(2,1)} %get-tuple-element.214.refs_6_), channel_id=1, source_target_pairs={{0,6},{8,14},{16,22},{24,30},{1,7},{9,15},{17,23},{25,31},{2,4},{1... | collective-permute-start | bytes 516104 | tf_op jit(solution)/shard_map/s_depth/ppermute | solution.py:1074
  346.7 16.5 %collective-permute-start.49 = (bf16[112,768]{1,0:T(8,128)(2,1)}, bf16[112,768]{1,0:T(8,128)(2,1)S(1)}, u32[]{:S(2)}, u32[]{:S(2)}) collective-permute-start(bf16[112,768]{1,0:T(8,128)(2,1)} %get-tuple-element.213.refs_5_), channel_id=1, source_target_pairs={{0,4},{8,12},{16,20},{24,28},{1,5},{9,13},{17,21},{25,29},{2,6},{1... | collective-permute-start | bytes 516104 | tf_op jit(solution)/shard_map/s_depth/ppermute | solution.py:1074
  346.7 18.3 %collective-permute-start.48 = (bf16[112,768]{1,0:T(8,128)(2,1)}, bf16[112,768]{1,0:T(8,128)(2,1)S(1)}, u32[]{:S(2)}, u32[]{:S(2)}) collective-permute-start(bf16[112,768]{1,0:T(8,128)(2,1)} %get-tuple-element.212.refs_4_), channel_id=1, source_target_pairs={{0,2},{8,10},{16,18},{24,26},{1,3},{9,11},{17,19},{25,27},{2,0},{1... | collective-permute-start | bytes 516104 | tf_op jit(solution)/shard_map/s_depth/ppermute | solution.py:1074
  355.3 16.8 %collective-permute-start.54 = (bf16[448,768]{1,0:T(8,128)(2,1)S(1)}, bf16[448,768]{1,0:T(8,128)(2,1)}, u32[]{:S(2)}, u32[]{:S(2)}) collective-permute-start(bf16[448,768]{1,0:T(8,128)(2,1)S(1)} %constant_dynamic-update-slice_fusion.refs_1_), channel_id=1, source_target_pairs={{0,1},{8,9},{16,17},{24,25},{1,0},{9,8},{17,16},{25,24},{2,3},{10,... | collective-permute-start | bytes 2064392 | tf_op jit(solution)/shard_map/c_far/ppermute | solution.py:1074
  363.1 23.2 %collective-permute-start.59 = (f32[96,768]{1,0:T(8,128)}, f32[96,768]{1,0:T(8,128)}, u32[]{:S(2)}, u32[]{:S(2)}) collective-permute-start(f32[96,768]{1,0:T(8,128)} %dynamic-slice_bitcast_fusion), channel_id=1, source_target_pairs={{0,1},{8,9},{16,17},{24,25},{1,0},{9,8},{17,16},{25,24},{2,3},{10,... | collective-permute-start | bytes 884744 | tf_op jit(solution)/shard_map/ff_last/ppermute | solution.py:1074
  365.7 9.4 %collective-permute-start.51 = (bf16[112,768]{1,0:T(8,128)(2,1)}, bf16[112,768]{1,0:T(8,128)(2,1)}, u32[]{:S(2)}, u32[]{:S(2)}) collective-permute-start(bf16[112,768]{1,0:T(8,128)(2,1)} %add_convert_fusion.refs_0_), channel_id=1, source_target_pairs={{0,2},{8,10},{16,18},{24,26},{1,3},{9,11},{17,19},{25,27},{2,0},{1... | collective-permute-start | bytes 516104 | tf_op jit(solution)/shard_map/s_back/ppermute | solution.py:1074
  367.7 12.6 %collective-permute-start.52 = (bf16[112,768]{1,0:T(8,128)(2,1)}, bf16[112,768]{1,0:T(8,128)(2,1)}, u32[]{:S(2)}, u32[]{:S(2)}) collective-permute-start(bf16[112,768]{1,0:T(8,128)(2,1)} %add_convert_fusion.refs_0_), channel_id=1, source_target_pairs={{0,4},{8,12},{16,20},{24,28},{1,5},{9,13},{17,21},{25,29},{2,6},{1... | collective-permute-start | bytes 516104 | tf_op jit(solution)/shard_map/s_back/ppermute | solution.py:1074
  368.8 16.3 %collective-permute-start.53 = (bf16[112,768]{1,0:T(8,128)(2,1)}, bf16[112,768]{1,0:T(8,128)(2,1)}, u32[]{:S(2)}, u32[]{:S(2)}) collective-permute-start(bf16[112,768]{1,0:T(8,128)(2,1)} %add_convert_fusion.refs_0_), channel_id=1, source_target_pairs={{0,6},{8,14},{16,22},{24,30},{1,7},{9,15},{17,23},{25,31},{2,4},{1... | collective-permute-start | bytes 516104 | tf_op jit(solution)/shard_map/s_back/ppermute | solution.py:1074
  (35 other events, 232.0 us)
Sparse Core Ops, SparseCore 0:
  311.6 55.5 all-gather.2
